TPU v7x, 512 devices: a whole 4x4x16 slice. The times are simulated.
512 devices in a mesh: section: 16 (over z), tm: 32 (over y, x, core).
Axes of the slice: x: 4, y: 4, z: 16, core: 2. Of those that a mesh axis runs over, the one named last changes fastest.
Arguments:
- resid: bfloat16 [16, 4096, 768], P('section', 'tm'), may hold values from -40 to 40
- queries: bfloat16 [16, 4096, 768], P('section', 'tm'), may hold values from -100 to 100
- keys: bfloat16 [16, 4096, 768], P('section', 'tm'), may hold values from -4 to 4
- values: bfloat16 [16, 4096, 768], P('section', 'tm'), may hold values from -5 to 5
- gain: float32 [16, 768], P('section'), may hold values from 0.5 to 1.5
- taps: float32 [16, 31, 768], P('section'), may hold values from -1 to 1
- cotangent: bfloat16 [16, 4096, 768], P('section', 'tm'), may hold values from -8 to 8
Outputs:
- next_input: bfloat16 [16, 4096, 768], P('section', 'tm')
- grad_resid: bfloat16 [16, 4096, 768], P('section', 'tm')
- grad_queries: bfloat16 [16, 4096, 768], P('section', 'tm')
- grad_keys: bfloat16 [16, 4096, 768], P('section', 'tm')
- grad_values: bfloat16 [16, 4096, 768], P('section', 'tm')
- grad_gain: float32 [16, 768], P('section')
- grad_taps: float32 [16, 31, 768], P('section')
All inputs are finite; a program needn't handle non-finite values.
Results may differ from a plain program's by a relative error of at most 0.024.
Values may be sent and summed in bfloat16 or wider, within the bound.
No kernel may reach another device: no remote copies, remote signals or barrier semaphores. Data moves between devices by JAX's collectives and lax.ppermute only.
A program may use at most 64 MiB of HBM per device.

v0:
```python
import jax
import jax.numpy as jnp
from jax import lax
from jax.sharding import PartitionSpec as P

HEADS = 8
HEAD_DIM = 96
TAPS = 31


EPS = 1e-06


def with_halo(array, sides, width):
    for axis, dim in sides:
        size, length = (lax.axis_size(axis), array.shape[dim])
        up = [(i, (i + 1) % size) for i in range(size - 1)]
        down = [(j, i) for i, j in up]
        last = lax.slice_in_dim(array, length - width, length, axis=dim)
        leading = lax.slice_in_dim(array, 0, width, axis=dim)
        before = lax.ppermute(last, axis, up)
        after = lax.ppermute(leading, axis, down)
        array = jnp.concatenate([before, array, after], axis=dim)
    return array


def passed_along(block, axis, distance):
    devices = range(lax.axis_size(axis))
    route = [((i - distance) % len(devices), i) for i in devices]
    return lax.ppermute(block, axis, route)


def to_pieces(rows, groups):
    frames = rows.shape[0]
    split = rows.reshape(groups, frames // groups, HEADS, HEAD_DIM)
    return split.transpose(2, 0, 1, 3).reshape(HEADS * groups, frames // groups, HEAD_DIM)


def from_pieces(pieces, groups):
    sub = pieces.shape[1]
    split = pieces.reshape(HEADS, groups, sub, HEAD_DIM)
    return split.transpose(1, 2, 0, 3).reshape(groups * sub, HEADS * HEAD_DIM)


def head_major(rows):
    return rows.reshape(rows.shape[0], HEADS, HEAD_DIM).transpose(1, 0, 2)


def block_len(count):
    return min(512, count)


def attend_forward(query_rows, key_rows, value_rows, scale):
    query_count = query_rows.shape[0]
    key_count = key_rows.shape[0]
    query_block = block_len(query_count)
    key_block = block_len(key_count)
    key_blocks = key_rows.reshape(key_count // key_block, key_block, HEAD_DIM)
    value_blocks = value_rows.reshape(key_count // key_block, key_block, HEAD_DIM)

    def one_block(rows):

        def stats(carry, keys_here):
            peak, total = carry
            logits = jnp.dot(rows, keys_here.T, preferred_element_type=jnp.float32) * scale
            fresh = jnp.maximum(peak, jnp.max(logits, axis=1))
            total = total * jnp.exp(peak - fresh) + jnp.sum(
                jnp.exp(logits - fresh[:, None]), axis=1
            )
            return ((fresh, total), None)

        start = (
            jnp.full((query_block,), -jnp.inf, jnp.float32),
            jnp.zeros((query_block,), jnp.float32),
        )
        (peak, total), unused = lax.scan(stats, start, key_blocks)
        log_total = peak + jnp.log(total)

        def accumulate(acc, pair):
            keys_here, values_here = pair
            logits = jnp.dot(rows, keys_here.T, preferred_element_type=jnp.float32) * scale
            weights = jnp.exp(logits - log_total[:, None]).astype(jnp.bfloat16)
            return (acc + jnp.dot(weights, values_here, preferred_element_type=jnp.float32), None)

        result, unused = lax.scan(
            accumulate, jnp.zeros((query_block, HEAD_DIM), jnp.float32), (key_blocks, value_blocks)
        )
        return (result.astype(jnp.bfloat16), log_total)

    results, log_totals = lax.map(
        one_block, query_rows.reshape(query_count // query_block, query_block, HEAD_DIM)
    )
    return (results.reshape(query_count, HEAD_DIM), log_totals.reshape(query_count))


def attend_backward(query_rows, key_rows, value_rows, results, log_totals, grad_rows, scale):
    query_count = query_rows.shape[0]
    key_count = key_rows.shape[0]
    query_block = block_len(query_count)
    key_block = block_len(key_count)
    key_steps = key_count // key_block
    key_blocks = key_rows.reshape(key_steps, key_block, HEAD_DIM)
    value_blocks = value_rows.reshape(key_steps, key_block, HEAD_DIM)
    deltas = jnp.sum(grad_rows.astype(jnp.float32) * results.astype(jnp.float32), axis=1)
    query_steps = query_count // query_block

    def one_block(carry, block):
        grad_key_acc, grad_value_acc = carry
        rows, grads_here, logs_here, delta_here = block

        def inner(acc, pair):
            keys_here, values_here = pair
            logits = jnp.dot(rows, keys_here.T, preferred_element_type=jnp.float32) * scale
            probs = jnp.exp(logits - logs_here[:, None])
            weights = probs.astype(jnp.bfloat16)
            grad_vals = jnp.dot(weights.T, grads_here, preferred_element_type=jnp.float32)
            grad_probs = jnp.dot(grads_here, values_here.T, preferred_element_type=jnp.float32)
            grad_scores = (probs * (grad_probs - delta_here[:, None])).astype(jnp.bfloat16)
            acc = acc + jnp.dot(grad_scores, keys_here, preferred_element_type=jnp.float32)
            grad_keys_here = jnp.dot(grad_scores.T, rows, preferred_element_type=jnp.float32)
            return (acc, (grad_keys_here, grad_vals))

        grad_q, (grad_k, grad_v) = lax.scan(
            inner, jnp.zeros((query_block, HEAD_DIM), jnp.float32), (key_blocks, value_blocks)
        )
        return ((grad_key_acc + grad_k, grad_value_acc + grad_v), grad_q)

    start = (
        jnp.zeros((key_steps, key_block, HEAD_DIM), jnp.float32),
        jnp.zeros((key_steps, key_block, HEAD_DIM), jnp.float32),
    )
    blocks = (
        query_rows.reshape(query_steps, query_block, HEAD_DIM),
        grad_rows.reshape(query_steps, query_block, HEAD_DIM),
        log_totals.reshape(query_steps, query_block),
        deltas.reshape(query_steps, query_block),
    )
    (grad_k, grad_v), grad_q = lax.scan(one_block, start, blocks)
    return (
        grad_q.reshape(query_count, HEAD_DIM) * scale,
        grad_k.reshape(key_count, HEAD_DIM) * scale,
        grad_v.reshape(key_count, HEAD_DIM),
    )


def local(resid, queries, keys, values, gain, taps, cotangent):
    groups = lax.axis_size("tm") // HEADS
    scale = HEAD_DIM ** (-0.5)
    resid_rows = resid[0]
    frames = resid_rows.shape[0]
    query_pieces = to_pieces(queries[0], groups)
    key_copies = jnp.repeat(head_major(keys[0]), groups, axis=0)
    value_copies = jnp.repeat(head_major(values[0]), groups, axis=0)
    got_q, got_k, got_v = (
        lax.all_to_all(query_pieces, "tm", split_axis=0, concat_axis=0, tiled=True),
        lax.all_to_all(key_copies, "tm", split_axis=0, concat_axis=0, tiled=True),
        lax.all_to_all(value_copies, "tm", split_axis=0, concat_axis=0, tiled=True),
    )
    key_rows = got_k.reshape(-1, HEAD_DIM)
    value_rows = got_v.reshape(-1, HEAD_DIM)
    query_rows = got_q.reshape(-1, HEAD_DIM)
    head_results, log_totals = attend_forward(query_rows, key_rows, value_rows, scale)
    returned = lax.all_to_all(
        head_results.reshape(query_pieces.shape), "tm", split_axis=0, concat_axis=0, tiled=True
    )
    attended = from_pieces(returned, groups)
    mixed = resid_rows.astype(jnp.float32) + attended.astype(jnp.float32)
    inverse = lax.rsqrt(jnp.mean(mixed * mixed, axis=1, keepdims=True) + EPS)
    unit = mixed * inverse
    gain_row = gain[0][None, :]
    normed = (unit * gain_row).astype(jnp.bfloat16)
    width = (TAPS - 1) // 2
    padded = with_halo(normed, (("tm", 0),), width)
    kernel = taps[0]
    conv = jnp.zeros(mixed.shape, jnp.float32)
    for tap in range(TAPS):
        conv = conv + kernel[tap][None, :] * padded[tap : tap + frames].astype(jnp.float32)
    block_out = (mixed + jax.nn.silu(conv)).astype(jnp.bfloat16)
    next_input = passed_along(block_out[None], "section", 1)
    cot_rows = cotangent[0].astype(jnp.float32)
    sig = jax.nn.sigmoid(conv)
    grad_conv = (cot_rows * sig * (1.0 + conv * (1.0 - sig))).astype(jnp.bfloat16)
    padded_grad = with_halo(grad_conv, (("tm", 0),), width)
    grad_conv_wide = grad_conv.astype(jnp.float32)
    grad_normed = jnp.zeros(mixed.shape, jnp.float32)
    tap_terms = []
    for tap in range(TAPS):
        grad_normed = grad_normed + kernel[tap][None, :] * padded_grad[
            2 * width - tap : 2 * width - tap + frames
        ].astype(jnp.float32)
        tap_terms.append(
            jnp.sum(grad_conv_wide * padded[tap : tap + frames].astype(jnp.float32), axis=0)
        )
    gain_term = jnp.sum(grad_normed * unit, axis=0)
    grad_gain, grad_taps = (
        lax.psum(gain_term.astype(jnp.bfloat16), "tm").astype(jnp.float32),
        lax.psum(jnp.stack(tap_terms).astype(jnp.bfloat16), "tm").astype(jnp.float32),
    )
    scaled = grad_normed * gain_row
    grad_mixed = cot_rows + inverse * (
        scaled - unit * jnp.mean(scaled * unit, axis=1, keepdims=True)
    )
    grad_resid = grad_mixed.astype(jnp.bfloat16)
    grad_heads = lax.all_to_all(
        to_pieces(grad_resid, groups), "tm", split_axis=0, concat_axis=0, tiled=True
    ).reshape(-1, HEAD_DIM)
    grad_q, grad_k, grad_v = attend_backward(
        query_rows, key_rows, value_rows, head_results, log_totals, grad_heads, scale
    )
    grad_q_pieces = grad_q.reshape(query_pieces.shape)
    key_shape = (query_pieces.shape[0], frames, HEAD_DIM)
    back_q, back_k, back_v = (
        lax.all_to_all(
            grad_q_pieces.astype(jnp.bfloat16), "tm", split_axis=0, concat_axis=0, tiled=True
        ).astype(grad_q_pieces.dtype),
        lax.all_to_all(
            grad_k.reshape(key_shape).astype(jnp.bfloat16),
            "tm",
            split_axis=0,
            concat_axis=0,
            tiled=True,
        ).astype(jnp.float32),
        lax.all_to_all(
            grad_v.reshape(key_shape).astype(jnp.bfloat16),
            "tm",
            split_axis=0,
            concat_axis=0,
            tiled=True,
        ).astype(jnp.float32),
    )
    grad_key_rows = (
        jnp.sum(back_k.reshape(HEADS, groups, frames, HEAD_DIM), axis=1)
        .transpose(1, 0, 2)
        .reshape(frames, HEADS * HEAD_DIM)
    )
    grad_value_rows = (
        jnp.sum(back_v.reshape(HEADS, groups, frames, HEAD_DIM), axis=1)
        .transpose(1, 0, 2)
        .reshape(frames, HEADS * HEAD_DIM)
    )
    grad_query_rows = from_pieces(back_q, groups)
    return (
        next_input,
        grad_resid[None],
        grad_query_rows.astype(jnp.bfloat16)[None],
        grad_key_rows.astype(jnp.bfloat16)[None],
        grad_value_rows.astype(jnp.bfloat16)[None],
        grad_gain[None],
        grad_taps[None],
    )


def solution(mesh):
    in_specs = (
        P("section", "tm", None),
        P("section", "tm", None),
        P("section", "tm", None),
        P("section", "tm", None),
        P("section", None),
        P("section", None, None),
        P("section", "tm", None),
    )
    out_specs = (
        P("section", "tm", None),
        P("section", "tm", None),
        P("section", "tm", None),
        P("section", "tm", None),
        P("section", "tm", None),
        P("section", None),
        P("section", None, None),
    )
    return jax.shard_map(local, mesh=mesh, in_specs=in_specs, out_specs=out_specs, check_vma=False)
```

profile of v0, /device:TPU:1, one launch (start us, length us, event | category | flops | bytes accessed | tf_op | source)
XLA Modules:
  0.0 395.4 jit_solution(2706086443212717527)
XLA Ops:
  2.8 10.4 %all-to-all-start.1 = ((bf16[32,128,96]{1,2,0:T(8,128)(2,1)}), bf16[32,128,96]{1,2,0:T(8,128)(2,1)S(1)}, u32[]{:S(2)}, u32[]{:S(2)}) async-start(bf16[32,128,96]{1,2,0:T(8,128)(2,1)} %bitcast.9), calls=%async_computation.1 | async-start | bytes 1572864 | tf_op jit(solution)/shard_map/all_to_all | solution.py:156
  13.4 14.2 %all-to-all-done.1 = bf16[32,128,96]{1,2,0:T(8,128)(2,1)S(1)} async-done(((bf16[32,128,96]{1,2,0:T(8,128)(2,1)}), bf16[32,128,96]{1,2,0:T(8,128)(2,1)S(1)}, u32[]{:S(2)}, u32[]{:S(2)}) %all-to-all-start.1) | async-done | bytes 786464 | tf_op jit(solution)/shard_map/all_to_all | solution.py:156
  28.6 4.1 %all-to-all-start.2 = ((bf16[32,128,96]{1,2,0:T(8,128)(2,1)}), bf16[32,128,96]{1,2,0:T(8,128)(2,1)S(1)}, u32[]{:S(2)}, u32[]{:S(2)}) async-start(bf16[32,128,96]{1,2,0:T(8,128)(2,1)} %bitcast.12), calls=%async_computation.2 | async-start | bytes 1572864 | tf_op jit(solution)/shard_map/all_to_all | solution.py:157
  33.8 13.3 %all-to-all-done.2 = bf16[32,128,96]{1,2,0:T(8,128)(2,1)S(1)} async-done(((bf16[32,128,96]{1,2,0:T(8,128)(2,1)}), bf16[32,128,96]{1,2,0:T(8,128)(2,1)S(1)}, u32[]{:S(2)}, u32[]{:S(2)}) %all-to-all-start.2) | async-done | bytes 786464 | tf_op jit(solution)/shard_map/all_to_all | solution.py:157
  47.0 4.1 %all-to-all-start = ((bf16[32,32,96]{2,1,0:T(8,128)(2,1)}), bf16[32,32,96]{2,1,0:T(8,128)(2,1)S(1)}, u32[]{:S(2)}, u32[]{:S(2)}) async-start(bf16[32,32,96]{2,1,0:T(8,128)(2,1)} %bitcast.5), calls=%async_computation | async-start | bytes 524288 | tf_op jit(solution)/shard_map/all_to_all | solution.py:155
  53.1 7.0 %all-to-all-done = bf16[32,32,96]{2,1,0:T(8,128)(2,1)S(1)} async-done(((bf16[32,32,96]{2,1,0:T(8,128)(2,1)}), bf16[32,32,96]{2,1,0:T(8,128)(2,1)S(1)}, u32[]{:S(2)}, u32[]{:S(2)}) %all-to-all-start) | async-done | bytes 196640 | tf_op jit(solution)/shard_map/all_to_all | solution.py:155
  60.1 32.2 %while.77 = (s32[]{:T(128)}, bf16[2,512,96]{1,2,0:T(8,128)(2,1)S(1)}, f32[2,512]{1,0:T(2,128)S(1)}, bf16[2,512,96]{2,1,0:T(8,128)(2,1)S(1)}, bf16[8,512,96]{2,1,...) while((s32[]{:T(128)}, bf16[2,512,96]{1,2,0:T(8,128)(2,1)S(1)}, ...), condition=%wide.region_7.8_spmd.clone, body=%wide.region_0.7_spmd.sunk.clone | while | flops 152980480 | bytes 3677604 | solution.py:90
  60.2 4.5 %while.75 = (s32[]{:T(128)}, f32[512]{0:T(512)S(1)}, f32[512]{0:T(512)S(1)}, bf16[8,512,96]{2,1,0:T(8,128)(2,1)S(1)}, bf16[512,96]{1,0:T(8,128)(2,1)S(1)}, /*index=5*/s32[]{:T(128)}, s32[]{:T(128)}) while((s32[]{:T(128)}, f32[512]{0:T(512)S(1)}, f32[512]{0:T(512)S(1)}, bf16[8,512,96]{2,1,0:T(8,128)(2,1)S(1)}, ...), condition=%wide.region_4.4_spmd.clone, body=%wide.region_1.3_spmd.clone.sunk | while | flops 51382784 | bytes 2386012 | solution.py:76
  64.7 11.4 %while.76 = (s32[]{:T(128)}, f32[512,96]{0,1:T(8,128)S(1)}, bf16[8,512,96]{2,1,0:T(8,128)(2,1)S(1)}, bf16[512,96]{1,0:T(8,128)(2,1)S(1)}, f32[512]{0:T(512)S(1)}...) while((s32[]{:T(128)}, f32[512,96]{0,1:T(8,128)S(1)}, bf16[8,512,96]{2,1,0:T(8,128)(2,1)S(1)}, ...), condition=%wide.region_6.6_spmd.clone, body=%wide.region_5.5_spmd.clone.sunk | while | flops 101548032 | bytes 789599 | solution.py:85
  76.3 4.5 %while.75 = (s32[]{:T(128)}, f32[512]{0:T(512)S(1)}, f32[512]{0:T(512)S(1)}, bf16[8,512,96]{2,1,0:T(8,128)(2,1)S(1)}, bf16[512,96]{1,0:T(8,128)(2,1)S(1)}, /*index=5*/s32[]{:T(128)}, s32[]{:T(128)}) while((s32[]{:T(128)}, f32[512]{0:T(512)S(1)}, f32[512]{0:T(512)S(1)}, bf16[8,512,96]{2,1,0:T(8,128)(2,1)S(1)}, ...), condition=%wide.region_4.4_spmd.clone, body=%wide.region_1.3_spmd.clone.sunk | while | flops 51382784 | bytes 2386012 | solution.py:76
  80.8 11.4 %while.76 = (s32[]{:T(128)}, f32[512,96]{0,1:T(8,128)S(1)}, bf16[8,512,96]{2,1,0:T(8,128)(2,1)S(1)}, bf16[512,96]{1,0:T(8,128)(2,1)S(1)}, f32[512]{0:T(512)S(1)}...) while((s32[]{:T(128)}, f32[512,96]{0,1:T(8,128)S(1)}, bf16[8,512,96]{2,1,0:T(8,128)(2,1)S(1)}, ...), condition=%wide.region_6.6_spmd.clone, body=%wide.region_5.5_spmd.clone.sunk | while | flops 101548032 | bytes 789599 | solution.py:85
  97.2 8.8 %all-to-all-done.3 = bf16[32,32,96]{2,1,0:T(8,128)(2,1)S(1)} async-done(((bf16[32,32,96]{2,1,0:T(8,128)(2,1)}), bf16[32,32,96]{2,1,0:T(8,128)(2,1)S(1)}, u32[]{:S(2)}, u32[]{:S(2)}) %all-to-all-start.3) | async-done | bytes 196640 | tf_op jit(solution)/shard_map/all_to_all | solution.py:163
  129.3 11.0 %all-to-all-start.4 = ((bf16[32,32,96]{2,1,0:T(8,128)(2,1)}), bf16[32,32,96]{2,1,0:T(8,128)(2,1)S(1)}, u32[]{:S(2)}, u32[]{:S(2)}) async-start(bf16[32,32,96]{2,1,0:T(8,128)(2,1)} %bitcast.21), calls=%async_computation.4 | async-start | bytes 524288 | tf_op jit(solution)/shard_map/all_to_all | solution.py:204
  140.3 8.9 %all-to-all-done.4 = bf16[32,32,96]{2,1,0:T(8,128)(2,1)S(1)} async-done(((bf16[32,32,96]{2,1,0:T(8,128)(2,1)}), bf16[32,32,96]{2,1,0:T(8,128)(2,1)S(1)}, u32[]{:S(2)}, u32[]{:S(2)}) %all-to-all-start.4) | async-done | bytes 196640 | tf_op jit(solution)/shard_map/all_to_all | solution.py:204
  150.4 73.4 %while.79 = (s32[]{:T(128)}, f32[8,512,96]{1,2,0:T(8,128)}, f32[8,512,96]{1,2,0:T(8,128)}, f32[2,512,96]{1,2,0:T(8,128)}, bf16[2,512,96]{2,1,0:T(8,128)(2,1)S(1)...) while((s32[]{:T(128)}, f32[8,512,96]{1,2,0:T(8,128)}, ...), condition=%wide.region_14.15_spmd.clone.clone, body=%wide.region_11.14_spmd.clone.sunk.clone | while | flops 254902272 | bytes 21280760 | solution.py:138
  151.1 30.3 %while.78 = (s32[]{:T(128)}, f32[512,96]{0,1:T(8,128)S(1)}, f32[8,512,96]{1,2,0:T(8,128)}, f32[8,512,96]{1,2,0:T(8,128)}, bf16[8,512,96]{2,1,0:T(8,128)(2,1)S(1)...) while((s32[]{:T(128)}, f32[512,96]{0,1:T(8,128)S(1)}, ...), condition=%wide.region_13.13_spmd.clone, body=%wide.region_12.12_spmd.clone.sunk | while | flops 253329408 | bytes 6329991 | solution.py:123
  181.4 4.5 %select_add_fusion.4 = (f32[8,512,96]{1,2,0:T(8,128)}, f32[8,512,96]{1,2,0:T(8,128)}) fusion(f32[8,512,96]{1,2,0:T(8,128)} %get-tuple-element.865, f32[8,512,96]{1,2,0:T(8,128)} %get-tuple-element.1008, pred[]{:T(512)S(6)} %compare.16, f32[8,512,96]{1,2,0:T(8,128)} %get-tuple-element.864, f32[8,512,96]{1,2,0:T(8,128)} %get-tuple-element.1007), kind=kLoop, calls=%fused_computation.46.clone.1.clone | loop fusion | flops 1572864 | bytes 9437185 | tf_op jit(solution)/shard_map/while/body/eval_jaxpr/add | solution.py:126
  187.3 30.3 %while.78 = (s32[]{:T(128)}, f32[512,96]{0,1:T(8,128)S(1)}, f32[8,512,96]{1,2,0:T(8,128)}, f32[8,512,96]{1,2,0:T(8,128)}, bf16[8,512,96]{2,1,0:T(8,128)(2,1)S(1)...) while((s32[]{:T(128)}, f32[512,96]{0,1:T(8,128)S(1)}, ...), condition=%wide.region_13.13_spmd.clone, body=%wide.region_12.12_spmd.clone.sunk | while | flops 253329408 | bytes 6329991 | solution.py:123
  217.6 5.4 %select_add_fusion.4 = (f32[8,512,96]{1,2,0:T(8,128)}, f32[8,512,96]{1,2,0:T(8,128)}) fusion(f32[8,512,96]{1,2,0:T(8,128)} %get-tuple-element.865, f32[8,512,96]{1,2,0:T(8,128)} %get-tuple-element.1008, pred[]{:T(512)S(6)} %compare.16, f32[8,512,96]{1,2,0:T(8,128)} %get-tuple-element.864, f32[8,512,96]{1,2,0:T(8,128)} %get-tuple-element.1007), kind=kLoop, calls=%fused_computation.46.clone.1.clone | loop fusion | flops 1572864 | bytes 9437185 | tf_op jit(solution)/shard_map/while/body/eval_jaxpr/add | solution.py:126
  234.2 4.5 %all-to-all-done.5 = bf16[32,32,96]{2,1,0:T(8,128)(2,1)S(1)} async-done(((bf16[32,32,96]{2,1,0:T(8,128)(2,1)}), bf16[32,32,96]{2,1,0:T(8,128)(2,1)S(1)}, u32[]{:S(2)}, u32[]{:S(2)}) %all-to-all-start.5) | async-done | bytes 196640 | tf_op jit(solution)/shard_map/all_to_all | solution.py:213
  238.7 4.4 %all-to-all-start.6 = ((bf16[32,128,96]{1,2,0:T(8,128)(2,1)}), bf16[32,128,96]{1,2,0:T(8,128)(2,1)}, u32[]{:S(2)}, u32[]{:S(2)}) async-start(bf16[32,128,96]{1,2,0:T(8,128)(2,1)} %copy.75), calls=%async_computation.6 | async-start | bytes 1572864 | tf_op jit(solution)/shard_map/all_to_all | solution.py:216
  245.5 12.0 %all-to-all-done.6 = bf16[32,128,96]{1,2,0:T(8,128)(2,1)} async-done(((bf16[32,128,96]{1,2,0:T(8,128)(2,1)}), bf16[32,128,96]{1,2,0:T(8,128)(2,1)}, u32[]{:S(2)}, u32[]{:S(2)}) %all-to-all-start.6) | async-done | bytes 786464 | tf_op jit(solution)/shard_map/all_to_all | solution.py:216
  257.5 4.1 %all-to-all-start.7 = ((bf16[32,128,96]{1,2,0:T(8,128)(2,1)}), bf16[32,128,96]{1,2,0:T(8,128)(2,1)S(1)}, u32[]{:S(2)}, u32[]{:S(2)}) async-start(bf16[32,128,96]{1,2,0:T(8,128)(2,1)} %copy.79), calls=%async_computation.7 | async-start | bytes 1572864 | tf_op jit(solution)/shard_map/all_to_all | solution.py:223
  265.7 123.6 %all-reduce = (bf16[1,768]{1,0:T(2,128)(2,1)S(1)}, bf16[1,31,768]{2,0,1:T(2,128)(2,1)S(1)}) all-reduce(bf16[1,768]{1,0:T(2,128)(2,1)S(1)} %broadcast_in_dim.68, bf16[1,31,768]{2,0,1:T(2,128)(2,1)S(1)} %broadcast_in_dim.70), channel_id=1, replica_groups=mesh['section'=16,'tm'=32] {'tm'}, use_global_device_ids=true, to_apply=%region_18.19 | all-reduce | flops 24576 | bytes 98304 | tf_op jit(solution)/shard_map/psum | solution.py:196
  (376 shorter events, 152.1 us)
Async XLA Ops:
  2.8 24.8 %all-to-all-start.1 = ((bf16[32,128,96]{1,2,0:T(8,128)(2,1)}), bf16[32,128,96]{1,2,0:T(8,128)(2,1)S(1)}, u32[]{:S(2)}, u32[]{:S(2)}) async-start(bf16[32,128,96]{1,2,0:T(8,128)(2,1)} %bitcast.9), calls=%async_computation.1 | async-start | bytes 1572864 | tf_op jit(solution)/shard_map/all_to_all | solution.py:156
  28.6 18.5 %all-to-all-start.2 = ((bf16[32,128,96]{1,2,0:T(8,128)(2,1)}), bf16[32,128,96]{1,2,0:T(8,128)(2,1)S(1)}, u32[]{:S(2)}, u32[]{:S(2)}) async-start(bf16[32,128,96]{1,2,0:T(8,128)(2,1)} %bitcast.12), calls=%async_computation.2 | async-start | bytes 1572864 | tf_op jit(solution)/shard_map/all_to_all | solution.py:157
  47.0 13.1 %all-to-all-start = ((bf16[32,32,96]{2,1,0:T(8,128)(2,1)}), bf16[32,32,96]{2,1,0:T(8,128)(2,1)S(1)}, u32[]{:S(2)}, u32[]{:S(2)}) async-start(bf16[32,32,96]{2,1,0:T(8,128)(2,1)} %bitcast.5), calls=%async_computation | async-start | bytes 524288 | tf_op jit(solution)/shard_map/all_to_all | solution.py:155
  60.1 36.8 %copy-start.29 = (f32[1,768]{1,0:T(1,128)S(1)}, f32[1,768]{1,0:T(1,128)}, u32[]{:S(2)}) copy-start(f32[1,768]{1,0:T(1,128)} %param.21) | copy-start | bytes 9220
  60.1 36.9 %copy-start.18 = (f32[1,31,768]{2,0,1:T(1,128)S(1)}, f32[1,31,768]{2,0,1:T(1,128)}, u32[]{:S(2)}) copy-start(f32[1,31,768]{2,0,1:T(1,128)} %param.22) | copy-start | bytes 285700
  93.2 12.8 %all-to-all-start.3 = ((bf16[32,32,96]{2,1,0:T(8,128)(2,1)}), bf16[32,32,96]{2,1,0:T(8,128)(2,1)S(1)}, u32[]{:S(2)}, u32[]{:S(2)}) async-start(bf16[32,32,96]{2,1,0:T(8,128)(2,1)} %bitcast.13), calls=%async_computation.3 | async-start | bytes 524288 | tf_op jit(solution)/shard_map/all_to_all | solution.py:163
  106.8 4.4 %collective-permute-start = (bf16[15,768]{1,0:T(8,128)(2,1)S(1)}, bf16[15,768]{1,0:T(8,128)(2,1)S(1)}, u32[]{:S(2)}, u32[]{:S(2)}) collective-permute-start(bf16[15,768]{1,0:T(8,128)(2,1)S(1)} %get-tuple-element.529), channel_id=1, source_target_pairs={{0,1},{1,2},{2,3},{3,4},{4,5},{5,6},{6,7},{7,8},{8,9},{9,10},{10,1... | collective-permute-start | bytes 69128 | tf_op jit(solution)/shard_map/ppermute | solution.py:21
  109.2 5.1 %collective-permute-start.1 = (bf16[15,768]{1,0:T(8,128)(2,1)S(1)}, bf16[15,768]{1,0:T(8,128)(2,1)S(1)}, u32[]{:S(2)}, u32[]{:S(2)}) collective-permute-start(bf16[15,768]{1,0:T(8,128)(2,1)S(1)} %get-tuple-element.530), channel_id=1, source_target_pairs={{1,0},{2,1},{3,2},{4,3},{5,4},{6,5},{7,6},{8,7},{9,8},{10,9},{11,1... | collective-permute-start | bytes 69128 | tf_op jit(solution)/shard_map/ppermute | solution.py:22
  117.6 5.6 %collective-permute-start.3 = (bf16[15,768]{1,0:T(8,128)(2,1)S(1)}, bf16[15,768]{1,0:T(8,128)(2,1)S(1)}, u32[]{:S(2)}, u32[]{:S(2)}) collective-permute-start(bf16[15,768]{1,0:T(8,128)(2,1)S(1)} %get-tuple-element.527), channel_id=1, source_target_pairs={{1,0},{2,1},{3,2},{4,3},{5,4},{6,5},{7,6},{8,7},{9,8},{10,9},{11,1... | collective-permute-start | bytes 69128 | tf_op jit(solution)/shard_map/ppermute | solution.py:22
  119.5 4.6 %collective-permute-start.4 = (bf16[15,768]{1,0:T(8,128)(2,1)S(1)}, bf16[15,768]{1,0:T(8,128)(2,1)S(1)}, u32[]{:S(2)}, u32[]{:S(2)}) collective-permute-start(bf16[15,768]{1,0:T(8,128)(2,1)S(1)} %get-tuple-element.528), channel_id=1, source_target_pairs={{0,1},{1,2},{2,3},{3,4},{4,5},{5,6},{6,7},{7,8},{8,9},{9,10},{10,1... | collective-permute-start | bytes 69128 | tf_op jit(solution)/shard_map/ppermute | solution.py:21
  128.2 22.2 %copy-start.7 = (bf16[128,768]{1,0:T(8,128)(2,1)}, bf16[128,768]{1,0:T(8,128)(2,1)S(1)}, u32[]{:S(2)}) copy-start(bf16[128,768]{1,0:T(8,128)(2,1)S(1)} %get-tuple-element.525) | copy-start | bytes 589828
  129.3 19.9 %all-to-all-start.4 = ((bf16[32,32,96]{2,1,0:T(8,128)(2,1)}), bf16[32,32,96]{2,1,0:T(8,128)(2,1)S(1)}, u32[]{:S(2)}, u32[]{:S(2)}) async-start(bf16[32,32,96]{2,1,0:T(8,128)(2,1)} %bitcast.21), calls=%async_computation.4 | async-start | bytes 524288 | tf_op jit(solution)/shard_map/all_to_all | solution.py:204
  225.9 12.8 %all-to-all-start.5 = ((bf16[32,32,96]{2,1,0:T(8,128)(2,1)}), bf16[32,32,96]{2,1,0:T(8,128)(2,1)S(1)}, u32[]{:S(2)}, u32[]{:S(2)}) async-start(bf16[32,32,96]{2,1,0:T(8,128)(2,1)} %bitcast.23), calls=%async_computation.5 | async-start | bytes 524288 | tf_op jit(solution)/shard_map/all_to_all | solution.py:213
  238.7 18.8 %all-to-all-start.6 = ((bf16[32,128,96]{1,2,0:T(8,128)(2,1)}), bf16[32,128,96]{1,2,0:T(8,128)(2,1)}, u32[]{:S(2)}, u32[]{:S(2)}) async-start(bf16[32,128,96]{1,2,0:T(8,128)(2,1)} %copy.75), calls=%async_computation.6 | async-start | bytes 1572864 | tf_op jit(solution)/shard_map/all_to_all | solution.py:216
  245.4 19.9 %copy-start.26 = (bf16[768]{0:T(1024)(128)(2,1)S(1)}, bf16[768]{0:T(1024)(128)(2,1)}, u32[]{:S(2)}) copy-start(bf16[768]{0:T(1024)(128)(2,1)} %get-tuple-element.381) | copy-start | bytes 4612
  245.4 19.9 %copy-start.25 = (bf16[768]{0:T(1024)(128)(2,1)S(1)}, bf16[768]{0:T(1024)(128)(2,1)}, u32[]{:S(2)}) copy-start(bf16[768]{0:T(1024)(128)(2,1)} %get-tuple-element.382) | copy-start | bytes 4612
  245.4 19.9 %copy-start.24 = (bf16[768]{0:T(1024)(128)(2,1)S(1)}, bf16[768]{0:T(1024)(128)(2,1)}, u32[]{:S(2)}) copy-start(bf16[768]{0:T(1024)(128)(2,1)} %get-tuple-element.383) | copy-start | bytes 4612
  245.4 19.9 %copy-start.23 = (bf16[768]{0:T(1024)(128)(2,1)S(1)}, bf16[768]{0:T(1024)(128)(2,1)}, u32[]{:S(2)}) copy-start(bf16[768]{0:T(1024)(128)(2,1)} %get-tuple-element.384) | copy-start | bytes 4612
  245.4 19.9 %copy-start.22 = (bf16[768]{0:T(1024)(128)(2,1)S(1)}, bf16[768]{0:T(1024)(128)(2,1)}, u32[]{:S(2)}) copy-start(bf16[768]{0:T(1024)(128)(2,1)} %get-tuple-element.385) | copy-start | bytes 4612
  245.5 19.9 %copy-start.21 = (bf16[768]{0:T(1024)(128)(2,1)S(1)}, bf16[768]{0:T(1024)(128)(2,1)}, u32[]{:S(2)}) copy-start(bf16[768]{0:T(1024)(128)(2,1)} %get-tuple-element.386) | copy-start | bytes 4612
  245.5 20.0 %copy-start.20 = (bf16[768]{0:T(1024)(128)(2,1)S(1)}, bf16[768]{0:T(1024)(128)(2,1)}, u32[]{:S(2)}) copy-start(bf16[768]{0:T(1024)(128)(2,1)} %get-tuple-element.378) | copy-start | bytes 4612
  245.5 20.2 %copy-start.19 = (bf16[768]{0:T(1024)(128)(2,1)S(1)}, bf16[768]{0:T(1024)(128)(2,1)}, u32[]{:S(2)}) copy-start(bf16[768]{0:T(1024)(128)(2,1)} %get-tuple-element.376) | copy-start | bytes 4612
  257.5 136.3 %all-to-all-start.7 = ((bf16[32,128,96]{1,2,0:T(8,128)(2,1)}), bf16[32,128,96]{1,2,0:T(8,128)(2,1)S(1)}, u32[]{:S(2)}, u32[]{:S(2)}) async-start(bf16[32,128,96]{1,2,0:T(8,128)(2,1)} %copy.79), calls=%async_computation.7 | async-start | bytes 1572864 | tf_op jit(solution)/shard_map/all_to_all | solution.py:223
  262.8 127.8 %collective-permute-start.2 = (bf16[1,128,768]{2,1,0:T(8,128)(2,1)S(1)}, bf16[1,128,768]{2,1,0:T(8,128)(2,1)S(1)}, u32[]{:S(2)}, u32[]{:S(2)}) collective-permute-start(bf16[1,128,768]{2,1,0:T(8,128)(2,1)S(1)} %copy-done.14), channel_id=1, source_target_pairs={{480,0},{0,32},{32,64},{64,96},{96,128},{128,160},{160,192},{192,2... | collective-permute-start | bytes 589832 | tf_op jit(solution)/shard_map/ppermute | solution.py:30
  (23 other events, 242.8 us)
where the time goes:
time: 402 us; the launch traced here: 395 us
  blocking collectives  124 us (31%)
  matrix products  87.6 us (22%)
  waiting for transfers between devices  72.5 us (18%)
  starting transfers between devices  57.6 us (14%)
  other arithmetic  27.4 us (7%)
  local copies, waits for them, and re-layouts  23.6 us (6%)
    psum x1, blocking collectives, local(): lax.psum(gain_term.astype(jnp.bfloat16), 'tm').astype(jnp.float32)  124 us
    dot_general x16, matrix products, accumulate(): jnp.dot(weights, values_here, preferred_element_type=jnp.float32)  22.5 us
    dot_general x16, matrix products, inner(): jnp.dot(grads_here, values_here.T, preferred_element_type=jnp.float32)  19.4 us
    dot_general x16, matrix products, inner(): jnp.dot(weights.T, grads_here, preferred_element_type=jnp.float32)  15.8 us
    dot_general x16, matrix products, inner(): jnp.dot(grad_scores.T, rows, preferred_element_type=jnp.float32)  15.6 us
    all_to_all x1, waiting for transfers between devices, local(): lax.all_to_all(key_copies, 'tm', split_axis=0, concat_axis=0, tiled=True)  14.2 us
    all_to_all x1, waiting for transfers between devices, local(): lax.all_to_all(value_copies, 'tm', split_axis=0, concat_axis=0, tiled=True)  13.3 us
    all_to_all x1, waiting for transfers between devices, local(): lax.all_to_all(grad_k.reshape(key_shape).astype(jnp.bfloat16), 'tm', spli...  12 us
  transfers between devices with their start and end apart: 13, of which 9 were waited for; matrix products, arithmetic and copies ran while one was open for 4% of the time, Pallas kernels for 0%

commit v1 on v0

v1 whole, which is shorter than its diff:
```python
import math

import jax
import jax.numpy as jnp
from jax import lax
from jax.experimental import pallas as pl
from jax.experimental.pallas import tpu as pltpu
from jax.sharding import PartitionSpec as P

HEADS = 8
HEAD_DIM = 96
TAPS = 31
CH = 768
LANES = 128
EPS = 1e-06

SCALE = HEAD_DIM ** (-0.5)
SCALE2 = SCALE * math.log2(math.e)

F32 = jnp.float32
BF16 = jnp.bfloat16

K_ROWS = slice(0, 96)
V_ROWS = slice(96, 192)
Q_ROWS = slice(192, 224)
PIECE_ROWS = 224

VMEM = pl.BlockSpec(memory_space=pltpu.VMEM)
SMEM = pl.BlockSpec(memory_space=pltpu.SMEM)
VMEM_LIMIT = 56 * 1024 * 1024


def lanes_of(rows):
    return lax.broadcasted_iota(jnp.int32, (rows, LANES), 1)


def roll_lanes(block, by):
    by = by % LANES
    return block if by == 0 else pltpu.roll(block, by, 1)


def heads_to_tiles(heads):
    lane = lanes_of(heads[0].shape[0])
    second = roll_lanes(heads[1], 96)
    third = roll_lanes(heads[2], 64)
    fourth = roll_lanes(heads[3], 32)
    return (
        jnp.where(lane < 96, heads[0], second),
        jnp.where(lane < 64, second, third),
        jnp.where(lane < 32, third, fourth),
    )


def tiles_to_heads(tiles):
    lane = lanes_of(tiles[0].shape[0])
    return (
        tiles[0],
        roll_lanes(jnp.where(lane >= 96, tiles[0], tiles[1]), 32),
        roll_lanes(jnp.where(lane >= 64, tiles[1], tiles[2]), 64),
        roll_lanes(tiles[2], 96),
    )


def call(kernel, out_shape, in_specs, scratch, flops, name, transcendentals=0):
    return pl.pallas_call(
        kernel,
        out_shape=out_shape,
        in_specs=in_specs,
        out_specs=jax.tree.map(lambda unused: VMEM, out_shape),
        scratch_shapes=scratch,
        compiler_params=pltpu.CompilerParams(vmem_limit_bytes=VMEM_LIMIT),
        cost_estimate=pl.CostEstimate(
            flops=flops, bytes_accessed=4 * 1024 * 1024, transcendentals=transcendentals
        ),
        name=name,
    )


def pack_kernel(groups, q_ref, k_ref, v_ref, send_ref, turned):
    frames = q_ref.shape[0]
    sub = frames // groups
    for source, rows in ((k_ref, K_ROWS), (v_ref, V_ROWS)):
        for tile in range(CH // LANES):
            at = slice(tile * LANES, (tile + 1) * LANES)
            turned[at, :] = source[:, at].astype(F32).T.astype(BF16)
        for head in range(HEADS):
            block = turned[head * HEAD_DIM : (head + 1) * HEAD_DIM, :]
            for group in range(groups):
                send_ref[head * groups + group, rows, :] = block
    lane = lanes_of(frames)
    for half in range(2):
        tiles = [
            q_ref[:, (3 * half + i) * LANES : (3 * half + i + 1) * LANES].astype(F32)
            for i in range(3)
        ]
        for i, block in enumerate(tiles_to_heads(tiles)):
            block = jnp.where(lane < HEAD_DIM, block, 0.0).astype(BF16)
            for group in range(groups):
                send_ref[(4 * half + i) * groups + group, Q_ROWS, :] = block[
                    group * sub : (group + 1) * sub
                ]


def fill_keys(got_ref, rows, turned, count):
    for source in range(count):
        at = slice(source * LANES, (source + 1) * LANES)
        turned[0:HEAD_DIM, at] = got_ref[source, rows, :]
        turned[HEAD_DIM:LANES, at] = jnp.zeros((LANES - HEAD_DIM, LANES), BF16)


def fill_natural(turned, natural, count):
    for source in range(count):
        at = slice(source * LANES, (source + 1) * LANES)
        natural[at, :] = turned[:, at].astype(F32).T.astype(BF16)


def forward_kernel(
    block, chunk, groups, place_ref, got_ref, send_ref, out_ref, log_ref, keys, values_t, values, scores
):
    count = got_ref.shape[0]
    key_count = keys.shape[1]
    sub = LANES // groups
    per = block // sub
    fill_keys(got_ref, K_ROWS, keys, count)
    fill_keys(got_ref, V_ROWS, values_t, count)
    fill_natural(values_t, values, count)

    def one_block(step, unused):
        rows = got_ref[pl.ds(step * per, per), Q_ROWS, :].reshape(block, LANES)
        peak = jnp.full((block, LANES), -jnp.inf, F32)
        for start in range(0, key_count, chunk):
            part = jnp.dot(rows, keys[:, start : start + chunk], preferred_element_type=F32)
            scores[:, start : start + chunk] = part
            for tile in range(0, chunk, LANES):
                peak = jnp.maximum(peak, part[:, tile : tile + LANES])
        peak = jnp.max(peak, axis=1, keepdims=True) * SCALE2
        total = jnp.zeros((block, LANES), F32)
        result = jnp.zeros((block, LANES), F32)
        for start in range(0, key_count, chunk):
            weights = jnp.exp2(scores[:, start : start + chunk] * SCALE2 - peak)
            for tile in range(0, chunk, LANES):
                total = total + weights[:, tile : tile + LANES]
            result = result + jnp.dot(
                weights.astype(BF16), values[start : start + chunk, :], preferred_element_type=F32
            )
        total = jnp.sum(total, axis=1, keepdims=True)
        here = (result / total).astype(BF16)
        at = pl.ds(pl.multiple_of(step * block, block), block)
        out_ref[at, :] = here
        log_ref[at, :] = jnp.broadcast_to(peak + jnp.log2(total), (block, LANES))
        send_ref[pl.ds(step * per, per), 0:sub, :] = here.reshape(per, sub, LANES)
        return 0

    lax.fori_loop(0, key_count // groups // block, one_block, 0)

    side = jnp.where(place_ref[0] % groups == groups - 1, -1, 1)
    for device in range(count):
        near = jnp.clip(device + side, 0, count - 1)
        send_ref[device, sub : 2 * sub, :] = send_ref[near, 0:sub, :]


def conv_kernel(
    groups,
    count,
    place_ref,
    got_ref,
    resid_ref,
    cot_ref,
    before_ref,
    after_ref,
    gain_ref,
    taps_ref,
    send_ref,
    out_ref,
    grad_ref,
    mixed,
    normed,
    grad_conv,
    scaled,
    sums,
):
    frames = resid_ref.shape[0]
    sub = frames // groups
    wide = frames + 2 * sub
    half_taps = (TAPS - 1) // 2
    edge = 16
    inner = frames + 2 * edge
    tiles = CH // LANES
    place = place_ref[0]

    square = jnp.zeros((wide, LANES), F32)
    for half in range(2):
        heads = []
        for i in range(4):
            first = (4 * half + i) * groups
            parts = [got_ref[first + groups - 1, sub : 2 * sub, :]]
            parts += [got_ref[first + group, 0:sub, :] for group in range(groups)]
            parts += [got_ref[first, sub : 2 * sub, :]]
            heads.append(jnp.concatenate(parts, axis=0).astype(F32))
        for i, attended in enumerate(heads_to_tiles(heads)):
            at = slice((3 * half + i) * LANES, (3 * half + i + 1) * LANES)
            block = jnp.concatenate(
                [before_ref[0:sub, at], resid_ref[:, at], after_ref[0:sub, at]], axis=0
            ).astype(F32)
            block = block + attended
            mixed[:, at] = block
            square = square + block * block
    inverse = lax.rsqrt(jnp.sum(square, axis=1, keepdims=True) * (1.0 / CH) + EPS)

    row = lax.broadcasted_iota(jnp.int32, (wide, LANES), 0)
    inside = ((row >= sub) | (place > 0)) & ((row < sub + frames) | (place < count - 1))
    lo, hi = sub - edge, sub - edge + inner
    row_inner = lax.broadcasted_iota(jnp.int32, (inner, LANES), 0) + lo
    inside_inner = ((row_inner >= sub) | (place > 0)) & (
        (row_inner < sub + frames) | (place < count - 1)
    )
    own = slice(sub, sub + frames)
    inverse_own = inverse[sub : sub + frames]

    dots = jnp.zeros((frames, LANES), F32)
    for tile in range(tiles):
        at = slice(tile * LANES, (tile + 1) * LANES)
        gain_row = gain_ref[0:1, at]
        value = (mixed[:, at] * inverse * gain_row).astype(BF16).astype(F32)
        normed[...] = jnp.where(inside, value, 0.0)
        conv = jnp.zeros((inner, LANES), F32)
        for tap in range(TAPS):
            first = lo + tap - half_taps
            conv = conv + taps_ref[tap : tap + 1, at] * normed[first : first + inner, :]
        sig = jax.nn.sigmoid(conv)
        out_ref[:, at] = (
            mixed[own, at] + (conv * sig)[edge : edge + frames]
        ).astype(BF16)
        cot = jnp.concatenate(
            [before_ref[sub : sub + edge, at], cot_ref[:, at], after_ref[sub : sub + edge, at]],
            axis=0,
        ).astype(F32)
        value = (cot * sig * (1.0 + conv * (1.0 - sig))).astype(BF16).astype(F32)
        grad_conv[...] = jnp.where(inside_inner, value, 0.0)
        grad_normed = jnp.zeros((frames, LANES), F32)
        grad_own = grad_conv[edge : edge + frames, :]
        for tap in range(TAPS):
            first = edge + half_taps - tap
            grad_normed = (
                grad_normed
                + taps_ref[tap : tap + 1, at] * grad_conv[first : first + frames, :]
            )
            first = sub + tap - half_taps
            sums[tap : tap + 1, at] = jnp.sum(
                grad_own * normed[first : first + frames, :], axis=0, keepdims=True
            )
        unit = mixed[own, at] * inverse_own
        sums[TAPS : TAPS + 1, at] = jnp.sum(grad_normed * unit, axis=0, keepdims=True)
        here = grad_normed * gain_row
        scaled[:, at] = here
        dots = dots + here * unit
    mean = jnp.sum(dots, axis=1, keepdims=True) * (1.0 / CH)

    lane = lanes_of(sub)
    sublane = lax.broadcasted_iota(jnp.int32, (8, LANES), 0)
    for half in range(2):
        grads = []
        for i in range(3):
            at = slice((3 * half + i) * LANES, (3 * half + i + 1) * LANES)
            unit = mixed[own, at] * inverse_own
            grad = cot_ref[:, at].astype(F32) + inverse_own * (scaled[:, at] - unit * mean)
            grad_ref[:, at] = grad.astype(BF16)
            grads.append(grad)
        for i, block in enumerate(tiles_to_heads(grads)):
            for group in range(groups):
                device = (4 * half + i) * groups + group
                eight = jnp.zeros((8, LANES), F32)
                for tile in range(tiles):
                    line = sums[device : device + 1, tile * LANES : (tile + 1) * LANES]
                    eight = jnp.where(sublane == tile, line, eight)
                spare = jnp.concatenate(
                    [roll_lanes(eight, 96 - 32 * a) for a in range(4)], axis=0
                )
                piece = jnp.where(lane < HEAD_DIM, block[group * sub : (group + 1) * sub], spare)
                send_ref[device] = piece.astype(BF16)


def backward_kernel(
    block,
    chunk,
    groups,
    got_ref,
    grads_ref,
    out_ref,
    log_ref,
    send_ref,
    keys_t,
    values_t,
    keys,
    grad_keys,
    grad_values,
):
    count = got_ref.shape[0]
    key_count = keys.shape[0]
    sub = LANES // groups
    per = block // sub
    fill_keys(got_ref, K_ROWS, keys_t, count)
    fill_keys(got_ref, V_ROWS, values_t, count)
    fill_natural(keys_t, keys, count)
    grad_keys[...] = jnp.zeros_like(grad_keys)
    grad_values[...] = jnp.zeros_like(grad_values)

    sums = jnp.zeros((sub, LANES), F32)
    for source in range(count):
        sums = sums + grads_ref[source].astype(F32)
    lane = lanes_of(block)
    lane_sub = lax.broadcasted_iota(jnp.int32, (per, sub, LANES), 2)

    def one_block(step, unused):
        rows = got_ref[pl.ds(step * per, per), Q_ROWS, :].reshape(block, LANES)
        grads = grads_ref[pl.ds(step * per, per), :, :].reshape(block, LANES).astype(F32)
        grads = jnp.where(lane < HEAD_DIM, grads, 0.0)
        at = pl.ds(pl.multiple_of(step * block, block), block)
        delta = jnp.sum(grads * out_ref[at, :].astype(F32), axis=1, keepdims=True)
        logs = jnp.concatenate([log_ref[at, :]] * (chunk // LANES), axis=1)
        rows_t = rows.astype(F32).T.astype(BF16)[0:HEAD_DIM]
        grads_t = grads.T.astype(BF16)[0:HEAD_DIM]
        grads = grads.astype(BF16)
        result = jnp.zeros((block, LANES), F32)
        for start in range(0, key_count, chunk):
            part = slice(start, start + chunk)
            logits = jnp.dot(rows, keys_t[:, part], preferred_element_type=F32)
            probs = jnp.exp2(logits * SCALE2 - logs)
            grad_probs = jnp.dot(grads, values_t[:, part], preferred_element_type=F32)
            grad_scores = (probs * (grad_probs - delta)).astype(BF16)
            result = result + jnp.dot(grad_scores, keys[part, :], preferred_element_type=F32)
            grad_keys[:, part] += jnp.dot(rows_t, grad_scores, preferred_element_type=F32)
            grad_values[:, part] += jnp.dot(
                grads_t, probs.astype(BF16), preferred_element_type=F32
            )
        piece = (result * SCALE).reshape(per, sub, LANES)
        piece = jnp.where(lane_sub < HEAD_DIM, piece, sums[None])
        send_ref[pl.ds(step * per, per), Q_ROWS, :] = piece.astype(BF16)
        return 0

    lax.fori_loop(0, key_count // groups // block, one_block, 0)
    for device in range(count):
        at = slice(device * LANES, (device + 1) * LANES)
        send_ref[device, K_ROWS, :] = (grad_keys[:, at] * SCALE).astype(BF16)
        send_ref[device, V_ROWS, :] = grad_values[:, at].astype(BF16)


def unpack_kernel(groups, got_ref, q_ref, k_ref, v_ref, gain_ref, taps_ref, turned):
    count = got_ref.shape[0]
    sub = LANES // groups
    for target, rows in ((k_ref, K_ROWS), (v_ref, V_ROWS)):
        for head in range(HEADS):
            total = got_ref[head * groups, rows, :].astype(F32)
            for group in range(1, groups):
                total = total + got_ref[head * groups + group, rows, :].astype(F32)
            turned[head * HEAD_DIM : (head + 1) * HEAD_DIM, :] = total
        for tile in range(CH // LANES):
            at = slice(tile * LANES, (tile + 1) * LANES)
            target[:, at] = turned[at, :].T.astype(BF16)
    for half in range(2):
        heads = [
            jnp.concatenate(
                [got_ref[(4 * half + i) * groups + group, Q_ROWS, :] for group in range(groups)],
                axis=0,
            ).astype(F32)
            for i in range(4)
        ]
        for i, block in enumerate(heads_to_tiles(heads)):
            at = slice((3 * half + i) * LANES, (3 * half + i + 1) * LANES)
            q_ref[:, at] = block.astype(BF16)
    lane = lanes_of(8)
    for device in range(count):
        piece = got_ref[device, Q_ROWS, :].astype(F32)
        eight = roll_lanes(piece[0:8], 32)
        for a in range(1, 4):
            eight = jnp.where(
                lane >= 32 * a, roll_lanes(piece[8 * a : 8 * a + 8], 32 * a - 96), eight
            )
        for tile in range(CH // LANES):
            at = slice(tile * LANES, (tile + 1) * LANES)
            if device < TAPS:
                taps_ref[device : device + 1, at] = eight[tile : tile + 1]
            else:
                gain_ref[:, at] = eight[tile : tile + 1]


def exchange(pieces):
    return lax.all_to_all(pieces, "tm", split_axis=0, concat_axis=0, tiled=True)


def local(resid, queries, keys, values, gain, taps, cotangent):
    count = lax.axis_size("tm")
    sections = lax.axis_size("section")
    groups = count // HEADS
    frames = resid.shape[1]
    sub = frames // groups
    total = frames * count
    per_device = total // groups
    place = lax.axis_index("tm").astype(jnp.int32).reshape(1)
    edge = 16
    block, chunk = 256, 512
    matmul = 2 * per_device * total * LANES

    resid, queries, keys, values, cotangent = (
        array[0] for array in (resid, queries, keys, values, cotangent)
    )
    up = [(i, i + 1) for i in range(count - 1)]
    down = [(i + 1, i) for i in range(count - 1)]
    before = lax.ppermute(
        jnp.concatenate([resid[frames - sub :], cotangent[frames - edge :]], axis=0), "tm", up
    )
    after = lax.ppermute(jnp.concatenate([resid[:sub], cotangent[:edge]], axis=0), "tm", down)

    pieces = jax.ShapeDtypeStruct((count, PIECE_ROWS, LANES), BF16)
    rows_shape = jax.ShapeDtypeStruct((frames, CH), BF16)
    sent = call(
        lambda *refs: pack_kernel(groups, *refs),
        pieces,
        [VMEM] * 3,
        [pltpu.VMEM((CH, LANES), BF16)],
        1000000,
        "pack_qkv",
    )(queries, keys, values)
    got = exchange(sent)

    results, head_out, logs = call(
        lambda *refs: forward_kernel(block, chunk, groups, *refs),
        (
            jax.ShapeDtypeStruct((count, 2 * sub, LANES), BF16),
            jax.ShapeDtypeStruct((per_device, LANES), BF16),
            jax.ShapeDtypeStruct((per_device, LANES), F32),
        ),
        [SMEM, VMEM],
        [
            pltpu.VMEM((LANES, total), BF16),
            pltpu.VMEM((LANES, total), BF16),
            pltpu.VMEM((total, LANES), BF16),
            pltpu.VMEM((block, total), F32),
        ],
        2 * matmul,
        "attend_forward",
        per_device * total,
    )(place, got)
    returned = exchange(results)

    grads_sent, block_out, grad_resid = call(
        lambda *refs: conv_kernel(groups, count, *refs),
        (
            jax.ShapeDtypeStruct((count, sub, LANES), BF16),
            rows_shape,
            rows_shape,
        ),
        [SMEM] + [VMEM] * 7,
        [
            pltpu.VMEM((frames + 2 * sub, CH), F32),
            pltpu.VMEM((frames + 2 * sub, LANES), F32),
            pltpu.VMEM((frames + 2 * edge, LANES), F32),
            pltpu.VMEM((frames, CH), F32),
            pltpu.VMEM((TAPS + 1, CH), F32),
        ],
        10000000,
        "conv_block",
    )(place, returned, resid, cotangent, before, after, gain, taps[0])
    grads_got = exchange(grads_sent)
    next_input = lax.ppermute(
        block_out, "section", [(i, (i + 1) % sections) for i in range(sections)]
    )

    grads_out = call(
        lambda *refs: backward_kernel(block, chunk, groups, *refs),
        pieces,
        [VMEM] * 4,
        [
            pltpu.VMEM((LANES, total), BF16),
            pltpu.VMEM((LANES, total), BF16),
            pltpu.VMEM((total, LANES), BF16),
            pltpu.VMEM((HEAD_DIM, total), F32),
            pltpu.VMEM((HEAD_DIM, total), F32),
        ],
        5 * matmul,
        "attend_backward",
        per_device * total,
    )(got, grads_got, head_out, logs)
    back = exchange(grads_out)

    grad_q, grad_k, grad_v, grad_gain, grad_taps = call(
        lambda *refs: unpack_kernel(groups, *refs),
        (
            rows_shape,
            rows_shape,
            rows_shape,
            jax.ShapeDtypeStruct((1, CH), F32),
            jax.ShapeDtypeStruct((TAPS, CH), F32),
        ),
        [VMEM],
        [pltpu.VMEM((CH, LANES), F32)],
        1000000,
        "unpack_grads",
    )(back)
    return (
        next_input[None],
        grad_resid[None],
        grad_q[None],
        grad_k[None],
        grad_v[None],
        grad_gain,
        grad_taps[None],
    )


def solution(mesh):
    rows = P("section", "tm", None)
    in_specs = (rows, rows, rows, rows, P("section", None), P("section", None, None), rows)
    out_specs = (rows, rows, rows, rows, rows, P("section", None), P("section", None, None))
    return jax.shard_map(local, mesh=mesh, in_specs=in_specs, out_specs=out_specs, check_vma=False)
```

time: 402 us -> 145 us (0.36); the launches traced: 395 us -> 144 us
  blocking collectives: 124 us -> 16 us
  matrix products: 87.6 us -> 0 us
  Pallas kernels: 0 us -> 39.6 us
  starting transfers between devices: 57.6 us -> 27.9 us
  other arithmetic: 27.4 us -> 0.01 us
  waiting for transfers between devices: 72.5 us -> 52.7 us
  local copies, waits for them, and re-layouts: 23.6 us -> 7.05 us
    psum x1 -> x0, blocking collectives: 124 us -> none  [local(): lax.psum(gain_term.astype(jnp.bfloat16), 'tm').astype(jnp.float32)]
    dot_general x112 -> x0, matrix products: 87.6 us -> none  [the longest x16 22.5 us: accumulate(): jnp.dot(weights, values_here, preferred_element_type=jnp.float32)]
    pallas_call x0 -> x5, Pallas kernels: none -> 39.6 us  [the longest x1 16.2 us: local(): call(lambda *refs: backward_kernel(block, chunk, groups, *refs), pieces,...]
    all_to_all x8 -> x3, waiting for transfers between devices: 68.6 us -> 37.2 us  [exchange(): return lax.all_to_all(pieces, 'tm', split_axis=0, concat_axis=0, tiled=True)]
    all_to_all x8 -> x3, starting transfers between devices: 45.8 us -> 20.5 us  [exchange(): return lax.all_to_all(pieces, 'tm', split_axis=0, concat_axis=0, tiled=True)]
    all_to_all x0 -> x1, blocking collectives: none -> 16 us  [exchange(): return lax.all_to_all(pieces, 'tm', split_axis=0, concat_axis=0, tiled=True)]
    reduce_sum x25 -> x0, other arithmetic: 13.5 us -> none  [the longest x4 4.61 us: local(): jnp.sum(grad_conv_wide * padded[tap:tap + frames].astype(jnp.float32), ax...]
    ppermute x5 -> x3, waiting for transfers between devices: 3.94 us -> 15.5 us  [the longest x1 12.2 us: local(): lax.ppermute(block_out, 'section', [(i, (i + 1) % sections) for i in rang...]
  transfers between devices with their start and end apart: 13 -> 6, of which waited for: 9 -> 6; matrix products, arithmetic and copies ran while one was open for 4% -> 1% of each run, Pallas kernels for 0% -> 0%
where the time goes in v1:
time: 145 us; the launch traced here: 144 us
  waiting for transfers between devices  52.7 us (36%)
  Pallas kernels  39.6 us (27%)
  starting transfers between devices  27.9 us (19%)
  blocking collectives  16 us (11%)
  local copies, waits for them, and re-layouts  7.05 us (5%)
    all_to_all x3, waiting for transfers between devices, exchange(): return lax.all_to_all(pieces, 'tm', split_axis=0, concat_axis=0, tiled=True)  37.2 us
    all_to_all x3, starting transfers between devices, exchange(): return lax.all_to_all(pieces, 'tm', split_axis=0, concat_axis=0, tiled=True)  20.5 us
    pallas_call x1, Pallas kernels, local(): call(lambda *refs: backward_kernel(block, chunk, groups, *refs), pieces,...  16.2 us
    all_to_all x1, blocking collectives, exchange(): return lax.all_to_all(pieces, 'tm', split_axis=0, concat_axis=0, tiled=True)  16 us
    ppermute x1, waiting for transfers between devices, local(): lax.ppermute(block_out, 'section', [(i, (i + 1) % sections) for i in rang...  12.2 us
    pallas_call x1, Pallas kernels, local(): call(lambda *refs: forward_kernel(block, chunk, groups, *refs), (jax.Shap...  11.2 us
    pallas_call x1, Pallas kernels, local(): call(lambda *refs: conv_kernel(groups, count, *refs), (jax.ShapeDtypeStru...  6.84 us
    unnamed x19, local copies, waits for them, and re-layouts  6.28 us
  transfers between devices with their start and end apart: 6, of which 6 were waited for; matrix products, arithmetic and copies ran while one was open for 1% of the time, Pallas kernels for 0%

profile of v1, /device:TPU:1, one launch (start us, length us, event | category | flops | bytes accessed | tf_op | source)
XLA Modules:
  0.0 144.0 jit_solution(17838929363741164676)
XLA Ops:
  0.6 2.8 %pack_qkv.1 = bf16[32,224,128]{2,1,0:T(8,128)(2,1)} custom-call(bf16[128,768]{1,0:T(8,128)(2,1)} %bitcast.26, bf16[128,768]{1,0:T(8,128)(2,1)} %bitcast.27, bf16[128,768]{1,0:T(8,128)(2,1)} %bitcast.28), custom_call_target="tpu_custom_call" | custom-call | flops 1000000 | bytes 4194304 | tf_op jit(solution)/shard_map/pack_qkv/pallas_call | solution.py:416
  3.4 10.7 %all-to-all-start = ((bf16[32,224,128]{2,1,0:T(8,128)(2,1)}), bf16[32,224,128]{2,1,0:T(8,128)(2,1)S(1)}, u32[]{:S(2)}, u32[]{:S(2)}) async-start(bf16[32,224,128]{2,1,0:T(8,128)(2,1)} %pack_qkv.1), calls=%async_computation | async-start | bytes 3670016 | tf_op jit(solution)/shard_map/all_to_all | solution.py:388
  14.1 25.0 %all-to-all-done.refs_1_.refs_0_ = bf16[32,224,128]{2,1,0:T(8,128)(2,1)S(1)} async-done(((bf16[32,224,128]{2,1,0:T(8,128)(2,1)}), bf16[32,224,128]{2,1,0:T(8,128)(2,1)S(1)}, u32[]{:S(2)}, u32[]{:S(2)}) %all-to-all-start) | async-done | bytes 1835040 | tf_op jit(solution)/shard_map/all_to_all | solution.py:388
  39.1 1.3 copy-done.2
  40.3 11.2 %attend_forward.1 = (bf16[32,64,128]{2,1,0:T(8,128)(2,1)}, bf16[1024,128]{1,0:T(8,128)(2,1)}, f32[1024,128]{1,0:T(8,128)}) custom-call(s32[1]{0:T(128)} %bitcast.refs_0_, bf16[32,224,128]{2,1,0:T(8,128)(2,1)} %copy-done.2), custom_call_target="tpu_custom_call" | custom-call | flops 2147483648 | bytes 4194304 | tf_op jit(solution)/shard_map/attend_forward/pallas_call | solution.py:426
  51.6 5.8 %all-to-all-start.1 = ((bf16[32,64,128]{2,1,0:T(8,128)(2,1)}), bf16[32,64,128]{2,1,0:T(8,128)(2,1)S(1)}, u32[]{:S(2)}, u32[]{:S(2)}) async-start(bf16[32,64,128]{2,1,0:T(8,128)(2,1)} %get-tuple-element.18), calls=%async_computation.1 | async-start | bytes 1048576 | tf_op jit(solution)/shard_map/all_to_all | solution.py:388
  57.4 0.8 slice_bitcast_fusion.2
  58.2 3.5 %collective-permute-start = (bf16[48,768]{1,0:T(8,128)(2,1)S(1)}, bf16[48,768]{1,0:T(8,128)(2,1)S(1)}, u32[]{:S(2)}, u32[]{:S(2)}) collective-permute-start(bf16[48,768]{1,0:T(8,128)(2,1)S(1)} %pad_maximum_fusion), channel_id=1, source_target_pairs={{0,1},{1,2},{2,3},{3,4},{4,5},{5,6},{6,7},{7,8},{8,9},{9,10},{10,1... | collective-permute-start | bytes 221192 | tf_op jit(solution)/shard_map/ppermute | solution.py:409
  61.7 1.9 %collective-permute-start.1 = (bf16[48,768]{1,0:T(8,128)(2,1)S(1)}, bf16[48,768]{1,0:T(8,128)(2,1)S(1)}, u32[]{:S(2)}, u32[]{:S(2)}) collective-permute-start(bf16[48,768]{1,0:T(8,128)(2,1)S(1)} %pad_maximum_fusion.1), channel_id=1, source_target_pairs={{1,0},{2,1},{3,2},{4,3},{5,4},{6,5},{7,6},{8,7},{9,8},{10,9},{11,1... | collective-permute-start | bytes 221192 | tf_op jit(solution)/shard_map/ppermute | solution.py:412
  63.7 0.6 copy.17
  64.4 3.3 %collective-permute-done.1.refs_5_ = bf16[48,768]{1,0:T(8,128)(2,1)S(1)} collective-permute-done((bf16[48,768]{1,0:T(8,128)(2,1)S(1)}, bf16[48,768]{1,0:T(8,128)(2,1)S(1)}, u32[]{:S(2)}, u32[]{:S(2)}) %collective-permute-start.1) | collective-permute-done | bytes 73760 | tf_op jit(solution)/shard_map/ppermute | solution.py:412
  67.7 1.4 all-to-all-done.1.refs_1_
  69.1 0.8 copy-done.1
  69.9 6.8 %conv_block.1 = (bf16[32,32,128]{2,1,0:T(8,128)(2,1)}, bf16[128,768]{1,0:T(8,128)(2,1)}, bf16[128,768]{1,0:T(8,128)(2,1)}) custom-call(s32[1]{0:T(128)} %bitcast.refs_0_, bf16[32,64,128]{2,1,0:T(8,128)(2,1)} %copy-done.1, bf16[128,768]{1,0:T(8,128)(2,1)} %bitcast.23, bf16[128,768]{1,0:T(8,128)(2,1)} %bitcast.25, bf16[48,768]{1,0:T(8,128)(2,1)} %copy-done.5, ...), custom_call_target="tpu_custom_call" | custom-call | flops 10000000 | bytes 4194304 | tf_op jit(solution)/shard_map/conv_block/pallas_call | solution.py:446
  76.7 16.0 %all_to_all.20.refs_1_ = bf16[32,32,128]{2,1,0:T(8,128)(2,1)} all-to-all(bf16[32,32,128]{2,1,0:T(8,128)(2,1)} %get-tuple-element.21), channel_id=1, replica_groups=mesh['section'=16,'tm'=32] {'tm'}, dimensions={0} | all-to-all | bytes 524288 | tf_op jit(solution)/shard_map/all_to_all | solution.py:388
  92.7 16.2 %attend_backward.1 = bf16[32,224,128]{2,1,0:T(8,128)(2,1)} custom-call(bf16[32,224,128]{2,1,0:T(8,128)(2,1)} %copy-done.2, bf16[32,32,128]{2,1,0:T(8,128)(2,1)} %all_to_all.20.refs_1_, bf16[1024,128]{1,0:T(8,128)(2,1)} %get-tuple-element.22.refs_2_, f32[1024,128]{1,0:T(8,128)} %get-tuple-element.23.refs_3_), custom_call_target="tpu_custom_call" | custom-call | flops 5368709120 | bytes 4194304 | tf_op jit(solution)/shard_map/attend_backward/pallas_call | solution.py:469
  108.8 4.0 %all-to-all-start.3 = ((bf16[32,224,128]{2,1,0:T(8,128)(2,1)}), bf16[32,224,128]{2,1,0:T(8,128)(2,1)S(1)}, u32[]{:S(2)}, u32[]{:S(2)}) async-start(bf16[32,224,128]{2,1,0:T(8,128)(2,1)} %attend_backward.1), calls=%async_computation.3 | async-start | bytes 3670016 | tf_op jit(solution)/shard_map/all_to_all | solution.py:388
  112.9 1.9 %collective-permute-start.2 = (bf16[128,768]{1,0:T(8,128)(2,1)S(1)}, bf16[128,768]{1,0:T(8,128)(2,1)S(1)}, u32[]{:S(2)}, u32[]{:S(2)}) collective-permute-start(bf16[128,768]{1,0:T(8,128)(2,1)S(1)} %copy-done.7), channel_id=1, source_target_pairs={{0,32},{32,64},{64,96},{96,128},{128,160},{160,192},{192,224},{224... | collective-permute-start | bytes 589832 | tf_op jit(solution)/shard_map/ppermute | solution.py:465
  114.8 12.2 %collective-permute-done.2 = bf16[128,768]{1,0:T(8,128)(2,1)S(1)} collective-permute-done((bf16[128,768]{1,0:T(8,128)(2,1)S(1)}, bf16[128,768]{1,0:T(8,128)(2,1)S(1)}, u32[]{:S(2)}, u32[]{:S(2)}) %collective-permute-start.2) | collective-permute-done | bytes 196640 | tf_op jit(solution)/shard_map/ppermute | solution.py:465
  127.0 10.9 %all-to-all-done.3.refs_0_ = bf16[32,224,128]{2,1,0:T(8,128)(2,1)S(1)} async-done(((bf16[32,224,128]{2,1,0:T(8,128)(2,1)}), bf16[32,224,128]{2,1,0:T(8,128)(2,1)S(1)}, u32[]{:S(2)}, u32[]{:S(2)}) %all-to-all-start.3) | async-done | bytes 1835040 | tf_op jit(solution)/shard_map/all_to_all | solution.py:388
  137.9 1.3 copy-done
  139.1 2.6 %unpack_grads.1 = (bf16[128,768]{1,0:T(8,128)(2,1)}, bf16[128,768]{1,0:T(8,128)(2,1)}, bf16[128,768]{1,0:T(8,128)(2,1)}, f32[1,768]{1,0:T(1,128)}, f32[31,768]{1,0:T(8,128)}) custom-call(bf16[32,224,128]{2,1,0:T(8,128)(2,1)} %copy-done), custom_call_target="tpu_custom_call" | custom-call | flops 1000000 | bytes 4194304 | tf_op jit(solution)/shard_map/unpack_grads/pallas_call | solution.py:486
  141.7 1.6 %copy.14 = f32[1,31,768]{2,0,1:T(1,128)} copy(f32[1,31,768]{2,1,0:T(8,128)} %bitcast.30) | data formatting | bytes 190464
  143.3 0.7 copy.19
  (17 shorter events, 0.1 us)
Async XLA Ops:
  3.4 10.7 %copy-start.3 = (bf16[1,128,768]{2,1,0:T(8,128)(2,1)S(1)}, bf16[1,128,768]{2,1,0:T(8,128)(2,1)}, u32[]{:S(2)}) copy-start(bf16[1,128,768]{2,1,0:T(8,128)(2,1)} %param.7) | copy-start | bytes 589828
  3.4 35.6 %all-to-all-start = ((bf16[32,224,128]{2,1,0:T(8,128)(2,1)}), bf16[32,224,128]{2,1,0:T(8,128)(2,1)S(1)}, u32[]{:S(2)}, u32[]{:S(2)}) async-start(bf16[32,224,128]{2,1,0:T(8,128)(2,1)} %pack_qkv.1), calls=%async_computation | async-start | bytes 3670016 | tf_op jit(solution)/shard_map/all_to_all | solution.py:388
  39.1 1.3 copy-start.2
  40.3 23.3 %copy-start.4 = (f32[1,31,768]{2,0,1:T(1,128)S(1)}, f32[1,31,768]{2,0,1:T(1,128)}, u32[]{:S(2)}) copy-start(f32[1,31,768]{2,0,1:T(1,128)} %param.12) | copy-start | bytes 285700
  51.6 17.5 %all-to-all-start.1 = ((bf16[32,64,128]{2,1,0:T(8,128)(2,1)}), bf16[32,64,128]{2,1,0:T(8,128)(2,1)S(1)}, u32[]{:S(2)}, u32[]{:S(2)}) async-start(bf16[32,64,128]{2,1,0:T(8,128)(2,1)} %get-tuple-element.18), calls=%async_computation.1 | async-start | bytes 1048576 | tf_op jit(solution)/shard_map/all_to_all | solution.py:388
  58.2 6.2 %collective-permute-start = (bf16[48,768]{1,0:T(8,128)(2,1)S(1)}, bf16[48,768]{1,0:T(8,128)(2,1)S(1)}, u32[]{:S(2)}, u32[]{:S(2)}) collective-permute-start(bf16[48,768]{1,0:T(8,128)(2,1)S(1)} %pad_maximum_fusion), channel_id=1, source_target_pairs={{0,1},{1,2},{2,3},{3,4},{4,5},{5,6},{6,7},{7,8},{8,9},{9,10},{10,1... | collective-permute-start | bytes 221192 | tf_op jit(solution)/shard_map/ppermute | solution.py:409
  61.7 6.0 %collective-permute-start.1 = (bf16[48,768]{1,0:T(8,128)(2,1)S(1)}, bf16[48,768]{1,0:T(8,128)(2,1)S(1)}, u32[]{:S(2)}, u32[]{:S(2)}) collective-permute-start(bf16[48,768]{1,0:T(8,128)(2,1)S(1)} %pad_maximum_fusion.1), channel_id=1, source_target_pairs={{1,0},{2,1},{3,2},{4,3},{5,4},{6,5},{7,6},{8,7},{9,8},{10,9},{11,1... | collective-permute-start | bytes 221192 | tf_op jit(solution)/shard_map/ppermute | solution.py:412
  64.4 4.7 %copy-start.5 = (bf16[48,768]{1,0:T(8,128)(2,1)}, bf16[48,768]{1,0:T(8,128)(2,1)S(1)}, u32[]{:S(2)}) copy-start(bf16[48,768]{1,0:T(8,128)(2,1)S(1)} %collective-permute-done.refs_4_) | copy-start | bytes 221188
  67.7 1.4 copy-start.6
  69.1 0.8 copy-start.1
  108.8 4.0 %copy-start.7 = (bf16[128,768]{1,0:T(8,128)(2,1)S(1)}, bf16[128,768]{1,0:T(8,128)(2,1)}, u32[]{:S(2)}) copy-start(bf16[128,768]{1,0:T(8,128)(2,1)} %get-tuple-element.19) | copy-start | bytes 589828
  108.8 29.0 %all-to-all-start.3 = ((bf16[32,224,128]{2,1,0:T(8,128)(2,1)}), bf16[32,224,128]{2,1,0:T(8,128)(2,1)S(1)}, u32[]{:S(2)}, u32[]{:S(2)}) async-start(bf16[32,224,128]{2,1,0:T(8,128)(2,1)} %attend_backward.1), calls=%async_computation.3 | async-start | bytes 3670016 | tf_op jit(solution)/shard_map/all_to_all | solution.py:388
  112.9 14.1 %collective-permute-start.2 = (bf16[128,768]{1,0:T(8,128)(2,1)S(1)}, bf16[128,768]{1,0:T(8,128)(2,1)S(1)}, u32[]{:S(2)}, u32[]{:S(2)}) collective-permute-start(bf16[128,768]{1,0:T(8,128)(2,1)S(1)} %copy-done.7), channel_id=1, source_target_pairs={{0,32},{32,64},{64,96},{96,128},{128,160},{160,192},{192,224},{224... | collective-permute-start | bytes 589832 | tf_op jit(solution)/shard_map/ppermute | solution.py:465
  137.9 1.3 copy-start

commit v2 on v1

v2 whole, which is shorter than its diff:
```python
import math

import jax
import jax.numpy as jnp
from jax import lax
from jax.experimental import pallas as pl
from jax.experimental.pallas import tpu as pltpu
from jax.sharding import PartitionSpec as P

HEADS = 8
HEAD_DIM = 96
TAPS = 31
CH = 768
LANES = 128
EPS = 1e-06

SCALE = HEAD_DIM ** (-0.5)
SCALE2 = SCALE * math.log2(math.e)

F32 = jnp.float32
BF16 = jnp.bfloat16

KV_ROWS = slice(0, 96)
Q_ROWS = slice(96, 128)
PIECE_ROWS = 128
HALF = 64
SUB = 32

VMEM = pl.BlockSpec(memory_space=pltpu.VMEM)
SMEM = pl.BlockSpec(memory_space=pltpu.SMEM)
HBM = pl.BlockSpec(memory_space=pltpu.HBM)
MIB = 1024 * 1024


def lanes_of(rows):
    return lax.broadcasted_iota(jnp.int32, (rows, LANES), 1)


def roll_lanes(block, by):
    by = by % LANES
    return block if by == 0 else pltpu.roll(block, by, 1)


def heads_to_tiles(heads):
    lane = lanes_of(heads[0].shape[0])
    second = roll_lanes(heads[1], 96)
    third = roll_lanes(heads[2], 64)
    fourth = roll_lanes(heads[3], 32)
    return (
        jnp.where(lane < 96, heads[0], second),
        jnp.where(lane < 64, second, third),
        jnp.where(lane < 32, third, fourth),
    )


def tiles_to_heads(tiles):
    lane = lanes_of(tiles[0].shape[0])
    return (
        tiles[0],
        roll_lanes(jnp.where(lane >= 96, tiles[0], tiles[1]), 32),
        roll_lanes(jnp.where(lane >= 64, tiles[1], tiles[2]), 64),
        roll_lanes(tiles[2], 96),
    )


def call(kernel, out_shape, in_specs, out_specs, scratch, limit, flops, name, transcendentals=0):
    return pl.pallas_call(
        kernel,
        out_shape=out_shape,
        in_specs=in_specs,
        out_specs=out_specs,
        scratch_shapes=scratch,
        compiler_params=pltpu.CompilerParams(vmem_limit_bytes=limit * MIB),
        cost_estimate=pl.CostEstimate(
            flops=flops, bytes_accessed=2 * MIB, transcendentals=transcendentals
        ),
        name=name,
    )


def pack_kernel(groups, q_ref, k_ref, v_ref, send_ref, keys_t, values_t):
    frames = q_ref.shape[0]
    for source, turned in ((k_ref, keys_t), (v_ref, values_t)):
        for tile in range(CH // LANES):
            at = slice(tile * LANES, (tile + 1) * LANES)
            turned[at, :] = source[:, at].astype(F32).T
    lane = lanes_of(HEAD_DIM)
    for head in range(HEADS):
        at = slice(head * HEAD_DIM, (head + 1) * HEAD_DIM)
        keys_here, values_here = keys_t[at, :], values_t[at, :]
        halves = (
            jnp.where(lane < HALF, keys_here, roll_lanes(values_here, HALF)).astype(BF16),
            jnp.where(lane < HALF, roll_lanes(keys_here, HALF), values_here).astype(BF16),
        )
        for group in range(groups):
            send_ref[head * groups + group, KV_ROWS, :] = halves[group % 2]
    lane = lanes_of(frames)
    for half in range(2):
        tiles = [
            q_ref[:, (3 * half + i) * LANES : (3 * half + i + 1) * LANES].astype(F32)
            for i in range(3)
        ]
        for i, block in enumerate(tiles_to_heads(tiles)):
            block = jnp.where(lane < HEAD_DIM, block, 0.0).astype(BF16)
            for group in range(groups):
                send_ref[(4 * half + i) * groups + group, Q_ROWS, :] = block[
                    group * SUB : (group + 1) * SUB
                ]


def fill_half(half_ref, keys_t, values_t, keys, values):
    lane = lanes_of(HEAD_DIM)
    zeros = jnp.zeros((LANES - HEAD_DIM, LANES), F32)
    for pair in range(half_ref.shape[0] // 2):
        at = slice(pair * LANES, (pair + 1) * LANES)
        even = half_ref[2 * pair, KV_ROWS, :].astype(F32)
        odd = half_ref[2 * pair + 1, KV_ROWS, :].astype(F32)
        for turned, natural, block in (
            (keys_t, keys, jnp.where(lane < HALF, even, roll_lanes(odd, HALF))),
            (values_t, values, jnp.where(lane < HALF, roll_lanes(even, HALF), odd)),
        ):
            block = jnp.concatenate([block, zeros], axis=0)
            if turned is not None:
                turned[:, at] = block.astype(BF16)
            if natural is not None:
                natural[at, :] = block.T.astype(BF16)


def attend(got_ref, state, finish, block, chunk, keys, values, scores):
    key_count = keys.shape[1]
    per = block // SUB
    blocks = got_ref.shape[0] // per

    def rows_of(step):
        return got_ref[step * per : (step + 1) * per, Q_ROWS, :].reshape(block, LANES)

    def score(step, rows, start, peak):
        part = jnp.dot(rows, keys[:, start : start + chunk], preferred_element_type=F32)
        scores[step % 2, :, start : start + chunk] = part
        for tile in range(0, chunk, LANES):
            peak = jnp.maximum(peak, part[:, tile : tile + LANES])
        return peak

    lowest = jnp.full((block, LANES), -jnp.inf, F32)
    peak = lowest
    rows = rows_of(0)
    for start in range(0, key_count, chunk):
        peak = score(0, rows, start, peak)
    for step in range(blocks):
        at = slice(step * block, (step + 1) * block)
        top = jnp.broadcast_to(jnp.max(peak, axis=1, keepdims=True) * SCALE2, (block, LANES))
        if state is None:
            total = jnp.zeros((block, LANES), F32)
            result = jnp.zeros((block, LANES), F32)
        else:
            old = state[0][at, :]
            top = jnp.maximum(top, old)
            shrink = jnp.exp2(old - top)
            total = state[1][at, :] * shrink
            result = state[2][at, :] * shrink
        tops = jnp.concatenate([top] * (chunk // LANES), axis=1)
        peak = lowest
        if step + 1 < blocks:
            rows = rows_of(step + 1)
        for start in range(0, key_count, chunk):
            if step + 1 < blocks:
                peak = score(step + 1, rows, start, peak)
            weights = jnp.exp2(scores[step % 2, :, start : start + chunk] * SCALE2 - tops)
            for tile in range(0, chunk, LANES):
                total = total + weights[:, tile : tile + LANES]
            result = result + jnp.dot(
                weights.astype(BF16), values[start : start + chunk, :], preferred_element_type=F32
            )
        finish(at, top, total, result)


def forward_first_kernel(block, chunk, got_ref, top_ref, total_ref, result_ref, keys, values, scores):
    fill_half(got_ref, keys, None, None, values)

    def finish(at, top, total, result):
        top_ref[at, :] = top
        total_ref[at, :] = total
        result_ref[at, :] = result

    attend(got_ref, None, finish, block, chunk, keys, values, scores)


def forward_second_kernel(
    block,
    chunk,
    groups,
    place_ref,
    got_ref,
    swapped_ref,
    top_ref,
    total_ref,
    result_ref,
    send_ref,
    out_hbm,
    log_hbm,
    keys,
    values,
    scores,
    out_ref,
    log_ref,
    sems,
):
    fill_half(swapped_ref, keys, None, None, values)

    def finish(at, top, total, result):
        total = jnp.sum(total, axis=1, keepdims=True)
        out_ref[at, :] = (result / total).astype(BF16)
        log_ref[at, :] = top + jnp.log2(total)

    attend(got_ref, (top_ref, total_ref, result_ref), finish, block, chunk, keys, values, scores)
    copies = (
        pltpu.make_async_copy(out_ref, out_hbm, sems.at[0]),
        pltpu.make_async_copy(log_ref, log_hbm, sems.at[1]),
    )
    for copy in copies:
        copy.start()
    count = got_ref.shape[0]
    side = jnp.where(place_ref[0] % groups == groups - 1, -1, 1)
    lane = lanes_of(48)
    for device in range(count):
        near = jnp.clip(device + side, 0, count - 1)
        beside = out_ref[pl.ds(pl.multiple_of(near * SUB, SUB), SUB), :].astype(F32)
        own = out_ref[device * SUB : (device + 1) * SUB, :].astype(F32)
        tail = beside[16:32]
        spare = jnp.concatenate([roll_lanes(tail, by) for by in (96, 64, 32)], axis=0)
        piece = jnp.concatenate([own, beside[0:16]], axis=0)
        send_ref[device] = jnp.where(lane < HEAD_DIM, piece, spare).astype(BF16)
    for copy in copies:
        copy.wait()


def halo_of(piece):
    lane = lanes_of(16)
    tail = jnp.where(
        lane < 32,
        roll_lanes(piece[0:16], 32),
        jnp.where(lane < 64, roll_lanes(piece[16:32], 64), roll_lanes(piece[32:48], 96)),
    )
    return [piece[32:48], tail]


def conv_kernel(
    groups,
    count,
    place_ref,
    got_ref,
    resid_ref,
    cot_ref,
    before_ref,
    after_ref,
    gain_ref,
    taps_ref,
    send_ref,
    out_ref,
    grad_ref,
    mixed,
    normed,
    grad_conv,
    scaled,
    sums,
):
    frames = resid_ref.shape[0]
    sub = frames // groups
    wide = frames + 2 * sub
    half_taps = (TAPS - 1) // 2
    edge = 16
    inner = frames + 2 * edge
    tiles = CH // LANES
    place = place_ref[0]

    square = jnp.zeros((wide, LANES), F32)
    for half in range(2):
        heads = []
        for i in range(4):
            first = (4 * half + i) * groups
            before_piece = got_ref[first + groups - 1].astype(F32)
            after_piece = got_ref[first].astype(F32)
            parts = halo_of(before_piece)
            parts += [got_ref[first + group, 0:sub, :].astype(F32) for group in range(groups)]
            parts += halo_of(after_piece)
            heads.append(jnp.concatenate(parts, axis=0))
        for i, attended in enumerate(heads_to_tiles(heads)):
            at = slice((3 * half + i) * LANES, (3 * half + i + 1) * LANES)
            block = jnp.concatenate(
                [before_ref[0:sub, at], resid_ref[:, at], after_ref[0:sub, at]], axis=0
            ).astype(F32)
            block = block + attended
            mixed[:, at] = block
            square = square + block * block
    inverse = lax.rsqrt(jnp.sum(square, axis=1, keepdims=True) * (1.0 / CH) + EPS)

    row = lax.broadcasted_iota(jnp.int32, (wide, LANES), 0)
    inside = ((row >= sub) | (place > 0)) & ((row < sub + frames) | (place < count - 1))
    lo, hi = sub - edge, sub - edge + inner
    row_inner = lax.broadcasted_iota(jnp.int32, (inner, LANES), 0) + lo
    inside_inner = ((row_inner >= sub) | (place > 0)) & (
        (row_inner < sub + frames) | (place < count - 1)
    )
    own = slice(sub, sub + frames)
    inverse_own = inverse[sub : sub + frames]

    dots = jnp.zeros((frames, LANES), F32)
    for tile in range(tiles):
        at = slice(tile * LANES, (tile + 1) * LANES)
        gain_row = gain_ref[0:1, at]
        value = (mixed[:, at] * inverse * gain_row).astype(BF16).astype(F32)
        normed[...] = jnp.where(inside, value, 0.0)
        conv = jnp.zeros((inner, LANES), F32)
        for tap in range(TAPS):
            first = lo + tap - half_taps
            conv = conv + taps_ref[tap, :, at] * normed[first : first + inner, :]
        sig = jax.nn.sigmoid(conv)
        out_ref[:, at] = (
            mixed[own, at] + (conv * sig)[edge : edge + frames]
        ).astype(BF16)
        cot = jnp.concatenate(
            [before_ref[sub : sub + edge, at], cot_ref[:, at], after_ref[sub : sub + edge, at]],
            axis=0,
        ).astype(F32)
        value = (cot * sig * (1.0 + conv * (1.0 - sig))).astype(BF16).astype(F32)
        grad_conv[...] = jnp.where(inside_inner, value, 0.0)
        grad_normed = jnp.zeros((frames, LANES), F32)
        grad_own = grad_conv[edge : edge + frames, :]
        for tap in range(TAPS):
            first = edge + half_taps - tap
            grad_normed = (
                grad_normed
                + taps_ref[tap, :, at] * grad_conv[first : first + frames, :]
            )
            first = sub + tap - half_taps
            sums[tap : tap + 1, at] = jnp.sum(
                grad_own * normed[first : first + frames, :], axis=0, keepdims=True
            )
        unit = mixed[own, at] * inverse_own
        sums[TAPS : TAPS + 1, at] = jnp.sum(grad_normed * unit, axis=0, keepdims=True)
        here = grad_normed * gain_row
        scaled[:, at] = here
        dots = dots + here * unit
    mean = jnp.sum(dots, axis=1, keepdims=True) * (1.0 / CH)

    lane = lanes_of(sub)
    sublane = lax.broadcasted_iota(jnp.int32, (8, LANES), 0)
    for half in range(2):
        grads = []
        for i in range(3):
            at = slice((3 * half + i) * LANES, (3 * half + i + 1) * LANES)
            unit = mixed[own, at] * inverse_own
            grad = cot_ref[:, at].astype(F32) + inverse_own * (scaled[:, at] - unit * mean)
            grad_ref[:, at] = grad.astype(BF16)
            grads.append(grad)
        for i, block in enumerate(tiles_to_heads(grads)):
            for group in range(groups):
                device = (4 * half + i) * groups + group
                eight = jnp.zeros((8, LANES), F32)
                for tile in range(tiles):
                    line = sums[device : device + 1, tile * LANES : (tile + 1) * LANES]
                    eight = jnp.where(sublane == tile, line, eight)
                spare = jnp.concatenate(
                    [roll_lanes(eight, 96 - 32 * a) for a in range(4)], axis=0
                )
                piece = jnp.where(lane < HEAD_DIM, block[group * sub : (group + 1) * sub], spare)
                send_ref[device] = piece.astype(BF16)


def backward(
    half_ref,
    got_ref,
    grads_ref,
    out_hbm,
    log_hbm,
    part_ref,
    finish,
    block,
    chunk,
    keys_t,
    values_t,
    keys,
    grad_keys,
    grad_values,
    out_ref,
    log_ref,
    sems,
):
    copies = (
        pltpu.make_async_copy(out_hbm, out_ref, sems.at[0]),
        pltpu.make_async_copy(log_hbm, log_ref, sems.at[1]),
    )
    for copy in copies:
        copy.start()
    fill_half(half_ref, keys_t, values_t, keys, None)
    for copy in copies:
        copy.wait()
    key_count = keys.shape[0]
    per = block // SUB
    lane = lanes_of(block)
    for step in range(got_ref.shape[0] // per):
        sources = slice(step * per, (step + 1) * per)
        at = slice(step * block, (step + 1) * block)
        rows = got_ref[sources, Q_ROWS, :].reshape(block, LANES)
        grads = grads_ref[sources].reshape(block, LANES).astype(F32)
        grads = jnp.where(lane < HEAD_DIM, grads, 0.0)
        delta = jnp.sum(grads * out_ref[at, :].astype(F32), axis=1, keepdims=True)
        logs = jnp.concatenate([log_ref[at, :]] * (chunk // LANES), axis=1)
        rows_t = rows.astype(F32).T.astype(BF16)[0:HEAD_DIM]
        grads_t = grads.T.astype(BF16)[0:HEAD_DIM]
        grads = grads.astype(BF16)
        result = jnp.zeros((block, LANES), F32)
        for start in range(0, key_count, chunk):
            part = slice(start, start + chunk)
            logits = jnp.dot(rows, keys_t[:, part], preferred_element_type=F32)
            probs = jnp.exp2(logits * SCALE2 - logs)
            grad_probs = jnp.dot(grads, values_t[:, part], preferred_element_type=F32)
            grad_scores = (probs * (grad_probs - delta)).astype(BF16)
            result = result + jnp.dot(grad_scores, keys[part, :], preferred_element_type=F32)
            grad_k = jnp.dot(rows_t, grad_scores, preferred_element_type=F32)
            grad_v = jnp.dot(grads_t, probs.astype(BF16), preferred_element_type=F32)
            if step == 0:
                grad_keys[:, part] = grad_k
                grad_values[:, part] = grad_v
            else:
                grad_keys[:, part] += grad_k
                grad_values[:, part] += grad_v
        finish(step, sources, at, result * SCALE)
    lane = lanes_of(HEAD_DIM)
    for pair in range(got_ref.shape[0] // 2):
        at = slice(pair * LANES, (pair + 1) * LANES)
        grad_k = grad_keys[:, at] * SCALE
        grad_v = grad_values[:, at]
        part_ref[2 * pair] = jnp.where(lane < HALF, grad_k, roll_lanes(grad_v, HALF)).astype(BF16)
        part_ref[2 * pair + 1] = jnp.where(
            lane < HALF, roll_lanes(grad_k, HALF), grad_v
        ).astype(BF16)


def backward_first_kernel(
    block, chunk, swapped_ref, got_ref, grads_ref, out_hbm, log_hbm, part_ref, grad_q_ref, *scratch
):
    def finish(step, sources, at, result):
        grad_q_ref[at, :] = result

    backward(
        swapped_ref, got_ref, grads_ref, out_hbm, log_hbm, part_ref, finish, block, chunk, *scratch
    )


def backward_second_kernel(
    block,
    chunk,
    got_ref,
    grads_ref,
    out_hbm,
    log_hbm,
    grad_q_ref,
    part_ref,
    piece_ref,
    *scratch,
):
    sums = jnp.zeros((SUB, LANES), F32)
    for source in range(grads_ref.shape[0]):
        sums = sums + grads_ref[source].astype(F32)

    def finish(step, sources, at, result):
        result = (result + grad_q_ref[at, :]).reshape(-1, SUB, LANES)
        lane = lax.broadcasted_iota(jnp.int32, result.shape, 2)
        piece_ref[sources] = jnp.where(lane < HEAD_DIM, result, sums[None]).astype(BF16)

    backward(
        got_ref, got_ref, grads_ref, out_hbm, log_hbm, part_ref, finish, block, chunk, *scratch
    )


def join_kernel(part_ref, other_ref, piece_ref, send_ref):
    for device in range(part_ref.shape[0]):
        send_ref[device, KV_ROWS, :] = (
            part_ref[device].astype(F32) + other_ref[device].astype(F32)
        ).astype(BF16)
        send_ref[device, Q_ROWS, :] = piece_ref[device]


def unpack_kernel(
    groups, got_ref, arrived_ref, q_ref, k_ref, v_ref, gain_ref, taps_ref, next_ref, keys_t, values_t
):
    next_ref[...] = arrived_ref[...]
    count = got_ref.shape[0]
    lane = lanes_of(HEAD_DIM)
    for head in range(HEADS):
        at = slice(head * HEAD_DIM, (head + 1) * HEAD_DIM)
        low, high = (
            sum(
                got_ref[head * groups + group, KV_ROWS, :].astype(F32)
                for group in range(parity, groups, 2)
            )
            for parity in range(2)
        )
        keys_t[at, :] = jnp.where(lane < HALF, low, roll_lanes(high, HALF))
        values_t[at, :] = jnp.where(lane < HALF, roll_lanes(low, HALF), high)
    for target, turned in ((k_ref, keys_t), (v_ref, values_t)):
        for tile in range(CH // LANES):
            at = slice(tile * LANES, (tile + 1) * LANES)
            target[:, at] = turned[at, :].T.astype(BF16)
    for half in range(2):
        heads = [
            jnp.concatenate(
                [got_ref[(4 * half + i) * groups + group, Q_ROWS, :] for group in range(groups)],
                axis=0,
            ).astype(F32)
            for i in range(4)
        ]
        for i, block in enumerate(heads_to_tiles(heads)):
            at = slice((3 * half + i) * LANES, (3 * half + i + 1) * LANES)
            q_ref[:, at] = block.astype(BF16)
    lane = lanes_of(8)
    for device in range(count):
        piece = got_ref[device, Q_ROWS, :].astype(F32)
        eight = roll_lanes(piece[0:8], 32)
        for a in range(1, 4):
            eight = jnp.where(
                lane >= 32 * a, roll_lanes(piece[8 * a : 8 * a + 8], 32 * a - 96), eight
            )
        for tile in range(CH // LANES):
            at = slice(tile * LANES, (tile + 1) * LANES)
            if device < TAPS:
                taps_ref[device, :, at] = eight[tile : tile + 1]
            else:
                gain_ref[:, at] = eight[tile : tile + 1]


def exchange(pieces):
    return lax.all_to_all(pieces, "tm", split_axis=0, concat_axis=0, tiled=True)


def local(resid, queries, keys, values, gain, taps, cotangent):
    count = lax.axis_size("tm")
    sections = lax.axis_size("section")
    groups = count // HEADS
    frames = resid.shape[1]
    total = frames * count
    own = total // groups
    half = total // 2
    place = lax.axis_index("tm").astype(jnp.int32).reshape(1)
    edge = 16
    matmul = 2 * own * half * LANES

    resid, queries, keys, values, cotangent = (
        array[0] for array in (resid, queries, keys, values, cotangent)
    )
    up = [(i, i + 1) for i in range(count - 1)]
    down = [(i + 1, i) for i in range(count - 1)]
    partner = [(i, i ^ 1) for i in range(count)]
    before = lax.ppermute(
        jnp.concatenate([resid[frames - SUB :], cotangent[frames - edge :]], axis=0), "tm", up
    )
    after = lax.ppermute(jnp.concatenate([resid[:SUB], cotangent[:edge]], axis=0), "tm", down)

    shape = jax.ShapeDtypeStruct
    pieces = shape((count, PIECE_ROWS, LANES), BF16)
    rows_shape = shape((frames, CH), BF16)
    own_shape = shape((own, LANES), F32)
    sent = call(
        lambda *refs: pack_kernel(groups, *refs),
        pieces,
        [VMEM] * 3,
        VMEM,
        [pltpu.VMEM((CH, LANES), F32)] * 2,
        8,
        1000000,
        "pack_qkv",
    )(queries, keys, values)
    got = exchange(sent)
    swapped = lax.ppermute(got, "tm", partner)

    block, chunk = 256, 512
    attend_scratch = [
        pltpu.VMEM((LANES, half), BF16),
        pltpu.VMEM((half, LANES), BF16),
        pltpu.VMEM((2, block, half), F32),
    ]
    state = call(
        lambda *refs: forward_first_kernel(block, chunk, *refs),
        (own_shape,) * 3,
        [VMEM],
        (VMEM,) * 3,
        attend_scratch,
        24,
        2 * matmul,
        "attend_forward_own",
        own * half,
    )(got)
    results, head_out, logs = call(
        lambda *refs: forward_second_kernel(block, chunk, groups, *refs),
        (shape((count, 48, LANES), BF16), shape((own, LANES), BF16), own_shape),
        [SMEM] + [VMEM] * 5,
        (VMEM, HBM, HBM),
        attend_scratch
        + [
            pltpu.VMEM((own, LANES), BF16),
            pltpu.VMEM((own, LANES), F32),
            pltpu.SemaphoreType.DMA((2,)),
        ],
        24,
        2 * matmul,
        "attend_forward_other",
        own * half,
    )(place, got, swapped, *state)
    returned = exchange(results)

    grads_sent, block_out, grad_resid = call(
        lambda *refs: conv_kernel(groups, count, *refs),
        (shape((count, SUB, LANES), BF16), rows_shape, rows_shape),
        [SMEM] + [VMEM] * 7,
        (VMEM,) * 3,
        [
            pltpu.VMEM((frames + 2 * SUB, CH), F32),
            pltpu.VMEM((frames + 2 * SUB, LANES), F32),
            pltpu.VMEM((frames + 2 * edge, LANES), F32),
            pltpu.VMEM((frames, CH), F32),
            pltpu.VMEM((TAPS + 1, CH), F32),
        ],
        16,
        10000000,
        "conv_block",
    )(place, returned, resid, cotangent, before, after, gain, taps.reshape(TAPS, 1, CH))
    grads_got = exchange(grads_sent)
    arrived = lax.ppermute(
        block_out, "section", [(i, (i + 1) % sections) for i in range(sections)]
    )

    block, chunk = 512, 512
    backward_scratch = [
        pltpu.VMEM((LANES, half), BF16),
        pltpu.VMEM((LANES, half), BF16),
        pltpu.VMEM((half, LANES), BF16),
        pltpu.VMEM((HEAD_DIM, half), F32),
        pltpu.VMEM((HEAD_DIM, half), F32),
        pltpu.VMEM((own, LANES), BF16),
        pltpu.VMEM((own, LANES), F32),
        pltpu.SemaphoreType.DMA((2,)),
    ]
    part_shape = shape((count, HEAD_DIM, LANES), BF16)
    other_part, grad_q = call(
        lambda *refs: backward_first_kernel(block, chunk, *refs),
        (part_shape, own_shape),
        [VMEM] * 3 + [HBM] * 2,
        (VMEM,) * 2,
        backward_scratch,
        24,
        5 * matmul,
        "attend_backward_other",
        own * half,
    )(swapped, got, grads_got, head_out, logs)
    arrived_part = lax.ppermute(other_part, "tm", partner)
    own_part, grad_q_pieces = call(
        lambda *refs: backward_second_kernel(block, chunk, *refs),
        (part_shape, shape((count, SUB, LANES), BF16)),
        [VMEM] * 2 + [HBM] * 2 + [VMEM],
        (VMEM,) * 2,
        backward_scratch,
        24,
        5 * matmul,
        "attend_backward_own",
        own * half,
    )(got, grads_got, head_out, logs, grad_q)
    grads_out = call(
        join_kernel,
        pieces,
        [VMEM] * 3,
        VMEM,
        [],
        8,
        1000000,
        "join_grads",
    )(own_part, arrived_part, grad_q_pieces)
    back = exchange(grads_out)

    grad_q, grad_k, grad_v, grad_gain, grad_taps, next_input = call(
        lambda *refs: unpack_kernel(groups, *refs),
        (
            rows_shape,
            rows_shape,
            rows_shape,
            shape((1, CH), F32),
            shape((TAPS, 1, CH), F32),
            rows_shape,
        ),
        [VMEM] * 2,
        (VMEM,) * 6,
        [pltpu.VMEM((CH, LANES), F32)] * 2,
        8,
        1000000,
        "unpack_grads",
    )(back, arrived)
    return (
        next_input[None],
        grad_resid[None],
        grad_q[None],
        grad_k[None],
        grad_v[None],
        grad_gain,
        grad_taps.reshape(1, TAPS, CH),
    )


def solution(mesh):
    rows = P("section", "tm", None)
    in_specs = (rows, rows, rows, rows, P("section", None), P("section", None, None), rows)
    out_specs = (rows, rows, rows, rows, rows, P("section", None), P("section", None, None))
    return jax.shard_map(local, mesh=mesh, in_specs=in_specs, out_specs=out_specs, check_vma=False)
```

time: 145 us -> 118 us (0.81)
  waiting for transfers between devices: 52.7 us -> 19.5 us
  blocking collectives: 16 us -> 43.5 us
  Pallas kernels: 39.6 us -> 28.6 us
  starting transfers between devices: 27.9 us -> 20.3 us
  local copies, waits for them, and re-layouts: 7.05 us -> 4.34 us
    all_to_all x3 -> x2, waiting for transfers between devices: 37.2 us -> 3.08 us  [exchange(): return lax.all_to_all(pieces, 'tm', split_axis=0, concat_axis=0, tiled=True)]
    all_to_all x1 -> x2, blocking collectives: 16 us -> 43.5 us  [exchange(): return lax.all_to_all(pieces, 'tm', split_axis=0, concat_axis=0, tiled=True)]
    all_to_all x3 -> x2, starting transfers between devices: 20.5 us -> 7.66 us  [exchange(): return lax.all_to_all(pieces, 'tm', split_axis=0, concat_axis=0, tiled=True)]
    pallas_call x4 -> x7, Pallas kernels: 37 us -> 27.3 us  [the longest x1 6.42 us: local(): call(lambda *refs: backward_second_kernel(block, chunk, *refs), (part_sha...]
    ppermute x2 -> x4, starting transfers between devices: 5.47 us -> 10.4 us  [the longest x1 3.66 us: local(): lax.ppermute(jnp.concatenate([resid[frames - SUB:], cotangent[frames - ed...]
    unnamed x19 -> x22, local copies, waits for them, and re-layouts: 6.28 us -> 4.33 us
    ppermute x2 -> x4, waiting for transfers between devices: 3.38 us -> 3.86 us  [the longest x1 3.85 us: local(): lax.ppermute(jnp.concatenate([resid[:SUB], cotangent[:edge]], axis=0), 't...]
  transfers between devices with their start and end apart: 6 -> 7, of which waited for: 6 -> 4; matrix products, arithmetic and copies ran while one was open for 1% -> 0% of each run, Pallas kernels for 0% -> 8%
where the time goes in v2:
time: 118 us; the launch traced here: 117 us
  blocking collectives  43.5 us (37%)
  Pallas kernels  28.6 us (24%)
  starting transfers between devices  20.3 us (17%)
  waiting for transfers between devices  19.5 us (17%)
  local copies, waits for them, and re-layouts  4.34 us (4%)
    all_to_all x2, blocking collectives, exchange(): return lax.all_to_all(pieces, 'tm', split_axis=0, concat_axis=0, tiled=True)  43.5 us
    ppermute x1, waiting for transfers between devices, local(): lax.ppermute(block_out, 'section', [(i, (i + 1) % sections) for i in rang...  12.6 us
    all_to_all x2, starting transfers between devices, exchange(): return lax.all_to_all(pieces, 'tm', split_axis=0, concat_axis=0, tiled=True)  7.66 us
    pallas_call x1, Pallas kernels, local(): call(lambda *refs: backward_second_kernel(block, chunk, *refs), (part_sha...  6.42 us
    pallas_call x1, Pallas kernels, local(): call(lambda *refs: backward_first_kernel(block, chunk, *refs), (part_shap...  6.38 us
    pallas_call x1, Pallas kernels, local(): call(lambda *refs: conv_kernel(groups, count, *refs), (shape((count, SUB,...  5.4 us
    pallas_call x1, Pallas kernels, local(): call(lambda *refs: forward_second_kernel(block, chunk, groups, *refs), (s...  4.45 us
    unnamed x22, local copies, waits for them, and re-layouts  4.33 us
  transfers between devices with their start and end apart: 7, of which 4 were waited for; matrix products, arithmetic and copies ran while one was open for 0% of the time, Pallas kernels for 8%

profile of v2, /device:TPU:1, one launch (start us, length us, event | category | flops | bytes accessed | tf_op | source)
XLA Modules:
  0.0 117.1 jit_solution(674749454241994511)
XLA Ops:
  0.6 0.9 copy-done.2
  1.6 0.9 copy-done.3
  2.5 0.9 copy-done.4
  3.8 27.0 %all_to_all.20.refs_0_.refs_1_ = bf16[32,128,128]{2,1,0:T(8,128)(2,1)S(1)} all-to-all(bf16[32,128,128]{2,1,0:T(8,128)(2,1)S(1)} %pack_qkv.1), channel_id=1, replica_groups=mesh['section'=16,'tm'=32] {'tm'}, dimensions={0} | all-to-all | bytes 2097152 | tf_op jit(solution)/shard_map/all_to_all | solution.py:534
  30.8 2.3 %collective-permute-start = (bf16[32,128,128]{2,1,0:T(8,128)(2,1)S(1)}, bf16[32,128,128]{2,1,0:T(8,128)(2,1)S(1)}, u32[]{:S(2)}, u32[]{:S(2)}) collective-permute-start(bf16[32,128,128]{2,1,0:T(8,128)(2,1)S(1)} %all_to_all.20.refs_0_.refs_1_), channel_id=1, source_target_pairs={{0,1},{1,0},{2,3},{3,2},{4,5},{5,4},{6,7},{7,6},{8,9},{9,8},{10,11... | collective-permute-start | bytes 3145736 | tf_op jit(solution)/shard_map/ppermute | solution.py:575
  33.1 3.1 %attend_forward_own.1 = (f32[1024,128]{1,0:T(8,128)S(1)}, f32[1024,128]{1,0:T(8,128)S(1)}, f32[1024,128]{1,0:T(8,128)S(1)}) custom-call(bf16[32,128,128]{2,1,0:T(8,128)(2,1)S(1)} %all_to_all.20.refs_0_.refs_1_), custom_call_target="tpu_custom_call" | custom-call | flops 1073741824 | bytes 2097152 | tf_op jit(solution)/shard_map/attend_forward_own/pallas_call | solution.py:583
  36.2 4.4 %attend_forward_other.1 = (bf16[32,48,128]{2,1,0:T(8,128)(2,1)}, bf16[1024,128]{1,0:T(8,128)(2,1)S(1)}, f32[1024,128]{1,0:T(8,128)S(1)}) custom-call(s32[1]{0:T(128)} %bitcast.3.refs_0_, bf16[32,128,128]{2,1,0:T(8,128)(2,1)S(1)} %all_to_all.20.refs_0_.refs_1_, bf16[32,128,128]{2,1,0:T(8,128)(2,1)S(1)} %collective-permute-done.refs_2_.refs_0_, ...), custom_call_target="tpu_custom_call" | custom-call | flops 1073741824 | bytes 2097152 | tf_op jit(solution)/shard_map/attend_forward_other/pallas_call | solution.py:594
  40.7 0.8 copy-done.7
  41.5 0.7 copy-done.9
  42.2 3.8 %all-to-all-start.1 = ((bf16[32,48,128]{2,1,0:T(8,128)(2,1)}), bf16[32,48,128]{2,1,0:T(8,128)(2,1)S(1)}, u32[]{:S(2)}, u32[]{:S(2)}) async-start(bf16[32,48,128]{2,1,0:T(8,128)(2,1)} %get-tuple-element.29), calls=%async_computation.1 | async-start | bytes 786432 | tf_op jit(solution)/shard_map/all_to_all | solution.py:534
  46.1 3.7 %collective-permute-start.1 = (bf16[48,768]{1,0:T(8,128)(2,1)S(1)}, bf16[48,768]{1,0:T(8,128)(2,1)S(1)}, u32[]{:S(2)}, u32[]{:S(2)}) collective-permute-start(bf16[48,768]{1,0:T(8,128)(2,1)S(1)} %pad_maximum_fusion), channel_id=1, source_target_pairs={{0,1},{1,2},{2,3},{3,4},{4,5},{5,6},{6,7},{7,8},{8,9},{9,10},{10,1... | collective-permute-start | bytes 221192 | tf_op jit(solution)/shard_map/ppermute | solution.py:555
  49.8 2.1 %collective-permute-start.2 = (bf16[48,768]{1,0:T(8,128)(2,1)S(1)}, bf16[48,768]{1,0:T(8,128)(2,1)S(1)}, u32[]{:S(2)}, u32[]{:S(2)}) collective-permute-start(bf16[48,768]{1,0:T(8,128)(2,1)S(1)} %pad_maximum_fusion.1), channel_id=1, source_target_pairs={{1,0},{2,1},{3,2},{4,3},{5,4},{6,5},{7,6},{8,7},{9,8},{10,9},{11,1... | collective-permute-start | bytes 221192 | tf_op jit(solution)/shard_map/ppermute | solution.py:558
  51.9 3.8 %collective-permute-done.2.refs_5_ = bf16[48,768]{1,0:T(8,128)(2,1)S(1)} collective-permute-done((bf16[48,768]{1,0:T(8,128)(2,1)S(1)}, bf16[48,768]{1,0:T(8,128)(2,1)S(1)}, u32[]{:S(2)}, u32[]{:S(2)}) %collective-permute-start.2) | collective-permute-done | bytes 73760 | tf_op jit(solution)/shard_map/ppermute | solution.py:558
  56.4 5.4 %conv_block.1 = (bf16[32,32,128]{2,1,0:T(8,128)(2,1)S(1)}, bf16[128,768]{1,0:T(8,128)(2,1)S(1)}, bf16[128,768]{1,0:T(8,128)(2,1)}) custom-call(s32[1]{0:T(128)} %bitcast.3.refs_0_, bf16[32,48,128]{2,1,0:T(8,128)(2,1)S(1)} %all-to-all-done.1.refs_1_, bf16[128,768]{1,0:T(8,128)(2,1)S(1)} %bitcast.21, bf16[128,768]{1,0:T(8,128)(2,1)S(1)} %bitcast.22, ...), custom_call_target="tpu_custom_call" | custom-call | flops 10000000 | bytes 2097152 | tf_op jit(solution)/shard_map/conv_block/pallas_call | solution.py:612
  61.8 16.5 %all_to_all.21.refs_2_.refs_1_ = bf16[32,32,128]{2,1,0:T(8,128)(2,1)S(1)} all-to-all(bf16[32,32,128]{2,1,0:T(8,128)(2,1)S(1)} %get-tuple-element.30), channel_id=1, replica_groups=mesh['section'=16,'tm'=32] {'tm'}, dimensions={0} | all-to-all | bytes 524288 | tf_op jit(solution)/shard_map/all_to_all | solution.py:534
  78.3 6.4 %attend_backward_other.1 = (bf16[32,96,128]{2,1,0:T(8,128)(2,1)S(1)}, f32[1024,128]{1,0:T(8,128)S(1)}) custom-call(bf16[32,128,128]{2,1,0:T(8,128)(2,1)S(1)} %collective-permute-done.refs_2_.refs_0_, bf16[32,128,128]{2,1,0:T(8,128)(2,1)S(1)} %all_to_all.20.refs_0_.refs_1_, bf16[32,32,128]{2,1,0:T(8,128)(2,1)S(1)} %all_to_all.21.refs_2_.refs_1_, ...), custom_call_target="tpu_custom_call" | custom-call | flops 2684354560 | bytes 2097152 | tf_op jit(solution)/shard_map/attend_backward_other/pallas_call | solution.py:645
  84.7 2.4 %collective-permute-start.3 = (bf16[32,96,128]{2,1,0:T(8,128)(2,1)S(1)}, bf16[32,96,128]{2,1,0:T(8,128)(2,1)S(1)}, u32[]{:S(2)}, u32[]{:S(2)}) collective-permute-start(bf16[32,96,128]{2,1,0:T(8,128)(2,1)S(1)} %get-tuple-element.35), channel_id=1, source_target_pairs={{0,1},{1,0},{2,3},{3,2},{4,5},{5,4},{6,7},{7,6},{8,9},{9,8},{10,11... | collective-permute-start | bytes 2359304 | tf_op jit(solution)/shard_map/ppermute | solution.py:656
  87.0 6.4 %attend_backward_own.1 = (bf16[32,96,128]{2,1,0:T(8,128)(2,1)S(1)}, bf16[32,32,128]{2,1,0:T(8,128)(2,1)S(1)}) custom-call(bf16[32,128,128]{2,1,0:T(8,128)(2,1)S(1)} %all_to_all.20.refs_0_.refs_1_, bf16[32,32,128]{2,1,0:T(8,128)(2,1)S(1)} %all_to_all.21.refs_2_.refs_1_, bf16[1024,128]{1,0:T(8,128)(2,1)S(1)} %copy-done.10, f32[1024,128]{1,0:T(8,128)S(1)} %copy-done.8, ...), custom_call_target="tpu_custom_call" | custom-call | flops 2684354560 | bytes 2097152 | tf_op jit(solution)/shard_map/attend_backward_own/pallas_call | solution.py:657
  93.5 1.2 %join_grads.1 = bf16[32,128,128]{2,1,0:T(8,128)(2,1)} custom-call(bf16[32,96,128]{2,1,0:T(8,128)(2,1)S(1)} %get-tuple-element.34.part_ref, bf16[32,96,128]{2,1,0:T(8,128)(2,1)S(1)} %collective-permute-done.3.other_ref, bf16[32,32,128]{2,1,0:T(8,128)(2,1)S(1)} %get-tuple-element.36.piece_ref), custom_call_target="tpu_custom_call" | custom-call | flops 1000000 | bytes 2097152 | tf_op jit(solution)/shard_map/join_grads/pallas_call | solution.py:668
  94.7 3.9 %all-to-all-start.3 = ((bf16[32,128,128]{2,1,0:T(8,128)(2,1)}), bf16[32,128,128]{2,1,0:T(8,128)(2,1)S(1)}, u32[]{:S(2)}, u32[]{:S(2)}) async-start(bf16[32,128,128]{2,1,0:T(8,128)(2,1)} %join_grads.1), calls=%async_computation.3 | async-start | bytes 2097152 | tf_op jit(solution)/shard_map/all_to_all | solution.py:534
  98.5 2.3 %collective-permute-start.4 = (bf16[128,768]{1,0:T(8,128)(2,1)S(1)}, bf16[128,768]{1,0:T(8,128)(2,1)S(1)}, u32[]{:S(2)}, u32[]{:S(2)}) collective-permute-start(bf16[128,768]{1,0:T(8,128)(2,1)S(1)} %get-tuple-element.37), channel_id=1, source_target_pairs={{0,32},{32,64},{64,96},{96,128},{128,160},{160,192},{192,224},{224... | collective-permute-start | bytes 589832 | tf_op jit(solution)/shard_map/ppermute | solution.py:629
  100.8 12.6 %collective-permute-done.4.refs_1_ = bf16[128,768]{1,0:T(8,128)(2,1)S(1)} collective-permute-done((bf16[128,768]{1,0:T(8,128)(2,1)S(1)}, bf16[128,768]{1,0:T(8,128)(2,1)S(1)}, u32[]{:S(2)}, u32[]{:S(2)}) %collective-permute-start.4) | collective-permute-done | bytes 196640 | tf_op jit(solution)/shard_map/ppermute | solution.py:629
  113.4 2.5 %all-to-all-done.3.refs_0_ = bf16[32,128,128]{2,1,0:T(8,128)(2,1)S(1)} async-done(((bf16[32,128,128]{2,1,0:T(8,128)(2,1)}), bf16[32,128,128]{2,1,0:T(8,128)(2,1)S(1)}, u32[]{:S(2)}, u32[]{:S(2)}) %all-to-all-start.3) | async-done | bytes 1048608 | tf_op jit(solution)/shard_map/all_to_all | solution.py:534
  115.8 1.3 %unpack_grads.1 = (bf16[128,768]{1,0:T(8,128)(2,1)}, bf16[128,768]{1,0:T(8,128)(2,1)}, bf16[128,768]{1,0:T(8,128)(2,1)}, f32[1,768]{1,0:T(1,128)}, f32[31,1,768]{2,1,0:T(1,128)}, /*index=5*/bf16[128,768]{1,0:T(8,128)(2,1)}) custom-call(bf16[32,128,128]{2,1,0:T(8,128)(2,1)S(1)} %all-to-all-done.3.refs_0_, bf16[128,768]{1,0:T(8,128)(2,1)S(1)} %collective-permute-done.4.refs_1_), custom_call_target="tpu_custom_call" | custom-call | flops 1000000 | bytes 2097152 | tf_op jit(solution)/shard_map/unpack_grads/pallas_call | solution.py:680
  (26 shorter events, 1.1 us)
Async XLA Ops:
  0.6 0.9 copy-start.2
  1.6 0.9 copy-start.3
  2.5 0.9 copy-start.4
  3.8 29.3 %copy-start = (bf16[1,128,768]{2,1,0:T(8,128)(2,1)S(1)}, bf16[1,128,768]{2,1,0:T(8,128)(2,1)}, u32[]{:S(2)}) copy-start(bf16[1,128,768]{2,1,0:T(8,128)(2,1)} %param.7) | copy-start | bytes 589828
  30.8 5.4 %collective-permute-start = (bf16[32,128,128]{2,1,0:T(8,128)(2,1)S(1)}, bf16[32,128,128]{2,1,0:T(8,128)(2,1)S(1)}, u32[]{:S(2)}, u32[]{:S(2)}) collective-permute-start(bf16[32,128,128]{2,1,0:T(8,128)(2,1)S(1)} %all_to_all.20.refs_0_.refs_1_), channel_id=1, source_target_pairs={{0,1},{1,0},{2,3},{3,2},{4,5},{5,4},{6,7},{7,6},{8,9},{9,8},{10,11... | collective-permute-start | bytes 3145736 | tf_op jit(solution)/shard_map/ppermute | solution.py:575
  40.7 0.8 copy-start.7
  41.5 0.7 copy-start.9
  42.2 3.8 %copy-start.1 = (bf16[1,128,768]{2,1,0:T(8,128)(2,1)S(1)}, bf16[1,128,768]{2,1,0:T(8,128)(2,1)}, u32[]{:S(2)}) copy-start(bf16[1,128,768]{2,1,0:T(8,128)(2,1)} %param.13) | copy-start | bytes 589828
  42.2 14.2 %all-to-all-start.1 = ((bf16[32,48,128]{2,1,0:T(8,128)(2,1)}), bf16[32,48,128]{2,1,0:T(8,128)(2,1)S(1)}, u32[]{:S(2)}, u32[]{:S(2)}) async-start(bf16[32,48,128]{2,1,0:T(8,128)(2,1)} %get-tuple-element.29), calls=%async_computation.1 | async-start | bytes 786432 | tf_op jit(solution)/shard_map/all_to_all | solution.py:534
  46.1 10.3 %copy-start.5 = (f32[1,31,768]{2,0,1:T(1,128)S(1)}, f32[1,31,768]{2,0,1:T(1,128)}, u32[]{:S(2)}) copy-start(f32[1,31,768]{2,0,1:T(1,128)} %param.12) | copy-start | bytes 285700
  46.1 5.8 %collective-permute-start.1 = (bf16[48,768]{1,0:T(8,128)(2,1)S(1)}, bf16[48,768]{1,0:T(8,128)(2,1)S(1)}, u32[]{:S(2)}, u32[]{:S(2)}) collective-permute-start(bf16[48,768]{1,0:T(8,128)(2,1)S(1)} %pad_maximum_fusion), channel_id=1, source_target_pairs={{0,1},{1,2},{2,3},{3,4},{4,5},{5,6},{6,7},{7,8},{8,9},{9,10},{10,1... | collective-permute-start | bytes 221192 | tf_op jit(solution)/shard_map/ppermute | solution.py:555
  49.8 6.6 %copy-start.6 = (f32[1,768]{1,0:T(1,128)S(1)}, f32[1,768]{1,0:T(1,128)}, u32[]{:S(2)}) copy-start(f32[1,768]{1,0:T(1,128)} %refs_6_.1) | copy-start | bytes 9220
  49.8 6.0 %collective-permute-start.2 = (bf16[48,768]{1,0:T(8,128)(2,1)S(1)}, bf16[48,768]{1,0:T(8,128)(2,1)S(1)}, u32[]{:S(2)}, u32[]{:S(2)}) collective-permute-start(bf16[48,768]{1,0:T(8,128)(2,1)S(1)} %pad_maximum_fusion.1), channel_id=1, source_target_pairs={{1,0},{2,1},{3,2},{4,3},{5,4},{6,5},{7,6},{8,7},{9,8},{10,9},{11,1... | collective-permute-start | bytes 221192 | tf_op jit(solution)/shard_map/ppermute | solution.py:558
  56.4 21.9 %copy-start.8 = (f32[1024,128]{1,0:T(8,128)S(1)}, f32[1024,128]{1,0:T(8,128)}, u32[]{:S(2)}) copy-start(f32[1024,128]{1,0:T(8,128)} %copy-done.7) | copy-start | bytes 1572868
  61.8 16.5 %copy-start.10 = (bf16[1024,128]{1,0:T(8,128)(2,1)S(1)}, bf16[1024,128]{1,0:T(8,128)(2,1)}, u32[]{:S(2)}) copy-start(bf16[1024,128]{1,0:T(8,128)(2,1)} %copy-done.9) | copy-start | bytes 786436
  84.7 8.8 %collective-permute-start.3 = (bf16[32,96,128]{2,1,0:T(8,128)(2,1)S(1)}, bf16[32,96,128]{2,1,0:T(8,128)(2,1)S(1)}, u32[]{:S(2)}, u32[]{:S(2)}) collective-permute-start(bf16[32,96,128]{2,1,0:T(8,128)(2,1)S(1)} %get-tuple-element.35), channel_id=1, source_target_pairs={{0,1},{1,0},{2,3},{3,2},{4,5},{5,4},{6,7},{7,6},{8,9},{9,8},{10,11... | collective-permute-start | bytes 2359304 | tf_op jit(solution)/shard_map/ppermute | solution.py:656
  94.7 21.1 %all-to-all-start.3 = ((bf16[32,128,128]{2,1,0:T(8,128)(2,1)}), bf16[32,128,128]{2,1,0:T(8,128)(2,1)S(1)}, u32[]{:S(2)}, u32[]{:S(2)}) async-start(bf16[32,128,128]{2,1,0:T(8,128)(2,1)} %join_grads.1), calls=%async_computation.3 | async-start | bytes 2097152 | tf_op jit(solution)/shard_map/all_to_all | solution.py:534
  98.5 14.8 %collective-permute-start.4 = (bf16[128,768]{1,0:T(8,128)(2,1)S(1)}, bf16[128,768]{1,0:T(8,128)(2,1)S(1)}, u32[]{:S(2)}, u32[]{:S(2)}) collective-permute-start(bf16[128,768]{1,0:T(8,128)(2,1)S(1)} %get-tuple-element.37), channel_id=1, source_target_pairs={{0,32},{32,64},{64,96},{96,128},{128,160},{160,192},{192,224},{224... | collective-permute-start | bytes 589832 | tf_op jit(solution)/shard_map/ppermute | solution.py:629

commit v3 on v2

--- a/solution.py
+++ b/solution.py
@@ -28,7 +28,7 @@
 
 VMEM = pl.BlockSpec(memory_space=pltpu.VMEM)
 SMEM = pl.BlockSpec(memory_space=pltpu.SMEM)
-HBM = pl.BlockSpec(memory_space=pltpu.HBM)
+ANY = pl.BlockSpec(memory_space=pl.ANY)
 MIB = 1024 * 1024
 
 
@@ -174,7 +174,17 @@
         finish(at, top, total, result)
 
 
-def forward_first_kernel(block, chunk, got_ref, top_ref, total_ref, result_ref, keys, values, scores):
+def forward_first_kernel(
+    block,
+    chunk,
+    got_ref,
+    top_ref,
+    total_ref,
+    result_ref,
+    keys,
+    values,
+    scores,
+):
     fill_half(got_ref, keys, None, None, values)
 
     def finish(at, top, total, result):
@@ -196,29 +206,25 @@
     total_ref,
     result_ref,
     send_ref,
-    out_hbm,
-    log_hbm,
+    out_ref,
     keys,
     values,
     scores,
-    out_ref,
-    log_ref,
-    sems,
 ):
     fill_half(swapped_ref, keys, None, None, values)
 
     def finish(at, top, total, result):
         total = jnp.sum(total, axis=1, keepdims=True)
-        out_ref[at, :] = (result / total).astype(BF16)
-        log_ref[at, :] = top + jnp.log2(total)
+        rest = top + jnp.log2(total)
+        merged = result / total
+        lane = lanes_of(block)
+        for spot in range(HEAD_DIM, HEAD_DIM + 3):
+            part = rest.astype(BF16).astype(F32)
+            merged = jnp.where(lane == spot, part, merged)
+            rest = rest - part
+        out_ref[at, :] = merged.astype(BF16)
 
     attend(got_ref, (top_ref, total_ref, result_ref), finish, block, chunk, keys, values, scores)
-    copies = (
-        pltpu.make_async_copy(out_ref, out_hbm, sems.at[0]),
-        pltpu.make_async_copy(log_ref, log_hbm, sems.at[1]),
-    )
-    for copy in copies:
-        copy.start()
     count = got_ref.shape[0]
     side = jnp.where(place_ref[0] % groups == groups - 1, -1, 1)
     lane = lanes_of(48)
@@ -230,8 +236,6 @@
         spare = jnp.concatenate([roll_lanes(tail, by) for by in (96, 64, 32)], axis=0)
         piece = jnp.concatenate([own, beside[0:16]], axis=0)
         send_ref[device] = jnp.where(lane < HEAD_DIM, piece, spare).astype(BF16)
-    for copy in copies:
-        copy.wait()
 
 
 def halo_of(piece):
@@ -367,34 +371,47 @@
                 send_ref[device] = piece.astype(BF16)
 
 
-def backward(
+def prepare_kernel(
+    block,
+    chunk,
     half_ref,
     got_ref,
+    out_ref,
+    unused_ref,
+    weights_ref,
+    values_t,
+    keys,
+    keys_t,
+):
+    fill_half(half_ref, keys_t, values_t, keys, None)
+    per = block // SUB
+    lane = lanes_of(block)
+    in_log = (lane >= HEAD_DIM) & (lane < HEAD_DIM + 3)
+    for step in range(got_ref.shape[0] // per):
+        at = slice(step * block, (step + 1) * block)
+        rows = got_ref[step * per : (step + 1) * per, Q_ROWS, :].reshape(block, LANES)
+        logs = jnp.where(in_log, out_ref[at, :].astype(F32), 0.0)
+        logs = jnp.sum(logs, axis=1, keepdims=True)
+        for start in range(0, keys.shape[0], chunk):
+            part = slice(start, start + chunk)
+            logits = jnp.dot(rows, keys_t[:, part], preferred_element_type=F32)
+            weights_ref[at, part] = jnp.exp2(logits * SCALE2 - logs).astype(BF16)
+
+
+def backward(
+    weights_ref,
+    values_t,
+    keys,
+    got_ref,
     grads_ref,
-    out_hbm,
-    log_hbm,
+    out_ref,
     part_ref,
     finish,
     block,
     chunk,
-    keys_t,
-    values_t,
-    keys,
     grad_keys,
     grad_values,
-    out_ref,
-    log_ref,
-    sems,
 ):
-    copies = (
-        pltpu.make_async_copy(out_hbm, out_ref, sems.at[0]),
-        pltpu.make_async_copy(log_hbm, log_ref, sems.at[1]),
-    )
-    for copy in copies:
-        copy.start()
-    fill_half(half_ref, keys_t, values_t, keys, None)
-    for copy in copies:
-        copy.wait()
     key_count = keys.shape[0]
     per = block // SUB
     lane = lanes_of(block)
@@ -404,21 +421,20 @@
         rows = got_ref[sources, Q_ROWS, :].reshape(block, LANES)
         grads = grads_ref[sources].reshape(block, LANES).astype(F32)
         grads = jnp.where(lane < HEAD_DIM, grads, 0.0)
-        delta = jnp.sum(grads * out_ref[at, :].astype(F32), axis=1, keepdims=True)
-        logs = jnp.concatenate([log_ref[at, :]] * (chunk // LANES), axis=1)
+        out = out_ref[at, :].astype(F32)
+        delta = jnp.sum(grads * out, axis=1, keepdims=True)
         rows_t = rows.astype(F32).T.astype(BF16)[0:HEAD_DIM]
         grads_t = grads.T.astype(BF16)[0:HEAD_DIM]
         grads = grads.astype(BF16)
         result = jnp.zeros((block, LANES), F32)
         for start in range(0, key_count, chunk):
             part = slice(start, start + chunk)
-            logits = jnp.dot(rows, keys_t[:, part], preferred_element_type=F32)
-            probs = jnp.exp2(logits * SCALE2 - logs)
+            weights = weights_ref[at, part]
             grad_probs = jnp.dot(grads, values_t[:, part], preferred_element_type=F32)
-            grad_scores = (probs * (grad_probs - delta)).astype(BF16)
+            grad_scores = (weights.astype(F32) * (grad_probs - delta)).astype(BF16)
             result = result + jnp.dot(grad_scores, keys[part, :], preferred_element_type=F32)
             grad_k = jnp.dot(rows_t, grad_scores, preferred_element_type=F32)
-            grad_v = jnp.dot(grads_t, probs.astype(BF16), preferred_element_type=F32)
+            grad_v = jnp.dot(grads_t, weights, preferred_element_type=F32)
             if step == 0:
                 grad_keys[:, part] = grad_k
                 grad_values[:, part] = grad_v
@@ -438,23 +454,34 @@
 
 
 def backward_first_kernel(
-    block, chunk, swapped_ref, got_ref, grads_ref, out_hbm, log_hbm, part_ref, grad_q_ref, *scratch
+    block,
+    chunk,
+    weights_ref,
+    values_t,
+    keys,
+    got_ref,
+    grads_ref,
+    out_ref,
+    part_ref,
+    grad_q_ref,
+    *scratch,
 ):
     def finish(step, sources, at, result):
         grad_q_ref[at, :] = result
 
-    backward(
-        swapped_ref, got_ref, grads_ref, out_hbm, log_hbm, part_ref, finish, block, chunk, *scratch
-    )
+    ready = (weights_ref, values_t, keys)
+    backward(*ready, got_ref, grads_ref, out_ref, part_ref, finish, block, chunk, *scratch)
 
 
 def backward_second_kernel(
     block,
     chunk,
+    weights_ref,
+    values_t,
+    keys,
     got_ref,
     grads_ref,
-    out_hbm,
-    log_hbm,
+    out_ref,
     grad_q_ref,
     part_ref,
     piece_ref,
@@ -469,9 +496,8 @@
         lane = lax.broadcasted_iota(jnp.int32, result.shape, 2)
         piece_ref[sources] = jnp.where(lane < HEAD_DIM, result, sums[None]).astype(BF16)
 
-    backward(
-        got_ref, got_ref, grads_ref, out_hbm, log_hbm, part_ref, finish, block, chunk, *scratch
-    )
+    ready = (weights_ref, values_t, keys)
+    backward(*ready, got_ref, grads_ref, out_ref, part_ref, finish, block, chunk, *scratch)
 
 
 def join_kernel(part_ref, other_ref, piece_ref, send_ref):
@@ -591,17 +617,12 @@
         "attend_forward_own",
         own * half,
     )(got)
-    results, head_out, logs = call(
+    results, head_out = call(
         lambda *refs: forward_second_kernel(block, chunk, groups, *refs),
-        (shape((count, 48, LANES), BF16), shape((own, LANES), BF16), own_shape),
+        (shape((count, 48, LANES), BF16), shape((own, LANES), BF16)),
         [SMEM] + [VMEM] * 5,
-        (VMEM, HBM, HBM),
-        attend_scratch
-        + [
-            pltpu.VMEM((own, LANES), BF16),
-            pltpu.VMEM((own, LANES), F32),
-            pltpu.SemaphoreType.DMA((2,)),
-        ],
+        (VMEM,) * 2,
+        attend_scratch,
         24,
         2 * matmul,
         "attend_forward_other",
@@ -631,40 +652,50 @@
     )
 
     block, chunk = 512, 512
+    other_ready, own_ready = (
+        call(
+            lambda *refs: prepare_kernel(block, chunk, *refs),
+            (
+                shape((own, half), BF16),
+                shape((LANES, half), BF16),
+                shape((half, LANES), BF16),
+            ),
+            [VMEM] * 3 + [ANY],
+            (VMEM,) * 3,
+            [pltpu.VMEM((LANES, half), BF16)],
+            24,
+            matmul,
+            name,
+            own * half,
+        )(here, got, head_out, block_out)
+        for here, name in ((swapped, "prepare_other"), (got, "prepare_own"))
+    )
     backward_scratch = [
-        pltpu.VMEM((LANES, half), BF16),
-        pltpu.VMEM((LANES, half), BF16),
-        pltpu.VMEM((half, LANES), BF16),
         pltpu.VMEM((HEAD_DIM, half), F32),
         pltpu.VMEM((HEAD_DIM, half), F32),
-        pltpu.VMEM((own, LANES), BF16),
-        pltpu.VMEM((own, LANES), F32),
-        pltpu.SemaphoreType.DMA((2,)),
     ]
     part_shape = shape((count, HEAD_DIM, LANES), BF16)
     other_part, grad_q = call(
         lambda *refs: backward_first_kernel(block, chunk, *refs),
         (part_shape, own_shape),
-        [VMEM] * 3 + [HBM] * 2,
+        [VMEM] * 6,
         (VMEM,) * 2,
         backward_scratch,
         24,
-        5 * matmul,
+        4 * matmul,
         "attend_backward_other",
-        own * half,
-    )(swapped, got, grads_got, head_out, logs)
+    )(*other_ready, got, grads_got, head_out)
     arrived_part = lax.ppermute(other_part, "tm", partner)
     own_part, grad_q_pieces = call(
         lambda *refs: backward_second_kernel(block, chunk, *refs),
         (part_shape, shape((count, SUB, LANES), BF16)),
-        [VMEM] * 2 + [HBM] * 2 + [VMEM],
+        [VMEM] * 7,
         (VMEM,) * 2,
         backward_scratch,
         24,
-        5 * matmul,
+        4 * matmul,
         "attend_backward_own",
-        own * half,
-    )(got, grads_got, head_out, logs, grad_q)
+    )(*own_ready, got, grads_got, head_out, grad_q)
     grads_out = call(
         join_kernel,
         pieces,

time: 118 us -> 121 us (1.025)
  blocking collectives: 43.5 us -> 26.8 us
  local copies, waits for them, and re-layouts: 4.34 us -> 13.1 us
  starting transfers between devices: 20.3 us -> 28.4 us
  waiting for transfers between devices: 19.5 us -> 22.1 us
    all_to_all x2 -> x1, blocking collectives: 43.5 us -> 26.8 us  [exchange(): return lax.all_to_all(pieces, 'tm', split_axis=0, concat_axis=0, tiled=True)]
    all_to_all x2 -> x3, starting transfers between devices: 7.66 us -> 15.9 us  [exchange(): return lax.all_to_all(pieces, 'tm', split_axis=0, concat_axis=0, tiled=True)]
    unnamed x22 -> x30, local copies, waits for them, and re-layouts: 4.33 us -> 12.3 us
    pallas_call x0 -> x2, Pallas kernels: none -> 3.43 us  [local(): call(lambda *refs: prepare_kernel(block, chunk, *refs), (shape((own, half...]
    all_to_all x2 -> x3, waiting for transfers between devices: 3.08 us -> 5.6 us  [exchange(): return lax.all_to_all(pieces, 'tm', split_axis=0, concat_axis=0, tiled=True)]
    pallas_call x1, Pallas kernels: 6.42 us -> 4.42 us  [local(): call(lambda *refs: backward_second_kernel(block, chunk, *refs), (part_sha...]
    pallas_call x1, Pallas kernels: 6.38 us -> 4.42 us  [local(): call(lambda *refs: backward_first_kernel(block, chunk, *refs), (part_shap...]
  transfers between devices with their start and end apart: 7 -> 8, of which waited for: 4 -> 5; matrix products, arithmetic and copies ran while one was open for 0% -> 1% of each run, Pallas kernels for 8% -> 9%
where the time goes in v3:
time: 121 us; the launch traced here: 120 us
  Pallas kernels  28.4 us (23%)
  starting transfers between devices  28.4 us (23%)
  blocking collectives  26.8 us (22%)
  waiting for transfers between devices  22.1 us (18%)
  local copies, waits for them, and re-layouts  13.1 us (11%)
    all_to_all x1, blocking collectives, exchange(): return lax.all_to_all(pieces, 'tm', split_axis=0, concat_axis=0, tiled=True)  26.8 us
    all_to_all x3, starting transfers between devices, exchange(): return lax.all_to_all(pieces, 'tm', split_axis=0, concat_axis=0, tiled=True)  15.9 us
    ppermute x1, waiting for transfers between devices, local(): lax.ppermute(block_out, 'section', [(i, (i + 1) % sections) for i in rang...  12.7 us
    unnamed x30, local copies, waits for them, and re-layouts  12.3 us
    all_to_all x3, waiting for transfers between devices, exchange(): return lax.all_to_all(pieces, 'tm', split_axis=0, concat_axis=0, tiled=True)  5.6 us
    pallas_call x1, Pallas kernels, local(): call(lambda *refs: conv_kernel(groups, count, *refs), (shape((count, SUB,...  5.51 us
    pallas_call x1, Pallas kernels, local(): call(lambda *refs: forward_second_kernel(block, chunk, groups, *refs), (s...  4.58 us
    pallas_call x1, Pallas kernels, local(): call(lambda *refs: backward_second_kernel(block, chunk, *refs), (part_sha...  4.42 us
  transfers between devices with their start and end apart: 8, of which 5 were waited for; matrix products, arithmetic and copies ran while one was open for 1% of the time, Pallas kernels for 9%

profile of v3, /device:TPU:1, one launch (start us, length us, event | category | flops | bytes accessed | tf_op | source)
XLA Modules:
  0.0 119.8 jit_solution(2428256800586314782)
XLA Ops:
  3.8 26.8 %all_to_all.20.refs_0_.refs_1_.refs_3_ = bf16[32,128,128]{2,1,0:T(8,128)(2,1)S(1)} all-to-all(bf16[32,128,128]{2,1,0:T(8,128)(2,1)S(1)} %pack_qkv.1), channel_id=1, replica_groups=mesh['section'=16,'tm'=32] {'tm'}, dimensions={0} | all-to-all | bytes 2097152 | tf_op jit(solution)/shard_map/all_to_all | solution.py:560
  30.6 2.3 %collective-permute-start = (bf16[32,128,128]{2,1,0:T(8,128)(2,1)S(1)}, bf16[32,128,128]{2,1,0:T(8,128)(2,1)S(1)}, u32[]{:S(2)}, u32[]{:S(2)}) collective-permute-start(bf16[32,128,128]{2,1,0:T(8,128)(2,1)S(1)} %all_to_all.20.refs_0_.refs_1_.refs_3_), channel_id=1, source_target_pairs={{0,1},{1,0},{2,3},{3,2},{4,5},{5,4},{6,7},{7,6},{8,9},{9,8},{10,11... | collective-permute-start | bytes 3145736 | tf_op jit(solution)/shard_map/ppermute | solution.py:601
  33.8 3.2 %attend_forward_own.1 = (f32[1024,128]{1,0:T(8,128)S(1)}, f32[1024,128]{1,0:T(8,128)S(1)}, f32[1024,128]{1,0:T(8,128)S(1)}) custom-call(bf16[32,128,128]{2,1,0:T(8,128)(2,1)S(1)} %all_to_all.20.refs_0_.refs_1_.refs_3_), custom_call_target="tpu_custom_call" | custom-call | flops 1073741824 | bytes 2097152 | tf_op jit(solution)/shard_map/attend_forward_own/pallas_call | solution.py:609
  37.0 4.6 %attend_forward_other.1 = (bf16[32,48,128]{2,1,0:T(8,128)(2,1)}, bf16[1024,128]{1,0:T(8,128)(2,1)S(1)}) custom-call(s32[1]{0:T(128)} %bitcast.3.refs_0_, bf16[32,128,128]{2,1,0:T(8,128)(2,1)S(1)} %all_to_all.20.refs_0_.refs_1_.refs_3_, bf16[32,128,128]{2,1,0:T(8,128)(2,1)S(1)} %collective-permute-done.refs_2_.refs_0_, ...), custom_call_target="tpu_custom_call" | custom-call | flops 1073741824 | bytes 2097152 | tf_op jit(solution)/shard_map/attend_forward_other/pallas_call | solution.py:620
  42.3 3.7 %all-to-all-start.1 = ((bf16[32,48,128]{2,1,0:T(8,128)(2,1)}), bf16[32,48,128]{2,1,0:T(8,128)(2,1)S(1)}, u32[]{:S(2)}, u32[]{:S(2)}) async-start(bf16[32,48,128]{2,1,0:T(8,128)(2,1)} %get-tuple-element.35), calls=%async_computation.1 | async-start | bytes 786432 | tf_op jit(solution)/shard_map/all_to_all | solution.py:560
  46.0 3.5 %collective-permute-start.1 = (bf16[48,768]{1,0:T(8,128)(2,1)S(1)}, bf16[48,768]{1,0:T(8,128)(2,1)S(1)}, u32[]{:S(2)}, u32[]{:S(2)}) collective-permute-start(bf16[48,768]{1,0:T(8,128)(2,1)S(1)} %pad_maximum_fusion), channel_id=1, source_target_pairs={{0,1},{1,2},{2,3},{3,4},{4,5},{5,6},{6,7},{7,8},{8,9},{9,10},{10,1... | collective-permute-start | bytes 221192 | tf_op jit(solution)/shard_map/ppermute | solution.py:581
  49.6 2.1 %collective-permute-start.2 = (bf16[48,768]{1,0:T(8,128)(2,1)S(1)}, bf16[48,768]{1,0:T(8,128)(2,1)S(1)}, u32[]{:S(2)}, u32[]{:S(2)}) collective-permute-start(bf16[48,768]{1,0:T(8,128)(2,1)S(1)} %pad_maximum_fusion.1), channel_id=1, source_target_pairs={{1,0},{2,1},{3,2},{4,3},{5,4},{6,5},{7,6},{8,7},{9,8},{10,9},{11,1... | collective-permute-start | bytes 221192 | tf_op jit(solution)/shard_map/ppermute | solution.py:584
  51.7 3.8 %collective-permute-done.2.refs_5_ = bf16[48,768]{1,0:T(8,128)(2,1)S(1)} collective-permute-done((bf16[48,768]{1,0:T(8,128)(2,1)S(1)}, bf16[48,768]{1,0:T(8,128)(2,1)S(1)}, u32[]{:S(2)}, u32[]{:S(2)}) %collective-permute-start.2) | collective-permute-done | bytes 73760 | tf_op jit(solution)/shard_map/ppermute | solution.py:584
  56.3 5.5 %conv_block.1 = (bf16[32,32,128]{2,1,0:T(8,128)(2,1)}, bf16[128,768]{1,0:T(8,128)(2,1)S(1)}, bf16[128,768]{1,0:T(8,128)(2,1)}) custom-call(s32[1]{0:T(128)} %bitcast.3.refs_0_, bf16[32,48,128]{2,1,0:T(8,128)(2,1)S(1)} %all-to-all-done.1.refs_1_, bf16[128,768]{1,0:T(8,128)(2,1)S(1)} %bitcast.21, bf16[128,768]{1,0:T(8,128)(2,1)S(1)} %bitcast.22, ...), custom_call_target="tpu_custom_call" | custom-call | flops 10000000 | bytes 2097152 | tf_op jit(solution)/shard_map/conv_block/pallas_call | solution.py:633
  61.8 7.5 %all-to-all-start.2 = ((bf16[32,32,128]{2,1,0:T(8,128)(2,1)}), bf16[32,32,128]{2,1,0:T(8,128)(2,1)S(1)}, u32[]{:S(2)}, u32[]{:S(2)}) async-start(bf16[32,32,128]{2,1,0:T(8,128)(2,1)} %get-tuple-element.40), calls=%async_computation.2 | async-start | bytes 524288 | tf_op jit(solution)/shard_map/all_to_all | solution.py:560
  70.3 1.7 %prepare_other.1 = (bf16[1024,2048]{1,0:T(8,128)(2,1)S(1)}, bf16[128,2048]{1,0:T(8,128)(2,1)S(1)}, bf16[2048,128]{1,0:T(8,128)(2,1)S(1)}) custom-call(bf16[32,128,128]{2,1,0:T(8,128)(2,1)S(1)} %collective-permute-done.refs_2_.refs_0_, bf16[32,128,128]{2,1,0:T(8,128)(2,1)S(1)} %all_to_all.20.refs_0_.refs_1_.refs_3_, bf16[1024,128]{1,0:T(8,128)(2,1)S(1)} %copy-done.10, ...), custom_call_target="tpu_custom_call" | custom-call | flops 536870912 | bytes 2097152 | tf_op jit(solution)/shard_map/prepare_other/pallas_call | solution.py:656
  72.0 2.0 %copy-done.7 = bf16[1024,2048]{1,0:T(8,128)(2,1)} copy-done((bf16[1024,2048]{1,0:T(8,128)(2,1)}, bf16[1024,2048]{1,0:T(8,128)(2,1)S(1)}, u32[]{:S(2)}) %copy-start.7) | copy-done | bytes 4194328
  75.6 2.6 %all-to-all-done.2.refs_4_ = bf16[32,32,128]{2,1,0:T(8,128)(2,1)S(1)} async-done(((bf16[32,32,128]{2,1,0:T(8,128)(2,1)}), bf16[32,32,128]{2,1,0:T(8,128)(2,1)S(1)}, u32[]{:S(2)}, u32[]{:S(2)}) %all-to-all-start.2) | async-done | bytes 262176 | tf_op jit(solution)/shard_map/all_to_all | solution.py:560
  78.2 2.2 %copy-done.8 = bf16[1024,2048]{1,0:T(8,128)(2,1)S(1)} copy-done((bf16[1024,2048]{1,0:T(8,128)(2,1)S(1)}, bf16[1024,2048]{1,0:T(8,128)(2,1)}, u32[]{:S(2)}) %copy-start.8) | copy-done | bytes 4194328
  82.5 4.4 %attend_backward_other.1 = (bf16[32,96,128]{2,1,0:T(8,128)(2,1)S(1)}, f32[1024,128]{1,0:T(8,128)S(1)}) custom-call(bf16[1024,2048]{1,0:T(8,128)(2,1)S(1)} %copy-done.8, bf16[128,2048]{1,0:T(8,128)(2,1)S(1)} %copy-done.12, bf16[2048,128]{1,0:T(8,128)(2,1)S(1)} %copy-done.14, bf16[32,128,128]{2,1,0:T(8,128)(2,1)S(1)} %all_to_all.20.refs_0_.refs_1_.refs_3_, ...), custom_call_target="tpu_custom_call" | custom-call | flops 2147483648 | bytes 2097152 | tf_op jit(solution)/shard_map/attend_backward_other/pallas_call | solution.py:678
  86.9 2.4 %collective-permute-start.3 = (bf16[32,96,128]{2,1,0:T(8,128)(2,1)S(1)}, bf16[32,96,128]{2,1,0:T(8,128)(2,1)S(1)}, u32[]{:S(2)}, u32[]{:S(2)}) collective-permute-start(bf16[32,96,128]{2,1,0:T(8,128)(2,1)S(1)} %get-tuple-element.46), channel_id=1, source_target_pairs={{0,1},{1,0},{2,3},{3,2},{4,5},{5,4},{6,7},{7,6},{8,9},{9,8},{10,11... | collective-permute-start | bytes 2359304 | tf_op jit(solution)/shard_map/ppermute | solution.py:688
  89.3 1.7 %prepare_own.1 = (bf16[1024,2048]{1,0:T(8,128)(2,1)S(1)}, bf16[128,2048]{1,0:T(8,128)(2,1)S(1)}, bf16[2048,128]{1,0:T(8,128)(2,1)S(1)}) custom-call(bf16[32,128,128]{2,1,0:T(8,128)(2,1)S(1)} %all_to_all.20.refs_0_.refs_1_.refs_3_, bf16[32,128,128]{2,1,0:T(8,128)(2,1)S(1)} %all_to_all.20.refs_0_.refs_1_.refs_3_, bf16[1024,128]{1,0:T(8,128)(2,1)S(1)} %copy-done.10, ...), custom_call_target="tpu_custom_call" | custom-call | flops 536870912 | bytes 2097152 | tf_op jit(solution)/shard_map/prepare_own/pallas_call | solution.py:656
  91.0 4.4 %attend_backward_own.1 = (bf16[32,96,128]{2,1,0:T(8,128)(2,1)S(1)}, bf16[32,32,128]{2,1,0:T(8,128)(2,1)S(1)}) custom-call(bf16[1024,2048]{1,0:T(8,128)(2,1)S(1)} %get-tuple-element.37.refs_0_, bf16[128,2048]{1,0:T(8,128)(2,1)S(1)} %get-tuple-element.38.refs_1_, bf16[2048,128]{1,0:T(8,128)(2,1)S(1)} %get-tuple-element.39.refs_2_, ...), custom_call_target="tpu_custom_call" | custom-call | flops 2147483648 | bytes 2097152 | tf_op jit(solution)/shard_map/attend_backward_own/pallas_call | solution.py:689
  95.5 1.2 join_grads.1
  96.7 4.7 %all-to-all-start.3 = ((bf16[32,128,128]{2,1,0:T(8,128)(2,1)}), bf16[32,128,128]{2,1,0:T(8,128)(2,1)S(1)}, u32[]{:S(2)}, u32[]{:S(2)}) async-start(bf16[32,128,128]{2,1,0:T(8,128)(2,1)} %join_grads.1), calls=%async_computation.3 | async-start | bytes 2097152 | tf_op jit(solution)/shard_map/all_to_all | solution.py:560
  101.3 2.3 %collective-permute-start.4 = (bf16[128,768]{1,0:T(8,128)(2,1)S(1)}, bf16[128,768]{1,0:T(8,128)(2,1)S(1)}, u32[]{:S(2)}, u32[]{:S(2)}) collective-permute-start(bf16[128,768]{1,0:T(8,128)(2,1)S(1)} %get-tuple-element.36.refs_3_), channel_id=1, source_target_pairs={{0,32},{32,64},{64,96},{96,128},{128,160},{160,192},{192,224},{224... | collective-permute-start | bytes 589832 | tf_op jit(solution)/shard_map/ppermute | solution.py:650
  103.6 12.7 %collective-permute-done.4.refs_1_ = bf16[128,768]{1,0:T(8,128)(2,1)S(1)} collective-permute-done((bf16[128,768]{1,0:T(8,128)(2,1)S(1)}, bf16[128,768]{1,0:T(8,128)(2,1)S(1)}, u32[]{:S(2)}, u32[]{:S(2)}) %collective-permute-start.4) | collective-permute-done | bytes 196640 | tf_op jit(solution)/shard_map/ppermute | solution.py:650
  116.3 2.2 %all-to-all-done.3.refs_0_ = bf16[32,128,128]{2,1,0:T(8,128)(2,1)S(1)} async-done(((bf16[32,128,128]{2,1,0:T(8,128)(2,1)}), bf16[32,128,128]{2,1,0:T(8,128)(2,1)S(1)}, u32[]{:S(2)}, u32[]{:S(2)}) %all-to-all-start.3) | async-done | bytes 1048608 | tf_op jit(solution)/shard_map/all_to_all | solution.py:560
  118.5 1.3 %unpack_grads.1 = (bf16[128,768]{1,0:T(8,128)(2,1)}, bf16[128,768]{1,0:T(8,128)(2,1)}, bf16[128,768]{1,0:T(8,128)(2,1)}, f32[1,768]{1,0:T(1,128)}, f32[31,1,768]{2,1,0:T(1,128)}, /*index=5*/bf16[128,768]{1,0:T(8,128)(2,1)}) custom-call(bf16[32,128,128]{2,1,0:T(8,128)(2,1)S(1)} %all-to-all-done.3.refs_0_, bf16[128,768]{1,0:T(8,128)(2,1)S(1)} %collective-permute-done.4.refs_1_), custom_call_target="tpu_custom_call" | custom-call | flops 1000000 | bytes 2097152 | tf_op jit(solution)/shard_map/unpack_grads/pallas_call | solution.py:711
  (37 shorter events, 10.2 us)
Async XLA Ops:
  0.6 0.9 copy-start.2
  1.6 0.9 copy-start.3
  2.5 0.9 copy-start.4
  30.6 6.4 %collective-permute-start = (bf16[32,128,128]{2,1,0:T(8,128)(2,1)S(1)}, bf16[32,128,128]{2,1,0:T(8,128)(2,1)S(1)}, u32[]{:S(2)}, u32[]{:S(2)}) collective-permute-start(bf16[32,128,128]{2,1,0:T(8,128)(2,1)S(1)} %all_to_all.20.refs_0_.refs_1_.refs_3_), channel_id=1, source_target_pairs={{0,1},{1,0},{2,3},{3,2},{4,5},{5,4},{6,7},{7,6},{8,9},{9,8},{10,11... | collective-permute-start | bytes 3145736 | tf_op jit(solution)/shard_map/ppermute | solution.py:601
  33.8 12.2 %copy-start.1 = (bf16[1,128,768]{2,1,0:T(8,128)(2,1)S(1)}, bf16[1,128,768]{2,1,0:T(8,128)(2,1)}, u32[]{:S(2)}) copy-start(bf16[1,128,768]{2,1,0:T(8,128)(2,1)} %param.13) | copy-start | bytes 589828
  33.8 22.5 %copy-start = (bf16[1,128,768]{2,1,0:T(8,128)(2,1)S(1)}, bf16[1,128,768]{2,1,0:T(8,128)(2,1)}, u32[]{:S(2)}) copy-start(bf16[1,128,768]{2,1,0:T(8,128)(2,1)} %param.7) | copy-start | bytes 589828
  33.8 22.5 %copy-start.5 = (f32[1,31,768]{2,0,1:T(1,128)S(1)}, f32[1,31,768]{2,0,1:T(1,128)}, u32[]{:S(2)}) copy-start(f32[1,31,768]{2,0,1:T(1,128)} %param.12) | copy-start | bytes 285700
  33.8 22.5 %copy-start.6 = (f32[1,768]{1,0:T(1,128)S(1)}, f32[1,768]{1,0:T(1,128)}, u32[]{:S(2)}) copy-start(f32[1,768]{1,0:T(1,128)} %refs_6_.1) | copy-start | bytes 9220
  41.6 0.7 copy-start.9
  42.3 14.0 %all-to-all-start.1 = ((bf16[32,48,128]{2,1,0:T(8,128)(2,1)}), bf16[32,48,128]{2,1,0:T(8,128)(2,1)S(1)}, u32[]{:S(2)}, u32[]{:S(2)}) async-start(bf16[32,48,128]{2,1,0:T(8,128)(2,1)} %get-tuple-element.35), calls=%async_computation.1 | async-start | bytes 786432 | tf_op jit(solution)/shard_map/all_to_all | solution.py:560
  46.0 5.7 %collective-permute-start.1 = (bf16[48,768]{1,0:T(8,128)(2,1)S(1)}, bf16[48,768]{1,0:T(8,128)(2,1)S(1)}, u32[]{:S(2)}, u32[]{:S(2)}) collective-permute-start(bf16[48,768]{1,0:T(8,128)(2,1)S(1)} %pad_maximum_fusion), channel_id=1, source_target_pairs={{0,1},{1,2},{2,3},{3,4},{4,5},{5,6},{6,7},{7,8},{8,9},{9,10},{10,1... | collective-permute-start | bytes 221192 | tf_op jit(solution)/shard_map/ppermute | solution.py:581
  49.6 6.0 %collective-permute-start.2 = (bf16[48,768]{1,0:T(8,128)(2,1)S(1)}, bf16[48,768]{1,0:T(8,128)(2,1)S(1)}, u32[]{:S(2)}, u32[]{:S(2)}) collective-permute-start(bf16[48,768]{1,0:T(8,128)(2,1)S(1)} %pad_maximum_fusion.1), channel_id=1, source_target_pairs={{1,0},{2,1},{3,2},{4,3},{5,4},{6,5},{7,6},{8,7},{9,8},{10,9},{11,1... | collective-permute-start | bytes 221192 | tf_op jit(solution)/shard_map/ppermute | solution.py:584
  61.8 16.4 %all-to-all-start.2 = ((bf16[32,32,128]{2,1,0:T(8,128)(2,1)}), bf16[32,32,128]{2,1,0:T(8,128)(2,1)S(1)}, u32[]{:S(2)}, u32[]{:S(2)}) async-start(bf16[32,32,128]{2,1,0:T(8,128)(2,1)} %get-tuple-element.40), calls=%async_computation.2 | async-start | bytes 524288 | tf_op jit(solution)/shard_map/all_to_all | solution.py:560
  69.3 1.0 copy-start.10
  72.0 2.0 %copy-start.7 = (bf16[1024,2048]{1,0:T(8,128)(2,1)}, bf16[1024,2048]{1,0:T(8,128)(2,1)S(1)}, u32[]{:S(2)}) copy-start(bf16[1024,2048]{1,0:T(8,128)(2,1)S(1)} %get-tuple-element.41.refs_0_) | copy-start | bytes 12582916
  74.0 0.8 copy-start.11
  74.8 0.8 copy-start.13
  78.2 2.2 %copy-start.8 = (bf16[1024,2048]{1,0:T(8,128)(2,1)S(1)}, bf16[1024,2048]{1,0:T(8,128)(2,1)}, u32[]{:S(2)}) copy-start(bf16[1024,2048]{1,0:T(8,128)(2,1)} %copy-done.7) | copy-start | bytes 12582916
  80.4 1.0 copy-start.12
  81.5 1.0 copy-start.14
  86.9 8.5 %collective-permute-start.3 = (bf16[32,96,128]{2,1,0:T(8,128)(2,1)S(1)}, bf16[32,96,128]{2,1,0:T(8,128)(2,1)S(1)}, u32[]{:S(2)}, u32[]{:S(2)}) collective-permute-start(bf16[32,96,128]{2,1,0:T(8,128)(2,1)S(1)} %get-tuple-element.46), channel_id=1, source_target_pairs={{0,1},{1,0},{2,3},{3,2},{4,5},{5,4},{6,7},{7,6},{8,9},{9,8},{10,11... | collective-permute-start | bytes 2359304 | tf_op jit(solution)/shard_map/ppermute | solution.py:688
  96.7 21.9 %all-to-all-start.3 = ((bf16[32,128,128]{2,1,0:T(8,128)(2,1)}), bf16[32,128,128]{2,1,0:T(8,128)(2,1)S(1)}, u32[]{:S(2)}, u32[]{:S(2)}) async-start(bf16[32,128,128]{2,1,0:T(8,128)(2,1)} %join_grads.1), calls=%async_computation.3 | async-start | bytes 2097152 | tf_op jit(solution)/shard_map/all_to_all | solution.py:560
  101.3 15.0 %collective-permute-start.4 = (bf16[128,768]{1,0:T(8,128)(2,1)S(1)}, bf16[128,768]{1,0:T(8,128)(2,1)S(1)}, u32[]{:S(2)}, u32[]{:S(2)}) collective-permute-start(bf16[128,768]{1,0:T(8,128)(2,1)S(1)} %get-tuple-element.36.refs_3_), channel_id=1, source_target_pairs={{0,32},{32,64},{64,96},{96,128},{128,160},{160,192},{192,224},{224... | collective-permute-start | bytes 589832 | tf_op jit(solution)/shard_map/ppermute | solution.py:650

commit v4 on v3

--- a/solution.py
+++ b/solution.py
@@ -63,13 +63,14 @@
     )
 
 
-def call(kernel, out_shape, in_specs, out_specs, scratch, limit, flops, name, transcendentals=0):
+def call(kernel, out_shape, in_specs, out_specs, scratch, limit, flops, name, transcendentals=0, aliases={}):
     return pl.pallas_call(
         kernel,
         out_shape=out_shape,
         in_specs=in_specs,
         out_specs=out_specs,
         scratch_shapes=scratch,
+        input_output_aliases=aliases,
         compiler_params=pltpu.CompilerParams(vmem_limit_bytes=limit * MIB),
         cost_estimate=pl.CostEstimate(
             flops=flops, bytes_accessed=2 * MIB, transcendentals=transcendentals
@@ -78,22 +79,17 @@
     )
 
 
-def pack_kernel(groups, q_ref, k_ref, v_ref, send_ref, keys_t, values_t):
+def pack_kernel(
+    groups, q_hbm, k_hbm, v_hbm, send_hbm, q_ref, k_ref, v_ref, send_ref, keys_t, values_t, sems, sent
+):
+    copies = [
+        pltpu.make_async_copy(source, target, sems.at[i])
+        for i, (source, target) in enumerate(((q_hbm, q_ref), (k_hbm, k_ref), (v_hbm, v_ref)))
+    ]
+    for copy in copies:
+        copy.start()
+    copies[0].wait()
     frames = q_ref.shape[0]
-    for source, turned in ((k_ref, keys_t), (v_ref, values_t)):
-        for tile in range(CH // LANES):
-            at = slice(tile * LANES, (tile + 1) * LANES)
-            turned[at, :] = source[:, at].astype(F32).T
-    lane = lanes_of(HEAD_DIM)
-    for head in range(HEADS):
-        at = slice(head * HEAD_DIM, (head + 1) * HEAD_DIM)
-        keys_here, values_here = keys_t[at, :], values_t[at, :]
-        halves = (
-            jnp.where(lane < HALF, keys_here, roll_lanes(values_here, HALF)).astype(BF16),
-            jnp.where(lane < HALF, roll_lanes(keys_here, HALF), values_here).astype(BF16),
-        )
-        for group in range(groups):
-            send_ref[head * groups + group, KV_ROWS, :] = halves[group % 2]
     lane = lanes_of(frames)
     for half in range(2):
         tiles = [
@@ -106,6 +102,29 @@
                 send_ref[(4 * half + i) * groups + group, Q_ROWS, :] = block[
                     group * SUB : (group + 1) * SUB
                 ]
+    for copy, source, turned in ((copies[1], k_ref, keys_t), (copies[2], v_ref, values_t)):
+        copy.wait()
+        for tile in range(CH // LANES):
+            at = slice(tile * LANES, (tile + 1) * LANES)
+            turned[at, :] = source[:, at].astype(F32).T
+    lane = lanes_of(HEAD_DIM)
+    out = []
+    for head in range(HEADS):
+        at = slice(head * HEAD_DIM, (head + 1) * HEAD_DIM)
+        keys_here, values_here = keys_t[at, :], values_t[at, :]
+        halves = (
+            jnp.where(lane < HALF, keys_here, roll_lanes(values_here, HALF)).astype(BF16),
+            jnp.where(lane < HALF, roll_lanes(keys_here, HALF), values_here).astype(BF16),
+        )
+        for group in range(groups):
+            send_ref[head * groups + group, KV_ROWS, :] = halves[group % 2]
+        devices = pl.ds(head * groups, groups)
+        out.append(
+            pltpu.make_async_copy(send_ref.at[devices], send_hbm.at[devices], sent.at[head])
+        )
+        out[-1].start()
+    for copy in out:
+        copy.wait()
 
 
 def fill_half(half_ref, keys_t, values_t, keys, values):
@@ -371,37 +390,8 @@
                 send_ref[device] = piece.astype(BF16)
 
 
-def prepare_kernel(
-    block,
-    chunk,
+def backward(
     half_ref,
-    got_ref,
-    out_ref,
-    unused_ref,
-    weights_ref,
-    values_t,
-    keys,
-    keys_t,
-):
-    fill_half(half_ref, keys_t, values_t, keys, None)
-    per = block // SUB
-    lane = lanes_of(block)
-    in_log = (lane >= HEAD_DIM) & (lane < HEAD_DIM + 3)
-    for step in range(got_ref.shape[0] // per):
-        at = slice(step * block, (step + 1) * block)
-        rows = got_ref[step * per : (step + 1) * per, Q_ROWS, :].reshape(block, LANES)
-        logs = jnp.where(in_log, out_ref[at, :].astype(F32), 0.0)
-        logs = jnp.sum(logs, axis=1, keepdims=True)
-        for start in range(0, keys.shape[0], chunk):
-            part = slice(start, start + chunk)
-            logits = jnp.dot(rows, keys_t[:, part], preferred_element_type=F32)
-            weights_ref[at, part] = jnp.exp2(logits * SCALE2 - logs).astype(BF16)
-
-
-def backward(
-    weights_ref,
-    values_t,
-    keys,
     got_ref,
     grads_ref,
     out_ref,
@@ -409,9 +399,13 @@
     finish,
     block,
     chunk,
+    keys_t,
+    values_t,
+    keys,
     grad_keys,
     grad_values,
 ):
+    fill_half(half_ref, keys_t, values_t, keys, None)
     key_count = keys.shape[0]
     per = block // SUB
     lane = lanes_of(block)
@@ -423,18 +417,21 @@
         grads = jnp.where(lane < HEAD_DIM, grads, 0.0)
         out = out_ref[at, :].astype(F32)
         delta = jnp.sum(grads * out, axis=1, keepdims=True)
+        in_log = (lane >= HEAD_DIM) & (lane < HEAD_DIM + 3)
+        logs = jnp.sum(jnp.where(in_log, out, 0.0), axis=1, keepdims=True)
         rows_t = rows.astype(F32).T.astype(BF16)[0:HEAD_DIM]
         grads_t = grads.T.astype(BF16)[0:HEAD_DIM]
         grads = grads.astype(BF16)
         result = jnp.zeros((block, LANES), F32)
         for start in range(0, key_count, chunk):
             part = slice(start, start + chunk)
-            weights = weights_ref[at, part]
+            logits = jnp.dot(rows, keys_t[:, part], preferred_element_type=F32)
+            probs = jnp.exp2(logits * SCALE2 - logs)
             grad_probs = jnp.dot(grads, values_t[:, part], preferred_element_type=F32)
-            grad_scores = (weights.astype(F32) * (grad_probs - delta)).astype(BF16)
+            grad_scores = (probs * (grad_probs - delta)).astype(BF16)
             result = result + jnp.dot(grad_scores, keys[part, :], preferred_element_type=F32)
             grad_k = jnp.dot(rows_t, grad_scores, preferred_element_type=F32)
-            grad_v = jnp.dot(grads_t, weights, preferred_element_type=F32)
+            grad_v = jnp.dot(grads_t, probs.astype(BF16), preferred_element_type=F32)
             if step == 0:
                 grad_keys[:, part] = grad_k
                 grad_values[:, part] = grad_v
@@ -456,9 +453,7 @@
 def backward_first_kernel(
     block,
     chunk,
-    weights_ref,
-    values_t,
-    keys,
+    swapped_ref,
     got_ref,
     grads_ref,
     out_ref,
@@ -469,24 +464,27 @@
     def finish(step, sources, at, result):
         grad_q_ref[at, :] = result
 
-    ready = (weights_ref, values_t, keys)
-    backward(*ready, got_ref, grads_ref, out_ref, part_ref, finish, block, chunk, *scratch)
+    backward(
+        swapped_ref, got_ref, grads_ref, out_ref, part_ref, finish, block, chunk, *scratch
+    )
 
 
 def backward_second_kernel(
     block,
     chunk,
-    weights_ref,
-    values_t,
-    keys,
     got_ref,
     grads_ref,
     out_ref,
     grad_q_ref,
+    arrived_ref,
     part_ref,
     piece_ref,
+    next_hbm,
     *scratch,
 ):
+    *scratch, next_sem = scratch
+    passed = pltpu.make_async_copy(arrived_ref, next_hbm, next_sem)
+    passed.start()
     sums = jnp.zeros((SUB, LANES), F32)
     for source in range(grads_ref.shape[0]):
         sums = sums + grads_ref[source].astype(F32)
@@ -496,8 +494,10 @@
         lane = lax.broadcasted_iota(jnp.int32, result.shape, 2)
         piece_ref[sources] = jnp.where(lane < HEAD_DIM, result, sums[None]).astype(BF16)
 
-    ready = (weights_ref, values_t, keys)
-    backward(*ready, got_ref, grads_ref, out_ref, part_ref, finish, block, chunk, *scratch)
+    backward(
+        got_ref, got_ref, grads_ref, out_ref, part_ref, finish, block, chunk, *scratch
+    )
+    passed.wait()
 
 
 def join_kernel(part_ref, other_ref, piece_ref, send_ref):
@@ -509,9 +509,8 @@
 
 
 def unpack_kernel(
-    groups, got_ref, arrived_ref, q_ref, k_ref, v_ref, gain_ref, taps_ref, next_ref, keys_t, values_t
+    groups, got_ref, q_ref, k_ref, v_ref, gain_ref, taps_ref, keys_t, values_t
 ):
-    next_ref[...] = arrived_ref[...]
     count = got_ref.shape[0]
     lane = lanes_of(HEAD_DIM)
     for head in range(HEADS):
@@ -590,14 +589,27 @@
     sent = call(
         lambda *refs: pack_kernel(groups, *refs),
         pieces,
-        [VMEM] * 3,
-        VMEM,
-        [pltpu.VMEM((CH, LANES), F32)] * 2,
-        8,
+        [ANY] * 3,
+        ANY,
+        [pltpu.VMEM((frames, CH), BF16)] * 3
+        + [pltpu.VMEM((count, PIECE_ROWS, LANES), BF16)]
+        + [pltpu.VMEM((CH, LANES), F32)] * 2
+        + [pltpu.SemaphoreType.DMA((3,)), pltpu.SemaphoreType.DMA((HEADS,))],
+        56,
         1000000,
         "pack_qkv",
     )(queries, keys, values)
-    got = exchange(sent)
+    got = call(
+        lambda *refs: None,
+        pieces,
+        [ANY] * 3,
+        ANY,
+        [],
+        8,
+        0,
+        "received",
+        aliases={0: 0},
+    )(exchange(sent), before, after)
     swapped = lax.ppermute(got, "tm", partner)
 
     block, chunk = 256, 512
@@ -652,25 +664,10 @@
     )
 
     block, chunk = 512, 512
-    other_ready, own_ready = (
-        call(
-            lambda *refs: prepare_kernel(block, chunk, *refs),
-            (
-                shape((own, half), BF16),
-                shape((LANES, half), BF16),
-                shape((half, LANES), BF16),
-            ),
-            [VMEM] * 3 + [ANY],
-            (VMEM,) * 3,
-            [pltpu.VMEM((LANES, half), BF16)],
-            24,
-            matmul,
-            name,
-            own * half,
-        )(here, got, head_out, block_out)
-        for here, name in ((swapped, "prepare_other"), (got, "prepare_own"))
-    )
     backward_scratch = [
+        pltpu.VMEM((LANES, half), BF16),
+        pltpu.VMEM((LANES, half), BF16),
+        pltpu.VMEM((half, LANES), BF16),
         pltpu.VMEM((HEAD_DIM, half), F32),
         pltpu.VMEM((HEAD_DIM, half), F32),
     ]
@@ -678,24 +675,25 @@
     other_part, grad_q = call(
         lambda *refs: backward_first_kernel(block, chunk, *refs),
         (part_shape, own_shape),
-        [VMEM] * 6,
+        [VMEM] * 4,
         (VMEM,) * 2,
         backward_scratch,
         24,
-        4 * matmul,
+        1000000,
         "attend_backward_other",
-    )(*other_ready, got, grads_got, head_out)
+    )(swapped, got, grads_got, head_out)
     arrived_part = lax.ppermute(other_part, "tm", partner)
-    own_part, grad_q_pieces = call(
+    own_part, grad_q_pieces, next_input = call(
         lambda *refs: backward_second_kernel(block, chunk, *refs),
-        (part_shape, shape((count, SUB, LANES), BF16)),
-        [VMEM] * 7,
-        (VMEM,) * 2,
-        backward_scratch,
+        (part_shape, shape((count, SUB, LANES), BF16), rows_shape),
+        [VMEM] * 4 + [ANY],
+        (VMEM,) * 2 + (ANY,),
+        backward_scratch + [pltpu.SemaphoreType.DMA],
         24,
-        4 * matmul,
+        5 * matmul,
         "attend_backward_own",
-    )(*own_ready, got, grads_got, head_out, grad_q)
+        own * half,
+    )(got, grads_got, head_out, grad_q, arrived)
     grads_out = call(
         join_kernel,
         pieces,
@@ -708,7 +706,7 @@
     )(own_part, arrived_part, grad_q_pieces)
     back = exchange(grads_out)
 
-    grad_q, grad_k, grad_v, grad_gain, grad_taps, next_input = call(
+    grad_q, grad_k, grad_v, grad_gain, grad_taps = call(
         lambda *refs: unpack_kernel(groups, *refs),
         (
             rows_shape,
@@ -716,15 +714,14 @@
             rows_shape,
             shape((1, CH), F32),
             shape((TAPS, 1, CH), F32),
-            rows_shape,
         ),
-        [VMEM] * 2,
-        (VMEM,) * 6,
+        [VMEM],
+        (VMEM,) * 5,
         [pltpu.VMEM((CH, LANES), F32)] * 2,
         8,
         1000000,
         "unpack_grads",
-    )(back, arrived)
+    )(back)
     return (
         next_input[None],
         grad_resid[None],

time: 121 us -> 124 us (1.025)
  blocking collectives: 26.8 us -> 47.8 us
  local copies, waits for them, and re-layouts: 13.1 us -> 0.72 us
  starting transfers between devices: 28.4 us -> 22.6 us
  waiting for transfers between devices: 22.1 us -> 23.9 us
    all_to_all x1 -> x3, blocking collectives: 26.8 us -> 47.8 us  [exchange(): return lax.all_to_all(pieces, 'tm', split_axis=0, concat_axis=0, tiled=True)]
    unnamed x30 -> x8, local copies, waits for them, and re-layouts: 12.3 us -> 0.7 us
    ppermute x1, waiting for transfers between devices: 0.01 us -> 7.07 us  [local(): lax.ppermute(jnp.concatenate([resid[frames - SUB:], cotangent[frames - ed...]
    all_to_all x3 -> x1, starting transfers between devices: 15.9 us -> 10.6 us  [exchange(): return lax.all_to_all(pieces, 'tm', split_axis=0, concat_axis=0, tiled=True)]
    all_to_all x3 -> x1, waiting for transfers between devices: 5.6 us -> 2.53 us  [exchange(): return lax.all_to_all(pieces, 'tm', split_axis=0, concat_axis=0, tiled=True)]
    ppermute x1, waiting for transfers between devices: 3.85 us -> 2.12 us  [local(): lax.ppermute(jnp.concatenate([resid[:SUB], cotangent[:edge]], axis=0), 't...]
    pallas_call x1, Pallas kernels: 4.42 us -> 5.96 us  [local(): call(lambda *refs: backward_second_kernel(block, chunk, *refs), (part_sha...]
    pallas_call x1, Pallas kernels: 4.42 us -> 5.94 us  [local(): call(lambda *refs: backward_first_kernel(block, chunk, *refs), (part_shap...]
  transfers between devices with their start and end apart: 8 -> 6, of which waited for: 5 -> 4; matrix products, arithmetic and copies ran while one was open for 1% -> 0% of each run, Pallas kernels for 9% -> 7%
where the time goes in v4:
time: 124 us
  blocking collectives  47.8 us (39%)
  Pallas kernels  28.1 us (23%)
  waiting for transfers between devices  23.9 us (19%)
  starting transfers between devices  22.6 us (18%)
    all_to_all x3, blocking collectives, exchange(): return lax.all_to_all(pieces, 'tm', split_axis=0, concat_axis=0, tiled=True)  47.8 us
    ppermute x1, waiting for transfers between devices, local(): lax.ppermute(block_out, 'section', [(i, (i + 1) % sections) for i in rang...  12.2 us
    all_to_all x1, starting transfers between devices, exchange(): return lax.all_to_all(pieces, 'tm', split_axis=0, concat_axis=0, tiled=True)  10.6 us
    ppermute x1, waiting for transfers between devices, local(): lax.ppermute(jnp.concatenate([resid[frames - SUB:], cotangent[frames - ed...  7.07 us
    pallas_call x1, Pallas kernels, local(): call(lambda *refs: backward_second_kernel(block, chunk, *refs), (part_sha...  5.96 us
    pallas_call x1, Pallas kernels, local(): call(lambda *refs: backward_first_kernel(block, chunk, *refs), (part_shap...  5.94 us
    pallas_call x1, Pallas kernels, local(): call(lambda *refs: conv_kernel(groups, count, *refs), (shape((count, SUB,...  5.4 us
    pallas_call x1, Pallas kernels, local(): call(lambda *refs: forward_second_kernel(block, chunk, groups, *refs), (s...  3.81 us
  transfers between devices with their start and end apart: 6, of which 4 were waited for; matrix products, arithmetic and copies ran while one was open for 0% of the time, Pallas kernels for 7%

profile of v4, /device:TPU:1, one launch (start us, length us, event | category | flops | bytes accessed | tf_op | source)
XLA Modules:
  0.0 124.0 jit_solution(1436160593719570652)
XLA Ops:
  0.6 2.4 %pack_qkv.1 = bf16[32,128,128]{2,1,0:T(8,128)(2,1)} custom-call(bf16[128,768]{1,0:T(8,128)(2,1)} %bitcast.24, bf16[128,768]{1,0:T(8,128)(2,1)} %bitcast.25, bf16[128,768]{1,0:T(8,128)(2,1)} %bitcast.26), custom_call_target="tpu_custom_call" | custom-call | flops 1000000 | bytes 2097152 | tf_op jit(solution)/shard_map/pack_qkv/pallas_call | solution.py:589
  3.1 0.0 copy-start
  3.1 10.6 %all-to-all-start = ((bf16[32,128,128]{2,1,0:T(8,128)(2,1)}), bf16[32,128,128]{2,1,0:T(8,128)(2,1)S(1)}, u32[]{:S(2)}, u32[]{:S(2)}) async-start(bf16[32,128,128]{2,1,0:T(8,128)(2,1)} %pack_qkv.1), calls=%async_computation | async-start | bytes 2097152 | tf_op jit(solution)/shard_map/all_to_all | solution.py:559
  13.8 3.5 %collective-permute-start = (bf16[48,768]{1,0:T(8,128)(2,1)S(1)}, bf16[48,768]{1,0:T(8,128)(2,1)S(1)}, u32[]{:S(2)}, u32[]{:S(2)}) collective-permute-start(bf16[48,768]{1,0:T(8,128)(2,1)S(1)} %pad_maximum_fusion), channel_id=1, source_target_pairs={{0,1},{1,2},{2,3},{3,4},{4,5},{5,6},{6,7},{7,8},{8,9},{9,10},{10,1... | collective-permute-start | bytes 221192 | tf_op jit(solution)/shard_map/ppermute | solution.py:580
  17.4 1.9 %collective-permute-start.1 = (bf16[48,768]{1,0:T(8,128)(2,1)S(1)}, bf16[48,768]{1,0:T(8,128)(2,1)S(1)}, u32[]{:S(2)}, u32[]{:S(2)}) collective-permute-start(bf16[48,768]{1,0:T(8,128)(2,1)S(1)} %pad_maximum_fusion.1), channel_id=1, source_target_pairs={{1,0},{2,1},{3,2},{4,3},{5,4},{6,5},{7,6},{8,7},{9,8},{10,9},{11,1... | collective-permute-start | bytes 221192 | tf_op jit(solution)/shard_map/ppermute | solution.py:583
  19.3 7.1 %collective-permute-done.refs_1_.refs_4_ = bf16[48,768]{1,0:T(8,128)(2,1)S(1)} collective-permute-done((bf16[48,768]{1,0:T(8,128)(2,1)S(1)}, bf16[48,768]{1,0:T(8,128)(2,1)S(1)}, u32[]{:S(2)}, u32[]{:S(2)}) %collective-permute-start) | collective-permute-done | bytes 73760 | tf_op jit(solution)/shard_map/ppermute | solution.py:580
  26.3 2.1 %collective-permute-done.1.refs_2_.refs_5_ = bf16[48,768]{1,0:T(8,128)(2,1)S(1)} collective-permute-done((bf16[48,768]{1,0:T(8,128)(2,1)S(1)}, bf16[48,768]{1,0:T(8,128)(2,1)S(1)}, u32[]{:S(2)}, u32[]{:S(2)}) %collective-permute-start.1) | collective-permute-done | bytes 73760 | tf_op jit(solution)/shard_map/ppermute | solution.py:583
  28.5 2.5 %all-to-all-done.refs_0_ = bf16[32,128,128]{2,1,0:T(8,128)(2,1)S(1)} async-done(((bf16[32,128,128]{2,1,0:T(8,128)(2,1)}), bf16[32,128,128]{2,1,0:T(8,128)(2,1)S(1)}, u32[]{:S(2)}, u32[]{:S(2)}) %all-to-all-start) | async-done | bytes 1048608 | tf_op jit(solution)/shard_map/all_to_all | solution.py:559
  31.0 2.3 %collective-permute-start.2 = (bf16[32,128,128]{2,1,0:T(8,128)(2,1)S(1)}, bf16[32,128,128]{2,1,0:T(8,128)(2,1)S(1)}, u32[]{:S(2)}, u32[]{:S(2)}) collective-permute-start(bf16[32,128,128]{2,1,0:T(8,128)(2,1)S(1)} %received.1.refs_0_.refs_1_), channel_id=1, source_target_pairs={{0,1},{1,0},{2,3},{3,2},{4,5},{5,4},{6,7},{7,6},{8,9},{9,8},{10,11... | collective-permute-start | bytes 3145736 | tf_op jit(solution)/shard_map/ppermute | solution.py:613
  33.3 3.1 %attend_forward_own.1 = (f32[1024,128]{1,0:T(8,128)S(1)}, f32[1024,128]{1,0:T(8,128)S(1)}, f32[1024,128]{1,0:T(8,128)S(1)}) custom-call(bf16[32,128,128]{2,1,0:T(8,128)(2,1)S(1)} %received.1.refs_0_.refs_1_), custom_call_target="tpu_custom_call" | custom-call | flops 1073741824 | bytes 2097152 | tf_op jit(solution)/shard_map/attend_forward_own/pallas_call | solution.py:621
  36.4 3.8 %attend_forward_other.1 = (bf16[32,48,128]{2,1,0:T(8,128)(2,1)S(1)}, bf16[1024,128]{1,0:T(8,128)(2,1)S(1)}) custom-call(s32[1]{0:T(128)} %bitcast.7.refs_0_, bf16[32,128,128]{2,1,0:T(8,128)(2,1)S(1)} %received.1.refs_0_.refs_1_, bf16[32,128,128]{2,1,0:T(8,128)(2,1)S(1)} %collective-permute-done.2.refs_2_.refs_0_, f32[1024,128]{1,0:T(8,128)S(1)} %get-tuple-element.25.refs_3_, ...), custom_call_target="tpu_custom_call" | custom-call | flops 1073741824 | bytes 2097152 | tf_op jit(solution)/shard_map/attend_forward_other/pallas_call | solution.py:632
  40.3 0.0 copy-start.2
  40.3 14.0 %all_to_all.20.refs_1_ = bf16[32,48,128]{2,1,0:T(8,128)(2,1)S(1)} all-to-all(bf16[32,48,128]{2,1,0:T(8,128)(2,1)S(1)} %get-tuple-element.28), channel_id=1, replica_groups=mesh['section'=16,'tm'=32] {'tm'}, dimensions={0} | all-to-all | bytes 786432 | tf_op jit(solution)/shard_map/all_to_all | solution.py:559
  54.3 0.7 copy-done.3
  55.0 5.4 %conv_block.1 = (bf16[32,32,128]{2,1,0:T(8,128)(2,1)S(1)}, bf16[128,768]{1,0:T(8,128)(2,1)S(1)}, bf16[128,768]{1,0:T(8,128)(2,1)}) custom-call(s32[1]{0:T(128)} %bitcast.7.refs_0_, bf16[32,48,128]{2,1,0:T(8,128)(2,1)S(1)} %all_to_all.20.refs_1_, bf16[128,768]{1,0:T(8,128)(2,1)S(1)} %bitcast.21, bf16[128,768]{1,0:T(8,128)(2,1)S(1)} %bitcast.22, ...), custom_call_target="tpu_custom_call" | custom-call | flops 10000000 | bytes 2097152 | tf_op jit(solution)/shard_map/conv_block/pallas_call | solution.py:645
  60.4 12.5 %all_to_all.21.refs_2_.refs_1_ = bf16[32,32,128]{2,1,0:T(8,128)(2,1)S(1)} all-to-all(bf16[32,32,128]{2,1,0:T(8,128)(2,1)S(1)} %get-tuple-element.29), channel_id=1, replica_groups=mesh['section'=16,'tm'=32] {'tm'}, dimensions={0} | all-to-all | bytes 524288 | tf_op jit(solution)/shard_map/all_to_all | solution.py:559
  72.9 5.9 %attend_backward_other.1 = (bf16[32,96,128]{2,1,0:T(8,128)(2,1)S(1)}, f32[1024,128]{1,0:T(8,128)S(1)}) custom-call(bf16[32,128,128]{2,1,0:T(8,128)(2,1)S(1)} %collective-permute-done.2.refs_2_.refs_0_, bf16[32,128,128]{2,1,0:T(8,128)(2,1)S(1)} %received.1.refs_0_.refs_1_, bf16[32,32,128]{2,1,0:T(8,128)(2,1)S(1)} %all_to_all.21.refs_2_.refs_1_, ...), custom_call_target="tpu_custom_call" | custom-call | flops 1000000 | bytes 2097152 | tf_op jit(solution)/shard_map/attend_backward_other/pallas_call | solution.py:675
  78.8 2.1 %collective-permute-start.4 = (bf16[32,96,128]{2,1,0:T(8,128)(2,1)S(1)}, bf16[32,96,128]{2,1,0:T(8,128)(2,1)S(1)}, u32[]{:S(2)}, u32[]{:S(2)}) collective-permute-start(bf16[32,96,128]{2,1,0:T(8,128)(2,1)S(1)} %get-tuple-element.36), channel_id=1, source_target_pairs={{0,1},{1,0},{2,3},{3,2},{4,5},{5,4},{6,7},{7,6},{8,9},{9,8},{10,11... | collective-permute-start | bytes 2359304 | tf_op jit(solution)/shard_map/ppermute | solution.py:685
  81.0 2.1 %collective-permute-start.3 = (bf16[128,768]{1,0:T(8,128)(2,1)S(1)}, bf16[128,768]{1,0:T(8,128)(2,1)S(1)}, u32[]{:S(2)}, u32[]{:S(2)}) collective-permute-start(bf16[128,768]{1,0:T(8,128)(2,1)S(1)} %get-tuple-element.32), channel_id=1, source_target_pairs={{0,32},{32,64},{64,96},{96,128},{128,160},{160,192},{192,224},{224... | collective-permute-start | bytes 589832 | tf_op jit(solution)/shard_map/ppermute | solution.py:662
  83.1 12.2 %collective-permute-done.3.refs_4_ = bf16[128,768]{1,0:T(8,128)(2,1)S(1)} collective-permute-done((bf16[128,768]{1,0:T(8,128)(2,1)S(1)}, bf16[128,768]{1,0:T(8,128)(2,1)S(1)}, u32[]{:S(2)}, u32[]{:S(2)}) %collective-permute-start.3) | collective-permute-done | bytes 196640 | tf_op jit(solution)/shard_map/ppermute | solution.py:662
  95.3 6.0 %attend_backward_own.1 = (bf16[32,96,128]{2,1,0:T(8,128)(2,1)S(1)}, bf16[32,32,128]{2,1,0:T(8,128)(2,1)S(1)}, bf16[128,768]{1,0:T(8,128)(2,1)}) custom-call(bf16[32,128,128]{2,1,0:T(8,128)(2,1)S(1)} %received.1.refs_0_.refs_1_, bf16[32,32,128]{2,1,0:T(8,128)(2,1)S(1)} %all_to_all.21.refs_2_.refs_1_, bf16[1024,128]{1,0:T(8,128)(2,1)S(1)} %get-tuple-element.30.refs_3_.refs_2_, ...), custom_call_target="tpu_custom_call" | custom-call | flops 2684354560 | bytes 2097152 | tf_op jit(solution)/shard_map/attend_backward_own/pallas_call | solution.py:686
  101.2 0.2 join_grads.1
  101.4 21.3 %all_to_all.22.refs_0_ = bf16[32,128,128]{2,1,0:T(8,128)(2,1)S(1)} all-to-all(bf16[32,128,128]{2,1,0:T(8,128)(2,1)S(1)} %join_grads.1), channel_id=1, replica_groups=mesh['section'=16,'tm'=32] {'tm'}, dimensions={0} | all-to-all | bytes 2097152 | tf_op jit(solution)/shard_map/all_to_all | solution.py:559
  122.7 1.3 %unpack_grads.1 = (bf16[128,768]{1,0:T(8,128)(2,1)}, bf16[128,768]{1,0:T(8,128)(2,1)}, bf16[128,768]{1,0:T(8,128)(2,1)}, f32[1,768]{1,0:T(1,128)}, f32[31,1,768]{2,1,0:T(1,128)}) custom-call(bf16[32,128,128]{2,1,0:T(8,128)(2,1)S(1)} %all_to_all.22.refs_0_), custom_call_target="tpu_custom_call" | custom-call | flops 1000000 | bytes 2097152 | tf_op jit(solution)/shard_map/unpack_grads/pallas_call | solution.py:709
  (12 shorter events, 0.0 us)
Async XLA Ops:
  3.1 10.6 %copy-start.1 = (bf16[1,128,768]{2,1,0:T(8,128)(2,1)S(1)}, bf16[1,128,768]{2,1,0:T(8,128)(2,1)}, u32[]{:S(2)}) copy-start(bf16[1,128,768]{2,1,0:T(8,128)(2,1)} %param.13) | copy-start | bytes 589828
  3.1 10.6 %copy-start = (bf16[1,128,768]{2,1,0:T(8,128)(2,1)S(1)}, bf16[1,128,768]{2,1,0:T(8,128)(2,1)}, u32[]{:S(2)}) copy-start(bf16[1,128,768]{2,1,0:T(8,128)(2,1)} %param.7) | copy-start | bytes 589828
  3.1 27.9 %all-to-all-start = ((bf16[32,128,128]{2,1,0:T(8,128)(2,1)}), bf16[32,128,128]{2,1,0:T(8,128)(2,1)S(1)}, u32[]{:S(2)}, u32[]{:S(2)}) async-start(bf16[32,128,128]{2,1,0:T(8,128)(2,1)} %pack_qkv.1), calls=%async_computation | async-start | bytes 2097152 | tf_op jit(solution)/shard_map/all_to_all | solution.py:559
  13.8 12.6 %collective-permute-start = (bf16[48,768]{1,0:T(8,128)(2,1)S(1)}, bf16[48,768]{1,0:T(8,128)(2,1)S(1)}, u32[]{:S(2)}, u32[]{:S(2)}) collective-permute-start(bf16[48,768]{1,0:T(8,128)(2,1)S(1)} %pad_maximum_fusion), channel_id=1, source_target_pairs={{0,1},{1,2},{2,3},{3,4},{4,5},{5,6},{6,7},{7,8},{8,9},{9,10},{10,1... | collective-permute-start | bytes 221192 | tf_op jit(solution)/shard_map/ppermute | solution.py:580
  17.4 11.1 %collective-permute-start.1 = (bf16[48,768]{1,0:T(8,128)(2,1)S(1)}, bf16[48,768]{1,0:T(8,128)(2,1)S(1)}, u32[]{:S(2)}, u32[]{:S(2)}) collective-permute-start(bf16[48,768]{1,0:T(8,128)(2,1)S(1)} %pad_maximum_fusion.1), channel_id=1, source_target_pairs={{1,0},{2,1},{3,2},{4,3},{5,4},{6,5},{7,6},{8,7},{9,8},{10,9},{11,1... | collective-permute-start | bytes 221192 | tf_op jit(solution)/shard_map/ppermute | solution.py:583
  31.0 5.4 %collective-permute-start.2 = (bf16[32,128,128]{2,1,0:T(8,128)(2,1)S(1)}, bf16[32,128,128]{2,1,0:T(8,128)(2,1)S(1)}, u32[]{:S(2)}, u32[]{:S(2)}) collective-permute-start(bf16[32,128,128]{2,1,0:T(8,128)(2,1)S(1)} %received.1.refs_0_.refs_1_), channel_id=1, source_target_pairs={{0,1},{1,0},{2,3},{3,2},{4,5},{5,4},{6,7},{7,6},{8,9},{9,8},{10,11... | collective-permute-start | bytes 3145736 | tf_op jit(solution)/shard_map/ppermute | solution.py:613
  40.3 14.1 %copy-start.2 = (f32[1,31,768]{2,0,1:T(1,128)S(1)}, f32[1,31,768]{2,0,1:T(1,128)}, u32[]{:S(2)}) copy-start(f32[1,31,768]{2,0,1:T(1,128)} %param.12) | copy-start | bytes 285700
  54.3 0.7 copy-start.3
  78.8 22.4 %collective-permute-start.4 = (bf16[32,96,128]{2,1,0:T(8,128)(2,1)S(1)}, bf16[32,96,128]{2,1,0:T(8,128)(2,1)S(1)}, u32[]{:S(2)}, u32[]{:S(2)}) collective-permute-start(bf16[32,96,128]{2,1,0:T(8,128)(2,1)S(1)} %get-tuple-element.36), channel_id=1, source_target_pairs={{0,1},{1,0},{2,3},{3,2},{4,5},{5,4},{6,7},{7,6},{8,9},{9,8},{10,11... | collective-permute-start | bytes 2359304 | tf_op jit(solution)/shard_map/ppermute | solution.py:685
  81.0 14.3 %collective-permute-start.3 = (bf16[128,768]{1,0:T(8,128)(2,1)S(1)}, bf16[128,768]{1,0:T(8,128)(2,1)S(1)}, u32[]{:S(2)}, u32[]{:S(2)}) collective-permute-start(bf16[128,768]{1,0:T(8,128)(2,1)S(1)} %get-tuple-element.32), channel_id=1, source_target_pairs={{0,32},{32,64},{64,96},{96,128},{128,160},{160,192},{192,224},{224... | collective-permute-start | bytes 589832 | tf_op jit(solution)/shard_map/ppermute | solution.py:662

commit v5 on v4

--- a/solution.py
+++ b/solution.py
@@ -93,11 +93,10 @@
     lane = lanes_of(frames)
     for half in range(2):
         tiles = [
-            q_ref[:, (3 * half + i) * LANES : (3 * half + i + 1) * LANES].astype(F32)
-            for i in range(3)
+            q_ref[:, (3 * half + i) * LANES : (3 * half + i + 1) * LANES] for i in range(3)
         ]
         for i, block in enumerate(tiles_to_heads(tiles)):
-            block = jnp.where(lane < HEAD_DIM, block, 0.0).astype(BF16)
+            block = jnp.where(lane < HEAD_DIM, block, jnp.zeros_like(block))
             for group in range(groups):
                 send_ref[(4 * half + i) * groups + group, Q_ROWS, :] = block[
                     group * SUB : (group + 1) * SUB
@@ -106,15 +105,15 @@
         copy.wait()
         for tile in range(CH // LANES):
             at = slice(tile * LANES, (tile + 1) * LANES)
-            turned[at, :] = source[:, at].astype(F32).T
+            turned[at, :] = source[:, at].T
     lane = lanes_of(HEAD_DIM)
     out = []
     for head in range(HEADS):
         at = slice(head * HEAD_DIM, (head + 1) * HEAD_DIM)
         keys_here, values_here = keys_t[at, :], values_t[at, :]
         halves = (
-            jnp.where(lane < HALF, keys_here, roll_lanes(values_here, HALF)).astype(BF16),
-            jnp.where(lane < HALF, roll_lanes(keys_here, HALF), values_here).astype(BF16),
+            jnp.where(lane < HALF, keys_here, roll_lanes(values_here, HALF)),
+            jnp.where(lane < HALF, roll_lanes(keys_here, HALF), values_here),
         )
         for group in range(groups):
             send_ref[head * groups + group, KV_ROWS, :] = halves[group % 2]
@@ -129,20 +128,20 @@
 
 def fill_half(half_ref, keys_t, values_t, keys, values):
     lane = lanes_of(HEAD_DIM)
-    zeros = jnp.zeros((LANES - HEAD_DIM, LANES), F32)
+    zeros = jnp.zeros((LANES - HEAD_DIM, LANES), BF16)
     for pair in range(half_ref.shape[0] // 2):
         at = slice(pair * LANES, (pair + 1) * LANES)
-        even = half_ref[2 * pair, KV_ROWS, :].astype(F32)
-        odd = half_ref[2 * pair + 1, KV_ROWS, :].astype(F32)
+        even = half_ref[2 * pair, KV_ROWS, :]
+        odd = half_ref[2 * pair + 1, KV_ROWS, :]
         for turned, natural, block in (
             (keys_t, keys, jnp.where(lane < HALF, even, roll_lanes(odd, HALF))),
             (values_t, values, jnp.where(lane < HALF, roll_lanes(even, HALF), odd)),
         ):
             block = jnp.concatenate([block, zeros], axis=0)
             if turned is not None:
-                turned[:, at] = block.astype(BF16)
+                turned[:, at] = block
             if natural is not None:
-                natural[at, :] = block.T.astype(BF16)
+                natural[at, :] = block.T
 
 
 def attend(got_ref, state, finish, block, chunk, keys, values, scores):
@@ -249,12 +248,12 @@
     lane = lanes_of(48)
     for device in range(count):
         near = jnp.clip(device + side, 0, count - 1)
-        beside = out_ref[pl.ds(pl.multiple_of(near * SUB, SUB), SUB), :].astype(F32)
-        own = out_ref[device * SUB : (device + 1) * SUB, :].astype(F32)
+        beside = out_ref[pl.ds(pl.multiple_of(near * SUB, SUB), SUB), :]
+        own = out_ref[device * SUB : (device + 1) * SUB, :]
         tail = beside[16:32]
         spare = jnp.concatenate([roll_lanes(tail, by) for by in (96, 64, 32)], axis=0)
         piece = jnp.concatenate([own, beside[0:16]], axis=0)
-        send_ref[device] = jnp.where(lane < HEAD_DIM, piece, spare).astype(BF16)
+        send_ref[device] = jnp.where(lane < HEAD_DIM, piece, spare)
 
 
 def halo_of(piece):
@@ -419,9 +418,9 @@
         delta = jnp.sum(grads * out, axis=1, keepdims=True)
         in_log = (lane >= HEAD_DIM) & (lane < HEAD_DIM + 3)
         logs = jnp.sum(jnp.where(in_log, out, 0.0), axis=1, keepdims=True)
-        rows_t = rows.astype(F32).T.astype(BF16)[0:HEAD_DIM]
-        grads_t = grads.T.astype(BF16)[0:HEAD_DIM]
         grads = grads.astype(BF16)
+        rows_t = rows.T[0:HEAD_DIM]
+        grads_t = grads.T[0:HEAD_DIM]
         result = jnp.zeros((block, LANES), F32)
         for start in range(0, key_count, chunk):
             part = slice(start, start + chunk)
@@ -442,12 +441,10 @@
     lane = lanes_of(HEAD_DIM)
     for pair in range(got_ref.shape[0] // 2):
         at = slice(pair * LANES, (pair + 1) * LANES)
-        grad_k = grad_keys[:, at] * SCALE
-        grad_v = grad_values[:, at]
-        part_ref[2 * pair] = jnp.where(lane < HALF, grad_k, roll_lanes(grad_v, HALF)).astype(BF16)
-        part_ref[2 * pair + 1] = jnp.where(
-            lane < HALF, roll_lanes(grad_k, HALF), grad_v
-        ).astype(BF16)
+        grad_k = (grad_keys[:, at] * SCALE).astype(BF16)
+        grad_v = grad_values[:, at].astype(BF16)
+        part_ref[2 * pair] = jnp.where(lane < HALF, grad_k, roll_lanes(grad_v, HALF))
+        part_ref[2 * pair + 1] = jnp.where(lane < HALF, roll_lanes(grad_k, HALF), grad_v)
 
 
 def backward_first_kernel(
@@ -476,15 +473,10 @@
     grads_ref,
     out_ref,
     grad_q_ref,
-    arrived_ref,
     part_ref,
     piece_ref,
-    next_hbm,
     *scratch,
 ):
-    *scratch, next_sem = scratch
-    passed = pltpu.make_async_copy(arrived_ref, next_hbm, next_sem)
-    passed.start()
     sums = jnp.zeros((SUB, LANES), F32)
     for source in range(grads_ref.shape[0]):
         sums = sums + grads_ref[source].astype(F32)
@@ -497,7 +489,6 @@
     backward(
         got_ref, got_ref, grads_ref, out_ref, part_ref, finish, block, chunk, *scratch
     )
-    passed.wait()
 
 
 def join_kernel(part_ref, other_ref, piece_ref, send_ref):
@@ -509,8 +500,9 @@
 
 
 def unpack_kernel(
-    groups, got_ref, q_ref, k_ref, v_ref, gain_ref, taps_ref, keys_t, values_t
+    groups, got_ref, arrived_ref, q_ref, k_ref, v_ref, gain_ref, taps_ref, next_ref, keys_t, values_t
 ):
+    next_ref[...] = arrived_ref[...]
     count = got_ref.shape[0]
     lane = lanes_of(HEAD_DIM)
     for head in range(HEADS):
@@ -519,7 +511,7 @@
             sum(
                 got_ref[head * groups + group, KV_ROWS, :].astype(F32)
                 for group in range(parity, groups, 2)
-            )
+            ).astype(BF16)
             for parity in range(2)
         )
         keys_t[at, :] = jnp.where(lane < HALF, low, roll_lanes(high, HALF))
@@ -527,18 +519,18 @@
     for target, turned in ((k_ref, keys_t), (v_ref, values_t)):
         for tile in range(CH // LANES):
             at = slice(tile * LANES, (tile + 1) * LANES)
-            target[:, at] = turned[at, :].T.astype(BF16)
+            target[:, at] = turned[at, :].T
     for half in range(2):
         heads = [
             jnp.concatenate(
                 [got_ref[(4 * half + i) * groups + group, Q_ROWS, :] for group in range(groups)],
                 axis=0,
-            ).astype(F32)
+            )
             for i in range(4)
         ]
         for i, block in enumerate(heads_to_tiles(heads)):
             at = slice((3 * half + i) * LANES, (3 * half + i + 1) * LANES)
-            q_ref[:, at] = block.astype(BF16)
+            q_ref[:, at] = block
     lane = lanes_of(8)
     for device in range(count):
         piece = got_ref[device, Q_ROWS, :].astype(F32)
@@ -574,6 +566,7 @@
     resid, queries, keys, values, cotangent = (
         array[0] for array in (resid, queries, keys, values, cotangent)
     )
+    taps = taps.reshape(TAPS, 1, CH)
     up = [(i, i + 1) for i in range(count - 1)]
     down = [(i + 1, i) for i in range(count - 1)]
     partner = [(i, i ^ 1) for i in range(count)]
@@ -593,7 +586,7 @@
         ANY,
         [pltpu.VMEM((frames, CH), BF16)] * 3
         + [pltpu.VMEM((count, PIECE_ROWS, LANES), BF16)]
-        + [pltpu.VMEM((CH, LANES), F32)] * 2
+        + [pltpu.VMEM((CH, LANES), BF16)] * 2
         + [pltpu.SemaphoreType.DMA((3,)), pltpu.SemaphoreType.DMA((HEADS,))],
         56,
         1000000,
@@ -602,14 +595,14 @@
     got = call(
         lambda *refs: None,
         pieces,
-        [ANY] * 3,
+        [ANY] * 5,
         ANY,
         [],
         8,
         0,
         "received",
         aliases={0: 0},
-    )(exchange(sent), before, after)
+    )(exchange(sent), before, after, gain, taps)
     swapped = lax.ppermute(got, "tm", partner)
 
     block, chunk = 256, 512
@@ -657,7 +650,7 @@
         16,
         10000000,
         "conv_block",
-    )(place, returned, resid, cotangent, before, after, gain, taps.reshape(TAPS, 1, CH))
+    )(place, returned, resid, cotangent, before, after, gain, taps)
     grads_got = exchange(grads_sent)
     arrived = lax.ppermute(
         block_out, "section", [(i, (i + 1) % sections) for i in range(sections)]
@@ -679,21 +672,21 @@
         (VMEM,) * 2,
         backward_scratch,
         24,
-        1000000,
+        5 * matmul,
         "attend_backward_other",
     )(swapped, got, grads_got, head_out)
     arrived_part = lax.ppermute(other_part, "tm", partner)
-    own_part, grad_q_pieces, next_input = call(
+    own_part, grad_q_pieces = call(
         lambda *refs: backward_second_kernel(block, chunk, *refs),
-        (part_shape, shape((count, SUB, LANES), BF16), rows_shape),
-        [VMEM] * 4 + [ANY],
-        (VMEM,) * 2 + (ANY,),
-        backward_scratch + [pltpu.SemaphoreType.DMA],
+        (part_shape, shape((count, SUB, LANES), BF16)),
+        [VMEM] * 4,
+        (VMEM,) * 2,
+        backward_scratch,
         24,
         5 * matmul,
         "attend_backward_own",
         own * half,
-    )(got, grads_got, head_out, grad_q, arrived)
+    )(got, grads_got, head_out, grad_q)
     grads_out = call(
         join_kernel,
         pieces,
@@ -706,7 +699,7 @@
     )(own_part, arrived_part, grad_q_pieces)
     back = exchange(grads_out)
 
-    grad_q, grad_k, grad_v, grad_gain, grad_taps = call(
+    grad_q, grad_k, grad_v, grad_gain, grad_taps, next_input = call(
         lambda *refs: unpack_kernel(groups, *refs),
         (
             rows_shape,
@@ -714,14 +707,15 @@
             rows_shape,
             shape((1, CH), F32),
             shape((TAPS, 1, CH), F32),
+            rows_shape,
         ),
-        [VMEM],
-        (VMEM,) * 5,
-        [pltpu.VMEM((CH, LANES), F32)] * 2,
+        [VMEM] * 2,
+        (VMEM,) * 6,
+        [pltpu.VMEM((CH, LANES), BF16)] * 2,
         8,
         1000000,
         "unpack_grads",
-    )(back)
+    )(back, arrived)
     return (
         next_input[None],
         grad_resid[None],

time: 124 us -> 110 us (0.89)
  blocking collectives: 47.8 us -> 26.4 us
  starting transfers between devices: 22.6 us -> 26.6 us
  waiting for transfers between devices: 23.9 us -> 26.9 us
    all_to_all x3 -> x2, blocking collectives: 47.8 us -> 26.4 us  [exchange(): return lax.all_to_all(pieces, 'tm', split_axis=0, concat_axis=0, tiled=True)]
    all_to_all x1 -> x2, starting transfers between devices: 10.6 us -> 14.5 us  [exchange(): return lax.all_to_all(pieces, 'tm', split_axis=0, concat_axis=0, tiled=True)]
    all_to_all x1 -> x2, waiting for transfers between devices: 2.53 us -> 5.63 us  [exchange(): return lax.all_to_all(pieces, 'tm', split_axis=0, concat_axis=0, tiled=True)]
  transfers between devices with their start and end apart: 6 -> 7, of which waited for: 4 -> 5; matrix products, arithmetic and copies ran while one was open for 0% -> 0% of each run, Pallas kernels for 7% -> 8%
where the time goes in v5:
time: 110 us
  Pallas kernels  28.7 us (26%)
  waiting for transfers between devices  26.9 us (24%)
  starting transfers between devices  26.6 us (24%)
  blocking collectives  26.4 us (24%)
    all_to_all x2, blocking collectives, exchange(): return lax.all_to_all(pieces, 'tm', split_axis=0, concat_axis=0, tiled=True)  26.4 us
    all_to_all x2, starting transfers between devices, exchange(): return lax.all_to_all(pieces, 'tm', split_axis=0, concat_axis=0, tiled=True)  14.5 us
    ppermute x1, waiting for transfers between devices, local(): lax.ppermute(block_out, 'section', [(i, (i + 1) % sections) for i in rang...  12.3 us
    ppermute x1, waiting for transfers between devices, local(): lax.ppermute(jnp.concatenate([resid[frames - SUB:], cotangent[frames - ed...  6.91 us
    pallas_call x1, Pallas kernels, local(): call(lambda *refs: backward_first_kernel(block, chunk, *refs), (part_shap...  5.88 us
    pallas_call x1, Pallas kernels, local(): call(lambda *refs: backward_second_kernel(block, chunk, *refs), (part_sha...  5.84 us
    all_to_all x2, waiting for transfers between devices, exchange(): return lax.all_to_all(pieces, 'tm', split_axis=0, concat_axis=0, tiled=True)  5.63 us
    pallas_call x1, Pallas kernels, local(): call(lambda *refs: conv_kernel(groups, count, *refs), (shape((count, SUB,...  5.41 us
  transfers between devices with their start and end apart: 7, of which 5 were waited for; matrix products, arithmetic and copies ran while one was open for 0% of the time, Pallas kernels for 8%

profile of v5, /device:TPU:1, one launch (start us, length us, event | category | flops | bytes accessed | tf_op | source)
XLA Modules:
  0.0 109.5 jit_solution(11288942672398643372)
XLA Ops:
  0.6 2.4 %pack_qkv.1 = bf16[32,128,128]{2,1,0:T(8,128)(2,1)} custom-call(bf16[128,768]{1,0:T(8,128)(2,1)} %bitcast.25, bf16[128,768]{1,0:T(8,128)(2,1)} %bitcast.26, bf16[128,768]{1,0:T(8,128)(2,1)} %bitcast.27), custom_call_target="tpu_custom_call" | custom-call | flops 1000000 | bytes 2097152 | tf_op jit(solution)/shard_map/pack_qkv/pallas_call | solution.py:582
  3.0 0.0 copy-start.2
  3.1 0.0 copy-start
  3.1 10.6 %all-to-all-start = ((bf16[32,128,128]{2,1,0:T(8,128)(2,1)}), bf16[32,128,128]{2,1,0:T(8,128)(2,1)S(1)}, u32[]{:S(2)}, u32[]{:S(2)}) async-start(bf16[32,128,128]{2,1,0:T(8,128)(2,1)} %pack_qkv.1), calls=%async_computation | async-start | bytes 2097152 | tf_op jit(solution)/shard_map/all_to_all | solution.py:551
  13.8 3.7 %collective-permute-start = (bf16[48,768]{1,0:T(8,128)(2,1)S(1)}, bf16[48,768]{1,0:T(8,128)(2,1)S(1)}, u32[]{:S(2)}, u32[]{:S(2)}) collective-permute-start(bf16[48,768]{1,0:T(8,128)(2,1)S(1)} %pad_maximum_fusion), channel_id=1, source_target_pairs={{0,1},{1,2},{2,3},{3,4},{4,5},{5,6},{6,7},{7,8},{8,9},{9,10},{10,1... | collective-permute-start | bytes 221192 | tf_op jit(solution)/shard_map/ppermute | solution.py:573
  17.5 1.9 %collective-permute-start.1 = (bf16[48,768]{1,0:T(8,128)(2,1)S(1)}, bf16[48,768]{1,0:T(8,128)(2,1)S(1)}, u32[]{:S(2)}, u32[]{:S(2)}) collective-permute-start(bf16[48,768]{1,0:T(8,128)(2,1)S(1)} %pad_maximum_fusion.1), channel_id=1, source_target_pairs={{1,0},{2,1},{3,2},{4,3},{5,4},{6,5},{7,6},{8,7},{9,8},{10,9},{11,1... | collective-permute-start | bytes 221192 | tf_op jit(solution)/shard_map/ppermute | solution.py:576
  19.4 6.9 %collective-permute-done.refs_1_.refs_4_ = bf16[48,768]{1,0:T(8,128)(2,1)S(1)} collective-permute-done((bf16[48,768]{1,0:T(8,128)(2,1)S(1)}, bf16[48,768]{1,0:T(8,128)(2,1)S(1)}, u32[]{:S(2)}, u32[]{:S(2)}) %collective-permute-start) | collective-permute-done | bytes 73760 | tf_op jit(solution)/shard_map/ppermute | solution.py:573
  26.3 2.1 %collective-permute-done.1.refs_2_.refs_5_ = bf16[48,768]{1,0:T(8,128)(2,1)S(1)} collective-permute-done((bf16[48,768]{1,0:T(8,128)(2,1)S(1)}, bf16[48,768]{1,0:T(8,128)(2,1)S(1)}, u32[]{:S(2)}, u32[]{:S(2)}) %collective-permute-start.1) | collective-permute-done | bytes 73760 | tf_op jit(solution)/shard_map/ppermute | solution.py:576
  28.4 2.5 %all-to-all-done.refs_0_ = bf16[32,128,128]{2,1,0:T(8,128)(2,1)S(1)} async-done(((bf16[32,128,128]{2,1,0:T(8,128)(2,1)}), bf16[32,128,128]{2,1,0:T(8,128)(2,1)S(1)}, u32[]{:S(2)}, u32[]{:S(2)}) %all-to-all-start) | async-done | bytes 1048608 | tf_op jit(solution)/shard_map/all_to_all | solution.py:551
  31.0 2.3 %collective-permute-start.2 = (bf16[32,128,128]{2,1,0:T(8,128)(2,1)S(1)}, bf16[32,128,128]{2,1,0:T(8,128)(2,1)S(1)}, u32[]{:S(2)}, u32[]{:S(2)}) collective-permute-start(bf16[32,128,128]{2,1,0:T(8,128)(2,1)S(1)} %received.1.refs_0_.refs_1_), channel_id=1, source_target_pairs={{0,1},{1,0},{2,3},{3,2},{4,5},{5,4},{6,7},{7,6},{8,9},{9,8},{10,11... | collective-permute-start | bytes 3145736 | tf_op jit(solution)/shard_map/ppermute | solution.py:606
  33.3 3.1 %attend_forward_own.1 = (f32[1024,128]{1,0:T(8,128)S(1)}, f32[1024,128]{1,0:T(8,128)S(1)}, f32[1024,128]{1,0:T(8,128)S(1)}) custom-call(bf16[32,128,128]{2,1,0:T(8,128)(2,1)S(1)} %received.1.refs_0_.refs_1_), custom_call_target="tpu_custom_call" | custom-call | flops 1073741824 | bytes 2097152 | tf_op jit(solution)/shard_map/attend_forward_own/pallas_call | solution.py:614
  36.4 3.6 %attend_forward_other.1 = (bf16[32,48,128]{2,1,0:T(8,128)(2,1)S(1)}, bf16[1024,128]{1,0:T(8,128)(2,1)S(1)}) custom-call(s32[1]{0:T(128)} %bitcast.8.refs_0_, bf16[32,128,128]{2,1,0:T(8,128)(2,1)S(1)} %received.1.refs_0_.refs_1_, bf16[32,128,128]{2,1,0:T(8,128)(2,1)S(1)} %collective-permute-done.2.refs_2_.refs_0_, f32[1024,128]{1,0:T(8,128)S(1)} %get-tuple-element.25.refs_3_, ...), custom_call_target="tpu_custom_call" | custom-call | flops 1073741824 | bytes 2097152 | tf_op jit(solution)/shard_map/attend_forward_other/pallas_call | solution.py:625
  40.0 13.9 %all_to_all.20.refs_1_ = bf16[32,48,128]{2,1,0:T(8,128)(2,1)S(1)} all-to-all(bf16[32,48,128]{2,1,0:T(8,128)(2,1)S(1)} %get-tuple-element.28), channel_id=1, replica_groups=mesh['section'=16,'tm'=32] {'tm'}, dimensions={0} | all-to-all | bytes 786432 | tf_op jit(solution)/shard_map/all_to_all | solution.py:551
  53.9 5.4 %conv_block.1 = (bf16[32,32,128]{2,1,0:T(8,128)(2,1)S(1)}, bf16[128,768]{1,0:T(8,128)(2,1)S(1)}, bf16[128,768]{1,0:T(8,128)(2,1)}) custom-call(s32[1]{0:T(128)} %bitcast.8.refs_0_, bf16[32,48,128]{2,1,0:T(8,128)(2,1)S(1)} %all_to_all.20.refs_1_, bf16[128,768]{1,0:T(8,128)(2,1)S(1)} %bitcast.21, bf16[128,768]{1,0:T(8,128)(2,1)S(1)} %bitcast.24, ...), custom_call_target="tpu_custom_call" | custom-call | flops 10000000 | bytes 2097152 | tf_op jit(solution)/shard_map/conv_block/pallas_call | solution.py:638
  59.3 12.5 %all_to_all.21.refs_2_.refs_1_ = bf16[32,32,128]{2,1,0:T(8,128)(2,1)S(1)} all-to-all(bf16[32,32,128]{2,1,0:T(8,128)(2,1)S(1)} %get-tuple-element.29), channel_id=1, replica_groups=mesh['section'=16,'tm'=32] {'tm'}, dimensions={0} | all-to-all | bytes 524288 | tf_op jit(solution)/shard_map/all_to_all | solution.py:551
  71.8 5.9 %attend_backward_other.1 = (bf16[32,96,128]{2,1,0:T(8,128)(2,1)S(1)}, f32[1024,128]{1,0:T(8,128)S(1)}) custom-call(bf16[32,128,128]{2,1,0:T(8,128)(2,1)S(1)} %collective-permute-done.2.refs_2_.refs_0_, bf16[32,128,128]{2,1,0:T(8,128)(2,1)S(1)} %received.1.refs_0_.refs_1_, bf16[32,32,128]{2,1,0:T(8,128)(2,1)S(1)} %all_to_all.21.refs_2_.refs_1_, ...), custom_call_target="tpu_custom_call" | custom-call | flops 2684354560 | bytes 2097152 | tf_op jit(solution)/shard_map/attend_backward_other/pallas_call | solution.py:668
  77.7 2.4 %collective-permute-start.3 = (bf16[32,96,128]{2,1,0:T(8,128)(2,1)S(1)}, bf16[32,96,128]{2,1,0:T(8,128)(2,1)S(1)}, u32[]{:S(2)}, u32[]{:S(2)}) collective-permute-start(bf16[32,96,128]{2,1,0:T(8,128)(2,1)S(1)} %get-tuple-element.33), channel_id=1, source_target_pairs={{0,1},{1,0},{2,3},{3,2},{4,5},{5,4},{6,7},{7,6},{8,9},{9,8},{10,11... | collective-permute-start | bytes 2359304 | tf_op jit(solution)/shard_map/ppermute | solution.py:678
  80.0 5.8 %attend_backward_own.1 = (bf16[32,96,128]{2,1,0:T(8,128)(2,1)S(1)}, bf16[32,32,128]{2,1,0:T(8,128)(2,1)S(1)}) custom-call(bf16[32,128,128]{2,1,0:T(8,128)(2,1)S(1)} %received.1.refs_0_.refs_1_, bf16[32,32,128]{2,1,0:T(8,128)(2,1)S(1)} %all_to_all.21.refs_2_.refs_1_, bf16[1024,128]{1,0:T(8,128)(2,1)S(1)} %get-tuple-element.30.refs_3_.refs_2_, ...), custom_call_target="tpu_custom_call" | custom-call | flops 2684354560 | bytes 2097152 | tf_op jit(solution)/shard_map/attend_backward_own/pallas_call | solution.py:679
  85.9 1.2 %join_grads.1 = bf16[32,128,128]{2,1,0:T(8,128)(2,1)} custom-call(bf16[32,96,128]{2,1,0:T(8,128)(2,1)S(1)} %get-tuple-element.32.part_ref, bf16[32,96,128]{2,1,0:T(8,128)(2,1)S(1)} %collective-permute-done.3.other_ref, bf16[32,32,128]{2,1,0:T(8,128)(2,1)S(1)} %get-tuple-element.34.piece_ref), custom_call_target="tpu_custom_call" | custom-call | flops 1000000 | bytes 2097152 | tf_op jit(solution)/shard_map/join_grads/pallas_call | solution.py:690
  87.1 3.9 %all-to-all-start.3 = ((bf16[32,128,128]{2,1,0:T(8,128)(2,1)}), bf16[32,128,128]{2,1,0:T(8,128)(2,1)S(1)}, u32[]{:S(2)}, u32[]{:S(2)}) async-start(bf16[32,128,128]{2,1,0:T(8,128)(2,1)} %join_grads.1), calls=%async_computation.3 | async-start | bytes 2097152 | tf_op jit(solution)/shard_map/all_to_all | solution.py:551
  90.9 1.9 %collective-permute-start.4 = (bf16[128,768]{1,0:T(8,128)(2,1)S(1)}, bf16[128,768]{1,0:T(8,128)(2,1)S(1)}, u32[]{:S(2)}, u32[]{:S(2)}) collective-permute-start(bf16[128,768]{1,0:T(8,128)(2,1)S(1)} %get-tuple-element.35), channel_id=1, source_target_pairs={{0,32},{32,64},{64,96},{96,128},{128,160},{160,192},{192,224},{224... | collective-permute-start | bytes 589832 | tf_op jit(solution)/shard_map/ppermute | solution.py:655
  92.9 12.3 %collective-permute-done.4.refs_1_ = bf16[128,768]{1,0:T(8,128)(2,1)S(1)} collective-permute-done((bf16[128,768]{1,0:T(8,128)(2,1)S(1)}, bf16[128,768]{1,0:T(8,128)(2,1)S(1)}, u32[]{:S(2)}, u32[]{:S(2)}) %collective-permute-start.4) | collective-permute-done | bytes 196640 | tf_op jit(solution)/shard_map/ppermute | solution.py:655
  105.1 3.1 %all-to-all-done.3.refs_0_ = bf16[32,128,128]{2,1,0:T(8,128)(2,1)S(1)} async-done(((bf16[32,128,128]{2,1,0:T(8,128)(2,1)}), bf16[32,128,128]{2,1,0:T(8,128)(2,1)S(1)}, u32[]{:S(2)}, u32[]{:S(2)}) %all-to-all-start.3) | async-done | bytes 1048608 | tf_op jit(solution)/shard_map/all_to_all | solution.py:551
  108.2 1.3 %unpack_grads.1 = (bf16[128,768]{1,0:T(8,128)(2,1)}, bf16[128,768]{1,0:T(8,128)(2,1)}, bf16[128,768]{1,0:T(8,128)(2,1)}, f32[1,768]{1,0:T(1,128)}, f32[31,1,768]{2,1,0:T(1,128)}, /*index=5*/bf16[128,768]{1,0:T(8,128)(2,1)}) custom-call(bf16[32,128,128]{2,1,0:T(8,128)(2,1)S(1)} %all-to-all-done.3.refs_0_, bf16[128,768]{1,0:T(8,128)(2,1)S(1)} %collective-permute-done.4.refs_1_), custom_call_target="tpu_custom_call" | custom-call | flops 1000000 | bytes 2097152 | tf_op jit(solution)/shard_map/unpack_grads/pallas_call | solution.py:702
  (13 shorter events, 0.1 us)
Async XLA Ops:
  3.0 10.6 %copy-start.2 = (bf16[1,128,768]{2,1,0:T(8,128)(2,1)S(1)}, bf16[1,128,768]{2,1,0:T(8,128)(2,1)}, u32[]{:S(2)}) copy-start(bf16[1,128,768]{2,1,0:T(8,128)(2,1)} %param.13) | copy-start | bytes 589828
  3.1 10.6 %copy-start = (bf16[1,128,768]{2,1,0:T(8,128)(2,1)S(1)}, bf16[1,128,768]{2,1,0:T(8,128)(2,1)}, u32[]{:S(2)}) copy-start(bf16[1,128,768]{2,1,0:T(8,128)(2,1)} %param.7) | copy-start | bytes 589828
  3.1 27.9 %all-to-all-start = ((bf16[32,128,128]{2,1,0:T(8,128)(2,1)}), bf16[32,128,128]{2,1,0:T(8,128)(2,1)S(1)}, u32[]{:S(2)}, u32[]{:S(2)}) async-start(bf16[32,128,128]{2,1,0:T(8,128)(2,1)} %pack_qkv.1), calls=%async_computation | async-start | bytes 2097152 | tf_op jit(solution)/shard_map/all_to_all | solution.py:551
  13.7 17.2 %copy-start.1 = (f32[1,31,768]{2,0,1:T(1,128)S(1)}, f32[1,31,768]{2,0,1:T(1,128)}, u32[]{:S(2)}) copy-start(f32[1,31,768]{2,0,1:T(1,128)} %param.12) | copy-start | bytes 285700
  13.8 12.6 %collective-permute-start = (bf16[48,768]{1,0:T(8,128)(2,1)S(1)}, bf16[48,768]{1,0:T(8,128)(2,1)S(1)}, u32[]{:S(2)}, u32[]{:S(2)}) collective-permute-start(bf16[48,768]{1,0:T(8,128)(2,1)S(1)} %pad_maximum_fusion), channel_id=1, source_target_pairs={{0,1},{1,2},{2,3},{3,4},{4,5},{5,6},{6,7},{7,8},{8,9},{9,10},{10,1... | collective-permute-start | bytes 221192 | tf_op jit(solution)/shard_map/ppermute | solution.py:573
  17.4 13.5 %copy-start.3 = (f32[1,768]{1,0:T(1,128)S(1)}, f32[1,768]{1,0:T(1,128)}, u32[]{:S(2)}) copy-start(f32[1,768]{1,0:T(1,128)} %refs_6_.1) | copy-start | bytes 9220
  17.5 11.0 %collective-permute-start.1 = (bf16[48,768]{1,0:T(8,128)(2,1)S(1)}, bf16[48,768]{1,0:T(8,128)(2,1)S(1)}, u32[]{:S(2)}, u32[]{:S(2)}) collective-permute-start(bf16[48,768]{1,0:T(8,128)(2,1)S(1)} %pad_maximum_fusion.1), channel_id=1, source_target_pairs={{1,0},{2,1},{3,2},{4,3},{5,4},{6,5},{7,6},{8,7},{9,8},{10,9},{11,1... | collective-permute-start | bytes 221192 | tf_op jit(solution)/shard_map/ppermute | solution.py:576
  31.0 5.4 %collective-permute-start.2 = (bf16[32,128,128]{2,1,0:T(8,128)(2,1)S(1)}, bf16[32,128,128]{2,1,0:T(8,128)(2,1)S(1)}, u32[]{:S(2)}, u32[]{:S(2)}) collective-permute-start(bf16[32,128,128]{2,1,0:T(8,128)(2,1)S(1)} %received.1.refs_0_.refs_1_), channel_id=1, source_target_pairs={{0,1},{1,0},{2,3},{3,2},{4,5},{5,4},{6,7},{7,6},{8,9},{9,8},{10,11... | collective-permute-start | bytes 3145736 | tf_op jit(solution)/shard_map/ppermute | solution.py:606
  77.7 8.2 %collective-permute-start.3 = (bf16[32,96,128]{2,1,0:T(8,128)(2,1)S(1)}, bf16[32,96,128]{2,1,0:T(8,128)(2,1)S(1)}, u32[]{:S(2)}, u32[]{:S(2)}) collective-permute-start(bf16[32,96,128]{2,1,0:T(8,128)(2,1)S(1)} %get-tuple-element.33), channel_id=1, source_target_pairs={{0,1},{1,0},{2,3},{3,2},{4,5},{5,4},{6,7},{7,6},{8,9},{9,8},{10,11... | collective-permute-start | bytes 2359304 | tf_op jit(solution)/shard_map/ppermute | solution.py:678
  87.1 21.2 %all-to-all-start.3 = ((bf16[32,128,128]{2,1,0:T(8,128)(2,1)}), bf16[32,128,128]{2,1,0:T(8,128)(2,1)S(1)}, u32[]{:S(2)}, u32[]{:S(2)}) async-start(bf16[32,128,128]{2,1,0:T(8,128)(2,1)} %join_grads.1), calls=%async_computation.3 | async-start | bytes 2097152 | tf_op jit(solution)/shard_map/all_to_all | solution.py:551
  90.9 14.2 %collective-permute-start.4 = (bf16[128,768]{1,0:T(8,128)(2,1)S(1)}, bf16[128,768]{1,0:T(8,128)(2,1)S(1)}, u32[]{:S(2)}, u32[]{:S(2)}) collective-permute-start(bf16[128,768]{1,0:T(8,128)(2,1)S(1)} %get-tuple-element.35), channel_id=1, source_target_pairs={{0,32},{32,64},{64,96},{96,128},{128,160},{160,192},{192,224},{224... | collective-permute-start | bytes 589832 | tf_op jit(solution)/shard_map/ppermute | solution.py:655

commit v6 on v5

--- a/solution.py
+++ b/solution.py
@@ -126,10 +126,10 @@
         copy.wait()
 
 
-def fill_half(half_ref, keys_t, values_t, keys, values):
+def fill_half(half_ref, start, stop, keys_t, values_t, keys, values):
     lane = lanes_of(HEAD_DIM)
     zeros = jnp.zeros((LANES - HEAD_DIM, LANES), BF16)
-    for pair in range(half_ref.shape[0] // 2):
+    for pair in range(start // LANES, stop // LANES):
         at = slice(pair * LANES, (pair + 1) * LANES)
         even = half_ref[2 * pair, KV_ROWS, :]
         odd = half_ref[2 * pair + 1, KV_ROWS, :]
@@ -144,7 +144,7 @@
                 natural[at, :] = block.T
 
 
-def attend(got_ref, state, finish, block, chunk, keys, values, scores):
+def attend(got_ref, half_ref, state, finish, block, chunk, keys, values, scores):
     key_count = keys.shape[1]
     per = block // SUB
     blocks = got_ref.shape[0] // per
@@ -163,6 +163,7 @@
     peak = lowest
     rows = rows_of(0)
     for start in range(0, key_count, chunk):
+        fill_half(half_ref, start, start + chunk, keys, None, None, values)
         peak = score(0, rows, start, peak)
     for step in range(blocks):
         at = slice(step * block, (step + 1) * block)
@@ -203,14 +204,12 @@
     values,
     scores,
 ):
-    fill_half(got_ref, keys, None, None, values)
-
     def finish(at, top, total, result):
         top_ref[at, :] = top
         total_ref[at, :] = total
         result_ref[at, :] = result
 
-    attend(got_ref, None, finish, block, chunk, keys, values, scores)
+    attend(got_ref, got_ref, None, finish, block, chunk, keys, values, scores)
 
 
 def forward_second_kernel(
@@ -229,8 +228,6 @@
     values,
     scores,
 ):
-    fill_half(swapped_ref, keys, None, None, values)
-
     def finish(at, top, total, result):
         total = jnp.sum(total, axis=1, keepdims=True)
         rest = top + jnp.log2(total)
@@ -242,7 +239,8 @@
             rest = rest - part
         out_ref[at, :] = merged.astype(BF16)
 
-    attend(got_ref, (top_ref, total_ref, result_ref), finish, block, chunk, keys, values, scores)
+    state = (top_ref, total_ref, result_ref)
+    attend(got_ref, swapped_ref, state, finish, block, chunk, keys, values, scores)
     count = got_ref.shape[0]
     side = jnp.where(place_ref[0] % groups == groups - 1, -1, 1)
     lane = lanes_of(48)
@@ -285,11 +283,12 @@
     grad_conv,
     scaled,
     sums,
+    shifted,
+    grad_wide,
 ):
     frames = resid_ref.shape[0]
     sub = frames // groups
     wide = frames + 2 * sub
-    half_taps = (TAPS - 1) // 2
     edge = 16
     inner = frames + 2 * edge
     tiles = CH // LANES
@@ -326,6 +325,8 @@
     own = slice(sub, sub + frames)
     inverse_own = inverse[sub : sub + frames]
 
+    grad_wide[0:8, :] = jnp.zeros((8, LANES), F32)
+    grad_wide[8 + frames : 16 + frames, :] = jnp.zeros((8, LANES), F32)
     dots = jnp.zeros((frames, LANES), F32)
     for tile in range(tiles):
         at = slice(tile * LANES, (tile + 1) * LANES)
@@ -333,9 +334,12 @@
         value = (mixed[:, at] * inverse * gain_row).astype(BF16).astype(F32)
         normed[...] = jnp.where(inside, value, 0.0)
         conv = jnp.zeros((inner, LANES), F32)
-        for tap in range(TAPS):
-            first = lo + tap - half_taps
-            conv = conv + taps_ref[tap, :, at] * normed[first : first + inner, :]
+        for b in range(8):
+            part = jnp.zeros((inner + 8, LANES), F32)
+            for tap in range(b, TAPS, 8):
+                part = part + taps_ref[tap, :, at] * normed[tap - b : tap - b + inner + 8, :]
+            shifted[...] = part
+            conv = conv + shifted[b + 1 : b + 1 + inner, :]
         sig = jax.nn.sigmoid(conv)
         out_ref[:, at] = (
             mixed[own, at] + (conv * sig)[edge : edge + frames]
@@ -347,17 +351,19 @@
         value = (cot * sig * (1.0 + conv * (1.0 - sig))).astype(BF16).astype(F32)
         grad_conv[...] = jnp.where(inside_inner, value, 0.0)
         grad_normed = jnp.zeros((frames, LANES), F32)
-        grad_own = grad_conv[edge : edge + frames, :]
-        for tap in range(TAPS):
-            first = edge + half_taps - tap
-            grad_normed = (
-                grad_normed
-                + taps_ref[tap, :, at] * grad_conv[first : first + frames, :]
-            )
-            first = sub + tap - half_taps
-            sums[tap : tap + 1, at] = jnp.sum(
-                grad_own * normed[first : first + frames, :], axis=0, keepdims=True
-            )
+        grad_wide[8 : 8 + frames, :] = grad_conv[edge : edge + frames, :]
+        for b in range(8):
+            part = jnp.zeros((frames + 8, LANES), F32)
+            grad_here = grad_wide[7 - b : 15 - b + frames, :]
+            for tap in range(b, TAPS, 8):
+                first = tap - b
+                part = part + taps_ref[TAPS - 1 - tap, :, at] * grad_conv[first : first + frames + 8, :]
+                first = first + edge
+                sums[tap : tap + 1, at] = jnp.sum(
+                    grad_here * normed[first : first + frames + 8, :], axis=0, keepdims=True
+                )
+            shifted[0 : frames + 8, :] = part
+            grad_normed = grad_normed + shifted[b + 1 : b + 1 + frames, :]
         unit = mixed[own, at] * inverse_own
         sums[TAPS : TAPS + 1, at] = jnp.sum(grad_normed * unit, axis=0, keepdims=True)
         here = grad_normed * gain_row
@@ -404,11 +410,13 @@
     grad_keys,
     grad_values,
 ):
-    fill_half(half_ref, keys_t, values_t, keys, None)
+    fill_half(half_ref, 0, chunk, keys_t, values_t, keys, None)
     key_count = keys.shape[0]
+    steps = got_ref.shape[0] * SUB // block
+    lane_part = lanes_of(HEAD_DIM)
     per = block // SUB
     lane = lanes_of(block)
-    for step in range(got_ref.shape[0] // per):
+    for step in range(steps):
         sources = slice(step * per, (step + 1) * per)
         at = slice(step * block, (step + 1) * block)
         rows = got_ref[sources, Q_ROWS, :].reshape(block, LANES)
@@ -424,6 +432,10 @@
         result = jnp.zeros((block, LANES), F32)
         for start in range(0, key_count, chunk):
             part = slice(start, start + chunk)
+            if step == 0 and start + chunk < key_count:
+                fill_half(
+                    half_ref, start + chunk, start + 2 * chunk, keys_t, values_t, keys, None
+                )
             logits = jnp.dot(rows, keys_t[:, part], preferred_element_type=F32)
             probs = jnp.exp2(logits * SCALE2 - logs)
             grad_probs = jnp.dot(grads, values_t[:, part], preferred_element_type=F32)
@@ -431,20 +443,24 @@
             result = result + jnp.dot(grad_scores, keys[part, :], preferred_element_type=F32)
             grad_k = jnp.dot(rows_t, grad_scores, preferred_element_type=F32)
             grad_v = jnp.dot(grads_t, probs.astype(BF16), preferred_element_type=F32)
-            if step == 0:
+            if step > 0:
+                grad_k = grad_k + grad_keys[:, part]
+                grad_v = grad_v + grad_values[:, part]
+            if step + 1 < steps:
                 grad_keys[:, part] = grad_k
                 grad_values[:, part] = grad_v
-            else:
-                grad_keys[:, part] += grad_k
-                grad_values[:, part] += grad_v
+                continue
+            grad_k = (grad_k * SCALE).astype(BF16)
+            grad_v = grad_v.astype(BF16)
+            for first in range(0, chunk, LANES):
+                pair = (start + first) // LANES
+                here_k = grad_k[:, first : first + LANES]
+                here_v = grad_v[:, first : first + LANES]
+                part_ref[2 * pair] = jnp.where(lane_part < HALF, here_k, roll_lanes(here_v, HALF))
+                part_ref[2 * pair + 1] = jnp.where(
+                    lane_part < HALF, roll_lanes(here_k, HALF), here_v
+                )
         finish(step, sources, at, result * SCALE)
-    lane = lanes_of(HEAD_DIM)
-    for pair in range(got_ref.shape[0] // 2):
-        at = slice(pair * LANES, (pair + 1) * LANES)
-        grad_k = (grad_keys[:, at] * SCALE).astype(BF16)
-        grad_v = grad_values[:, at].astype(BF16)
-        part_ref[2 * pair] = jnp.where(lane < HALF, grad_k, roll_lanes(grad_v, HALF))
-        part_ref[2 * pair + 1] = jnp.where(lane < HALF, roll_lanes(grad_k, HALF), grad_v)
 
 
 def backward_first_kernel(
@@ -646,6 +662,8 @@
             pltpu.VMEM((frames + 2 * edge, LANES), F32),
             pltpu.VMEM((frames, CH), F32),
             pltpu.VMEM((TAPS + 1, CH), F32),
+            pltpu.VMEM((frames + 2 * edge + 8, LANES), F32),
+            pltpu.VMEM((frames + 16, LANES), F32),
         ],
         16,
         10000000,

time: 110 us -> 110 us (level)
  no operation moved by 1% of the time
where the time goes in v6:
time: 110 us; the launch traced here: 109 us
  Pallas kernels  28.4 us (26%)
  waiting for transfers between devices  26.9 us (24%)
  starting transfers between devices  26.6 us (24%)
  blocking collectives  26.4 us (24%)
    all_to_all x2, blocking collectives, exchange(): return lax.all_to_all(pieces, 'tm', split_axis=0, concat_axis=0, tiled=True)  26.4 us
    all_to_all x2, starting transfers between devices, exchange(): return lax.all_to_all(pieces, 'tm', split_axis=0, concat_axis=0, tiled=True)  14.5 us
    ppermute x1, waiting for transfers between devices, local(): lax.ppermute(block_out, 'section', [(i, (i + 1) % sections) for i in rang...  12.3 us
    ppermute x1, waiting for transfers between devices, local(): lax.ppermute(jnp.concatenate([resid[frames - SUB:], cotangent[frames - ed...  6.91 us
    pallas_call x1, Pallas kernels, local(): call(lambda *refs: backward_first_kernel(block, chunk, *refs), (part_shap...  5.87 us
    pallas_call x1, Pallas kernels, local(): call(lambda *refs: backward_second_kernel(block, chunk, *refs), (part_sha...  5.84 us
    all_to_all x2, waiting for transfers between devices, exchange(): return lax.all_to_all(pieces, 'tm', split_axis=0, concat_axis=0, tiled=True)  5.62 us
    pallas_call x1, Pallas kernels, local(): call(lambda *refs: conv_kernel(groups, count, *refs), (shape((count, SUB,...  5.1 us
  transfers between devices with their start and end apart: 7, of which 5 were waited for; matrix products, arithmetic and copies ran while one was open for 0% of the time, Pallas kernels for 8%

profile of v6, /device:TPU:1, one launch (start us, length us, event | category | flops | bytes accessed | tf_op | source)
XLA Modules:
  0.0 109.2 jit_solution(10512695278547657344)
XLA Ops:
  0.6 2.4 %pack_qkv.1 = bf16[32,128,128]{2,1,0:T(8,128)(2,1)} custom-call(bf16[128,768]{1,0:T(8,128)(2,1)} %bitcast.25, bf16[128,768]{1,0:T(8,128)(2,1)} %bitcast.26, bf16[128,768]{1,0:T(8,128)(2,1)} %bitcast.27), custom_call_target="tpu_custom_call" | custom-call | flops 1000000 | bytes 2097152 | tf_op jit(solution)/shard_map/pack_qkv/pallas_call | solution.py:598
  3.0 0.0 copy-start.2
  3.1 0.0 copy-start
  3.1 10.6 %all-to-all-start = ((bf16[32,128,128]{2,1,0:T(8,128)(2,1)}), bf16[32,128,128]{2,1,0:T(8,128)(2,1)S(1)}, u32[]{:S(2)}, u32[]{:S(2)}) async-start(bf16[32,128,128]{2,1,0:T(8,128)(2,1)} %pack_qkv.1), calls=%async_computation | async-start | bytes 2097152 | tf_op jit(solution)/shard_map/all_to_all | solution.py:567
  13.8 3.7 %collective-permute-start = (bf16[48,768]{1,0:T(8,128)(2,1)S(1)}, bf16[48,768]{1,0:T(8,128)(2,1)S(1)}, u32[]{:S(2)}, u32[]{:S(2)}) collective-permute-start(bf16[48,768]{1,0:T(8,128)(2,1)S(1)} %pad_maximum_fusion), channel_id=1, source_target_pairs={{0,1},{1,2},{2,3},{3,4},{4,5},{5,6},{6,7},{7,8},{8,9},{9,10},{10,1... | collective-permute-start | bytes 221192 | tf_op jit(solution)/shard_map/ppermute | solution.py:589
  17.5 1.9 %collective-permute-start.1 = (bf16[48,768]{1,0:T(8,128)(2,1)S(1)}, bf16[48,768]{1,0:T(8,128)(2,1)S(1)}, u32[]{:S(2)}, u32[]{:S(2)}) collective-permute-start(bf16[48,768]{1,0:T(8,128)(2,1)S(1)} %pad_maximum_fusion.1), channel_id=1, source_target_pairs={{1,0},{2,1},{3,2},{4,3},{5,4},{6,5},{7,6},{8,7},{9,8},{10,9},{11,1... | collective-permute-start | bytes 221192 | tf_op jit(solution)/shard_map/ppermute | solution.py:592
  19.4 6.9 %collective-permute-done.refs_1_.refs_4_ = bf16[48,768]{1,0:T(8,128)(2,1)S(1)} collective-permute-done((bf16[48,768]{1,0:T(8,128)(2,1)S(1)}, bf16[48,768]{1,0:T(8,128)(2,1)S(1)}, u32[]{:S(2)}, u32[]{:S(2)}) %collective-permute-start) | collective-permute-done | bytes 73760 | tf_op jit(solution)/shard_map/ppermute | solution.py:589
  26.3 2.1 %collective-permute-done.1.refs_2_.refs_5_ = bf16[48,768]{1,0:T(8,128)(2,1)S(1)} collective-permute-done((bf16[48,768]{1,0:T(8,128)(2,1)S(1)}, bf16[48,768]{1,0:T(8,128)(2,1)S(1)}, u32[]{:S(2)}, u32[]{:S(2)}) %collective-permute-start.1) | collective-permute-done | bytes 73760 | tf_op jit(solution)/shard_map/ppermute | solution.py:592
  28.4 2.5 %all-to-all-done.refs_0_ = bf16[32,128,128]{2,1,0:T(8,128)(2,1)S(1)} async-done(((bf16[32,128,128]{2,1,0:T(8,128)(2,1)}), bf16[32,128,128]{2,1,0:T(8,128)(2,1)S(1)}, u32[]{:S(2)}, u32[]{:S(2)}) %all-to-all-start) | async-done | bytes 1048608 | tf_op jit(solution)/shard_map/all_to_all | solution.py:567
  31.0 2.3 %collective-permute-start.2 = (bf16[32,128,128]{2,1,0:T(8,128)(2,1)S(1)}, bf16[32,128,128]{2,1,0:T(8,128)(2,1)S(1)}, u32[]{:S(2)}, u32[]{:S(2)}) collective-permute-start(bf16[32,128,128]{2,1,0:T(8,128)(2,1)S(1)} %received.1.refs_0_.refs_1_), channel_id=1, source_target_pairs={{0,1},{1,0},{2,3},{3,2},{4,5},{5,4},{6,7},{7,6},{8,9},{9,8},{10,11... | collective-permute-start | bytes 3145736 | tf_op jit(solution)/shard_map/ppermute | solution.py:622
  33.3 3.0 %attend_forward_own.1 = (f32[1024,128]{1,0:T(8,128)S(1)}, f32[1024,128]{1,0:T(8,128)S(1)}, f32[1024,128]{1,0:T(8,128)S(1)}) custom-call(bf16[32,128,128]{2,1,0:T(8,128)(2,1)S(1)} %received.1.refs_0_.refs_1_), custom_call_target="tpu_custom_call" | custom-call | flops 1073741824 | bytes 2097152 | tf_op jit(solution)/shard_map/attend_forward_own/pallas_call | solution.py:630
  36.3 3.6 %attend_forward_other.1 = (bf16[32,48,128]{2,1,0:T(8,128)(2,1)S(1)}, bf16[1024,128]{1,0:T(8,128)(2,1)S(1)}) custom-call(s32[1]{0:T(128)} %bitcast.8.refs_0_, bf16[32,128,128]{2,1,0:T(8,128)(2,1)S(1)} %received.1.refs_0_.refs_1_, bf16[32,128,128]{2,1,0:T(8,128)(2,1)S(1)} %collective-permute-done.2.refs_2_.refs_0_, f32[1024,128]{1,0:T(8,128)S(1)} %get-tuple-element.25.refs_3_, ...), custom_call_target="tpu_custom_call" | custom-call | flops 1073741824 | bytes 2097152 | tf_op jit(solution)/shard_map/attend_forward_other/pallas_call | solution.py:641
  39.9 13.9 %all_to_all.20.refs_1_ = bf16[32,48,128]{2,1,0:T(8,128)(2,1)S(1)} all-to-all(bf16[32,48,128]{2,1,0:T(8,128)(2,1)S(1)} %get-tuple-element.28), channel_id=1, replica_groups=mesh['section'=16,'tm'=32] {'tm'}, dimensions={0} | all-to-all | bytes 786432 | tf_op jit(solution)/shard_map/all_to_all | solution.py:567
  53.9 5.1 %conv_block.1 = (bf16[32,32,128]{2,1,0:T(8,128)(2,1)S(1)}, bf16[128,768]{1,0:T(8,128)(2,1)S(1)}, bf16[128,768]{1,0:T(8,128)(2,1)}) custom-call(s32[1]{0:T(128)} %bitcast.8.refs_0_, bf16[32,48,128]{2,1,0:T(8,128)(2,1)S(1)} %all_to_all.20.refs_1_, bf16[128,768]{1,0:T(8,128)(2,1)S(1)} %bitcast.21, bf16[128,768]{1,0:T(8,128)(2,1)S(1)} %bitcast.24, ...), custom_call_target="tpu_custom_call" | custom-call | flops 10000000 | bytes 2097152 | tf_op jit(solution)/shard_map/conv_block/pallas_call | solution.py:654
  59.0 12.5 %all_to_all.21.refs_2_.refs_1_ = bf16[32,32,128]{2,1,0:T(8,128)(2,1)S(1)} all-to-all(bf16[32,32,128]{2,1,0:T(8,128)(2,1)S(1)} %get-tuple-element.29), channel_id=1, replica_groups=mesh['section'=16,'tm'=32] {'tm'}, dimensions={0} | all-to-all | bytes 524288 | tf_op jit(solution)/shard_map/all_to_all | solution.py:567
  71.4 5.9 %attend_backward_other.1 = (bf16[32,96,128]{2,1,0:T(8,128)(2,1)S(1)}, f32[1024,128]{1,0:T(8,128)S(1)}) custom-call(bf16[32,128,128]{2,1,0:T(8,128)(2,1)S(1)} %collective-permute-done.2.refs_2_.refs_0_, bf16[32,128,128]{2,1,0:T(8,128)(2,1)S(1)} %received.1.refs_0_.refs_1_, bf16[32,32,128]{2,1,0:T(8,128)(2,1)S(1)} %all_to_all.21.refs_2_.refs_1_, ...), custom_call_target="tpu_custom_call" | custom-call | flops 2684354560 | bytes 2097152 | tf_op jit(solution)/shard_map/attend_backward_other/pallas_call | solution.py:686
  77.3 2.4 %collective-permute-start.3 = (bf16[32,96,128]{2,1,0:T(8,128)(2,1)S(1)}, bf16[32,96,128]{2,1,0:T(8,128)(2,1)S(1)}, u32[]{:S(2)}, u32[]{:S(2)}) collective-permute-start(bf16[32,96,128]{2,1,0:T(8,128)(2,1)S(1)} %get-tuple-element.33), channel_id=1, source_target_pairs={{0,1},{1,0},{2,3},{3,2},{4,5},{5,4},{6,7},{7,6},{8,9},{9,8},{10,11... | collective-permute-start | bytes 2359304 | tf_op jit(solution)/shard_map/ppermute | solution.py:696
  79.7 5.8 %attend_backward_own.1 = (bf16[32,96,128]{2,1,0:T(8,128)(2,1)S(1)}, bf16[32,32,128]{2,1,0:T(8,128)(2,1)S(1)}) custom-call(bf16[32,128,128]{2,1,0:T(8,128)(2,1)S(1)} %received.1.refs_0_.refs_1_, bf16[32,32,128]{2,1,0:T(8,128)(2,1)S(1)} %all_to_all.21.refs_2_.refs_1_, bf16[1024,128]{1,0:T(8,128)(2,1)S(1)} %get-tuple-element.30.refs_3_.refs_2_, ...), custom_call_target="tpu_custom_call" | custom-call | flops 2684354560 | bytes 2097152 | tf_op jit(solution)/shard_map/attend_backward_own/pallas_call | solution.py:697
  85.6 1.2 %join_grads.1 = bf16[32,128,128]{2,1,0:T(8,128)(2,1)} custom-call(bf16[32,96,128]{2,1,0:T(8,128)(2,1)S(1)} %get-tuple-element.32.part_ref, bf16[32,96,128]{2,1,0:T(8,128)(2,1)S(1)} %collective-permute-done.3.other_ref, bf16[32,32,128]{2,1,0:T(8,128)(2,1)S(1)} %get-tuple-element.34.piece_ref), custom_call_target="tpu_custom_call" | custom-call | flops 1000000 | bytes 2097152 | tf_op jit(solution)/shard_map/join_grads/pallas_call | solution.py:708
  86.7 3.9 %all-to-all-start.3 = ((bf16[32,128,128]{2,1,0:T(8,128)(2,1)}), bf16[32,128,128]{2,1,0:T(8,128)(2,1)S(1)}, u32[]{:S(2)}, u32[]{:S(2)}) async-start(bf16[32,128,128]{2,1,0:T(8,128)(2,1)} %join_grads.1), calls=%async_computation.3 | async-start | bytes 2097152 | tf_op jit(solution)/shard_map/all_to_all | solution.py:567
  90.6 1.9 %collective-permute-start.4 = (bf16[128,768]{1,0:T(8,128)(2,1)S(1)}, bf16[128,768]{1,0:T(8,128)(2,1)S(1)}, u32[]{:S(2)}, u32[]{:S(2)}) collective-permute-start(bf16[128,768]{1,0:T(8,128)(2,1)S(1)} %get-tuple-element.35), channel_id=1, source_target_pairs={{0,32},{32,64},{64,96},{96,128},{128,160},{160,192},{192,224},{224... | collective-permute-start | bytes 589832 | tf_op jit(solution)/shard_map/ppermute | solution.py:673
  92.5 12.3 %collective-permute-done.4.refs_1_ = bf16[128,768]{1,0:T(8,128)(2,1)S(1)} collective-permute-done((bf16[128,768]{1,0:T(8,128)(2,1)S(1)}, bf16[128,768]{1,0:T(8,128)(2,1)S(1)}, u32[]{:S(2)}, u32[]{:S(2)}) %collective-permute-start.4) | collective-permute-done | bytes 196640 | tf_op jit(solution)/shard_map/ppermute | solution.py:673
  104.8 3.1 %all-to-all-done.3.refs_0_ = bf16[32,128,128]{2,1,0:T(8,128)(2,1)S(1)} async-done(((bf16[32,128,128]{2,1,0:T(8,128)(2,1)}), bf16[32,128,128]{2,1,0:T(8,128)(2,1)S(1)}, u32[]{:S(2)}, u32[]{:S(2)}) %all-to-all-start.3) | async-done | bytes 1048608 | tf_op jit(solution)/shard_map/all_to_all | solution.py:567
  107.9 1.3 %unpack_grads.1 = (bf16[128,768]{1,0:T(8,128)(2,1)}, bf16[128,768]{1,0:T(8,128)(2,1)}, bf16[128,768]{1,0:T(8,128)(2,1)}, f32[1,768]{1,0:T(1,128)}, f32[31,1,768]{2,1,0:T(1,128)}, /*index=5*/bf16[128,768]{1,0:T(8,128)(2,1)}) custom-call(bf16[32,128,128]{2,1,0:T(8,128)(2,1)S(1)} %all-to-all-done.3.refs_0_, bf16[128,768]{1,0:T(8,128)(2,1)S(1)} %collective-permute-done.4.refs_1_), custom_call_target="tpu_custom_call" | custom-call | flops 1000000 | bytes 2097152 | tf_op jit(solution)/shard_map/unpack_grads/pallas_call | solution.py:720
  (13 shorter events, 0.1 us)
Async XLA Ops:
  3.0 10.6 %copy-start.2 = (bf16[1,128,768]{2,1,0:T(8,128)(2,1)S(1)}, bf16[1,128,768]{2,1,0:T(8,128)(2,1)}, u32[]{:S(2)}) copy-start(bf16[1,128,768]{2,1,0:T(8,128)(2,1)} %param.13) | copy-start | bytes 589828
  3.1 10.6 %copy-start = (bf16[1,128,768]{2,1,0:T(8,128)(2,1)S(1)}, bf16[1,128,768]{2,1,0:T(8,128)(2,1)}, u32[]{:S(2)}) copy-start(bf16[1,128,768]{2,1,0:T(8,128)(2,1)} %param.7) | copy-start | bytes 589828
  3.1 27.9 %all-to-all-start = ((bf16[32,128,128]{2,1,0:T(8,128)(2,1)}), bf16[32,128,128]{2,1,0:T(8,128)(2,1)S(1)}, u32[]{:S(2)}, u32[]{:S(2)}) async-start(bf16[32,128,128]{2,1,0:T(8,128)(2,1)} %pack_qkv.1), calls=%async_computation | async-start | bytes 2097152 | tf_op jit(solution)/shard_map/all_to_all | solution.py:567
  13.7 17.2 %copy-start.1 = (f32[1,31,768]{2,0,1:T(1,128)S(1)}, f32[1,31,768]{2,0,1:T(1,128)}, u32[]{:S(2)}) copy-start(f32[1,31,768]{2,0,1:T(1,128)} %param.12) | copy-start | bytes 285700
  13.8 12.6 %collective-permute-start = (bf16[48,768]{1,0:T(8,128)(2,1)S(1)}, bf16[48,768]{1,0:T(8,128)(2,1)S(1)}, u32[]{:S(2)}, u32[]{:S(2)}) collective-permute-start(bf16[48,768]{1,0:T(8,128)(2,1)S(1)} %pad_maximum_fusion), channel_id=1, source_target_pairs={{0,1},{1,2},{2,3},{3,4},{4,5},{5,6},{6,7},{7,8},{8,9},{9,10},{10,1... | collective-permute-start | bytes 221192 | tf_op jit(solution)/shard_map/ppermute | solution.py:589
  17.4 13.5 %copy-start.3 = (f32[1,768]{1,0:T(1,128)S(1)}, f32[1,768]{1,0:T(1,128)}, u32[]{:S(2)}) copy-start(f32[1,768]{1,0:T(1,128)} %refs_6_.1) | copy-start | bytes 9220
  17.5 11.0 %collective-permute-start.1 = (bf16[48,768]{1,0:T(8,128)(2,1)S(1)}, bf16[48,768]{1,0:T(8,128)(2,1)S(1)}, u32[]{:S(2)}, u32[]{:S(2)}) collective-permute-start(bf16[48,768]{1,0:T(8,128)(2,1)S(1)} %pad_maximum_fusion.1), channel_id=1, source_target_pairs={{1,0},{2,1},{3,2},{4,3},{5,4},{6,5},{7,6},{8,7},{9,8},{10,9},{11,1... | collective-permute-start | bytes 221192 | tf_op jit(solution)/shard_map/ppermute | solution.py:592
  31.0 5.4 %collective-permute-start.2 = (bf16[32,128,128]{2,1,0:T(8,128)(2,1)S(1)}, bf16[32,128,128]{2,1,0:T(8,128)(2,1)S(1)}, u32[]{:S(2)}, u32[]{:S(2)}) collective-permute-start(bf16[32,128,128]{2,1,0:T(8,128)(2,1)S(1)} %received.1.refs_0_.refs_1_), channel_id=1, source_target_pairs={{0,1},{1,0},{2,3},{3,2},{4,5},{5,4},{6,7},{7,6},{8,9},{9,8},{10,11... | collective-permute-start | bytes 3145736 | tf_op jit(solution)/shard_map/ppermute | solution.py:622
  77.3 8.2 %collective-permute-start.3 = (bf16[32,96,128]{2,1,0:T(8,128)(2,1)S(1)}, bf16[32,96,128]{2,1,0:T(8,128)(2,1)S(1)}, u32[]{:S(2)}, u32[]{:S(2)}) collective-permute-start(bf16[32,96,128]{2,1,0:T(8,128)(2,1)S(1)} %get-tuple-element.33), channel_id=1, source_target_pairs={{0,1},{1,0},{2,3},{3,2},{4,5},{5,4},{6,7},{7,6},{8,9},{9,8},{10,11... | collective-permute-start | bytes 2359304 | tf_op jit(solution)/shard_map/ppermute | solution.py:696
  86.7 21.1 %all-to-all-start.3 = ((bf16[32,128,128]{2,1,0:T(8,128)(2,1)}), bf16[32,128,128]{2,1,0:T(8,128)(2,1)S(1)}, u32[]{:S(2)}, u32[]{:S(2)}) async-start(bf16[32,128,128]{2,1,0:T(8,128)(2,1)} %join_grads.1), calls=%async_computation.3 | async-start | bytes 2097152 | tf_op jit(solution)/shard_map/all_to_all | solution.py:567
  90.6 14.2 %collective-permute-start.4 = (bf16[128,768]{1,0:T(8,128)(2,1)S(1)}, bf16[128,768]{1,0:T(8,128)(2,1)S(1)}, u32[]{:S(2)}, u32[]{:S(2)}) collective-permute-start(bf16[128,768]{1,0:T(8,128)(2,1)S(1)} %get-tuple-element.35), channel_id=1, source_target_pairs={{0,32},{32,64},{64,96},{96,128},{128,160},{160,192},{192,224},{224... | collective-permute-start | bytes 589832 | tf_op jit(solution)/shard_map/ppermute | solution.py:673

commit v7 on v6

--- a/solution.py
+++ b/solution.py
@@ -24,6 +24,8 @@
 Q_ROWS = slice(96, 128)
 PIECE_ROWS = 128
 HALF = 64
+OWN_FACTOR = range(96, 99)
+OTHER_FACTOR = range(99, 102)
 SUB = 32
 
 VMEM = pl.BlockSpec(memory_space=pltpu.VMEM)
@@ -144,7 +146,7 @@
                 natural[at, :] = block.T
 
 
-def attend(got_ref, half_ref, state, finish, block, chunk, keys, values, scores):
+def attend(got_ref, half_ref, state, finish, block, chunk, kept_ref, keys, values, scores):
     key_count = keys.shape[1]
     per = block // SUB
     blocks = got_ref.shape[0] // per
@@ -187,8 +189,10 @@
             weights = jnp.exp2(scores[step % 2, :, start : start + chunk] * SCALE2 - tops)
             for tile in range(0, chunk, LANES):
                 total = total + weights[:, tile : tile + LANES]
+            weights = weights.astype(BF16)
+            kept_ref[at, start : start + chunk] = weights
             result = result + jnp.dot(
-                weights.astype(BF16), values[start : start + chunk, :], preferred_element_type=F32
+                weights, values[start : start + chunk, :], preferred_element_type=F32
             )
         finish(at, top, total, result)
 
@@ -200,6 +204,7 @@
     top_ref,
     total_ref,
     result_ref,
+    kept_ref,
     keys,
     values,
     scores,
@@ -209,7 +214,7 @@
         total_ref[at, :] = total
         result_ref[at, :] = result
 
-    attend(got_ref, got_ref, None, finish, block, chunk, keys, values, scores)
+    attend(got_ref, got_ref, None, finish, block, chunk, kept_ref, keys, values, scores)
 
 
 def forward_second_kernel(
@@ -224,23 +229,27 @@
     result_ref,
     send_ref,
     out_ref,
+    kept_ref,
     keys,
     values,
     scores,
 ):
     def finish(at, top, total, result):
         total = jnp.sum(total, axis=1, keepdims=True)
-        rest = top + jnp.log2(total)
         merged = result / total
         lane = lanes_of(block)
-        for spot in range(HEAD_DIM, HEAD_DIM + 3):
-            part = rest.astype(BF16).astype(F32)
-            merged = jnp.where(lane == spot, part, merged)
-            rest = rest - part
+        for spots, rest in (
+            (OWN_FACTOR, jnp.exp2(top_ref[at, :] - top) / total),
+            (OTHER_FACTOR, jnp.broadcast_to(1.0 / total, (block, LANES))),
+        ):
+            for spot in spots:
+                part = rest.astype(BF16).astype(F32)
+                merged = jnp.where(lane == spot, part, merged)
+                rest = rest - part
         out_ref[at, :] = merged.astype(BF16)
 
     state = (top_ref, total_ref, result_ref)
-    attend(got_ref, swapped_ref, state, finish, block, chunk, keys, values, scores)
+    attend(got_ref, swapped_ref, state, finish, block, chunk, kept_ref, keys, values, scores)
     count = got_ref.shape[0]
     side = jnp.where(place_ref[0] % groups == groups - 1, -1, 1)
     lane = lanes_of(48)
@@ -396,6 +405,8 @@
 
 
 def backward(
+    factor_lanes,
+    kept_ref,
     half_ref,
     got_ref,
     grads_ref,
@@ -404,13 +415,12 @@
     finish,
     block,
     chunk,
-    keys_t,
     values_t,
     keys,
     grad_keys,
     grad_values,
 ):
-    fill_half(half_ref, 0, chunk, keys_t, values_t, keys, None)
+    fill_half(half_ref, 0, chunk, None, values_t, keys, None)
     key_count = keys.shape[0]
     steps = got_ref.shape[0] * SUB // block
     lane_part = lanes_of(HEAD_DIM)
@@ -421,28 +431,24 @@
         at = slice(step * block, (step + 1) * block)
         rows = got_ref[sources, Q_ROWS, :].reshape(block, LANES)
         grads = grads_ref[sources].reshape(block, LANES).astype(F32)
-        grads = jnp.where(lane < HEAD_DIM, grads, 0.0)
         out = out_ref[at, :].astype(F32)
-        delta = jnp.sum(grads * out, axis=1, keepdims=True)
-        in_log = (lane >= HEAD_DIM) & (lane < HEAD_DIM + 3)
-        logs = jnp.sum(jnp.where(in_log, out, 0.0), axis=1, keepdims=True)
-        grads = grads.astype(BF16)
+        in_factor = (lane >= factor_lanes.start) & (lane < factor_lanes.stop)
+        factor = jnp.sum(jnp.where(in_factor, out, 0.0), axis=1, keepdims=True)
+        grads = jnp.where(lane < HEAD_DIM, grads * factor, 0.0).astype(BF16)
+        delta = jnp.sum(grads.astype(F32) * out, axis=1, keepdims=True)
         rows_t = rows.T[0:HEAD_DIM]
         grads_t = grads.T[0:HEAD_DIM]
         result = jnp.zeros((block, LANES), F32)
         for start in range(0, key_count, chunk):
             part = slice(start, start + chunk)
             if step == 0 and start + chunk < key_count:
-                fill_half(
-                    half_ref, start + chunk, start + 2 * chunk, keys_t, values_t, keys, None
-                )
-            logits = jnp.dot(rows, keys_t[:, part], preferred_element_type=F32)
-            probs = jnp.exp2(logits * SCALE2 - logs)
+                fill_half(half_ref, start + chunk, start + 2 * chunk, None, values_t, keys, None)
+            weights = kept_ref[at, part]
             grad_probs = jnp.dot(grads, values_t[:, part], preferred_element_type=F32)
-            grad_scores = (probs * (grad_probs - delta)).astype(BF16)
+            grad_scores = (weights.astype(F32) * (grad_probs - delta)).astype(BF16)
             result = result + jnp.dot(grad_scores, keys[part, :], preferred_element_type=F32)
             grad_k = jnp.dot(rows_t, grad_scores, preferred_element_type=F32)
-            grad_v = jnp.dot(grads_t, probs.astype(BF16), preferred_element_type=F32)
+            grad_v = jnp.dot(grads_t, weights, preferred_element_type=F32)
             if step > 0:
                 grad_k = grad_k + grad_keys[:, part]
                 grad_v = grad_v + grad_values[:, part]
@@ -466,6 +472,7 @@
 def backward_first_kernel(
     block,
     chunk,
+    kept_ref,
     swapped_ref,
     got_ref,
     grads_ref,
@@ -477,14 +484,14 @@
     def finish(step, sources, at, result):
         grad_q_ref[at, :] = result
 
-    backward(
-        swapped_ref, got_ref, grads_ref, out_ref, part_ref, finish, block, chunk, *scratch
-    )
+    given = (kept_ref, swapped_ref, got_ref, grads_ref, out_ref)
+    backward(OTHER_FACTOR, *given, part_ref, finish, block, chunk, *scratch)
 
 
 def backward_second_kernel(
     block,
     chunk,
+    kept_ref,
     got_ref,
     grads_ref,
     out_ref,
@@ -502,9 +509,8 @@
         lane = lax.broadcasted_iota(jnp.int32, result.shape, 2)
         piece_ref[sources] = jnp.where(lane < HEAD_DIM, result, sums[None]).astype(BF16)
 
-    backward(
-        got_ref, got_ref, grads_ref, out_ref, part_ref, finish, block, chunk, *scratch
-    )
+    given = (kept_ref, got_ref, got_ref, grads_ref, out_ref)
+    backward(OWN_FACTOR, *given, part_ref, finish, block, chunk, *scratch)
 
 
 def join_kernel(part_ref, other_ref, piece_ref, send_ref):
@@ -595,6 +601,7 @@
     pieces = shape((count, PIECE_ROWS, LANES), BF16)
     rows_shape = shape((frames, CH), BF16)
     own_shape = shape((own, LANES), F32)
+    kept_shape = shape((own, half), BF16)
     sent = call(
         lambda *refs: pack_kernel(groups, *refs),
         pieces,
@@ -627,22 +634,22 @@
         pltpu.VMEM((half, LANES), BF16),
         pltpu.VMEM((2, block, half), F32),
     ]
-    state = call(
+    *state, own_kept = call(
         lambda *refs: forward_first_kernel(block, chunk, *refs),
-        (own_shape,) * 3,
+        (own_shape,) * 3 + (kept_shape,),
         [VMEM],
-        (VMEM,) * 3,
+        (VMEM,) * 4,
         attend_scratch,
         24,
         2 * matmul,
         "attend_forward_own",
         own * half,
     )(got)
-    results, head_out = call(
+    results, head_out, other_kept = call(
         lambda *refs: forward_second_kernel(block, chunk, groups, *refs),
-        (shape((count, 48, LANES), BF16), shape((own, LANES), BF16)),
+        (shape((count, 48, LANES), BF16), shape((own, LANES), BF16), kept_shape),
         [SMEM] + [VMEM] * 5,
-        (VMEM,) * 2,
+        (VMEM,) * 3,
         attend_scratch,
         24,
         2 * matmul,
@@ -677,7 +684,6 @@
     block, chunk = 512, 512
     backward_scratch = [
         pltpu.VMEM((LANES, half), BF16),
-        pltpu.VMEM((LANES, half), BF16),
         pltpu.VMEM((half, LANES), BF16),
         pltpu.VMEM((HEAD_DIM, half), F32),
         pltpu.VMEM((HEAD_DIM, half), F32),
@@ -686,25 +692,24 @@
     other_part, grad_q = call(
         lambda *refs: backward_first_kernel(block, chunk, *refs),
         (part_shape, own_shape),
-        [VMEM] * 4,
+        [VMEM] * 5,
         (VMEM,) * 2,
         backward_scratch,
         24,
-        5 * matmul,
+        4 * matmul,
         "attend_backward_other",
-    )(swapped, got, grads_got, head_out)
+    )(other_kept, swapped, got, grads_got, head_out)
     arrived_part = lax.ppermute(other_part, "tm", partner)
     own_part, grad_q_pieces = call(
         lambda *refs: backward_second_kernel(block, chunk, *refs),
         (part_shape, shape((count, SUB, LANES), BF16)),
-        [VMEM] * 4,
+        [VMEM] * 5,
         (VMEM,) * 2,
         backward_scratch,
         24,
-        5 * matmul,
+        4 * matmul,
         "attend_backward_own",
-        own * half,
-    )(got, grads_got, head_out, grad_q)
+    )(own_kept, got, grads_got, head_out, grad_q)
     grads_out = call(
         join_kernel,
         pieces,

time: 110 us -> 108 us (0.982)
  Pallas kernels: 28.4 us -> 26.4 us
  local copies, waits for them, and re-layouts: 0.04 us -> 1.61 us
  waiting for transfers between devices: 26.9 us -> 25.5 us
    ppermute x1, waiting for transfers between devices: 6.91 us -> 5.53 us  [local(): lax.ppermute(jnp.concatenate([resid[frames - SUB:], cotangent[frames - ed...]
    pallas_call x1, Pallas kernels: 5.87 us -> 4.63 us  [local(): call(lambda *refs: backward_first_kernel(block, chunk, *refs), (part_shap...]
    pallas_call x1, Pallas kernels: 5.84 us -> 4.63 us  [local(): call(lambda *refs: backward_second_kernel(block, chunk, *refs), (part_sha...]
  transfers between devices with their start and end apart: 7 -> 7, of which waited for: 5 -> 5; matrix products, arithmetic and copies ran while one was open for 0% -> 1% of each run, Pallas kernels for 8% -> 7%
where the time goes in v7:
time: 108 us; the launch traced here: 107 us
  Pallas kernels  26.4 us (24%)
  starting transfers between devices  26.4 us (24%)
  blocking collectives  26.4 us (24%)
  waiting for transfers between devices  25.5 us (24%)
  local copies, waits for them, and re-layouts  1.61 us (1%)
    all_to_all x2, blocking collectives, exchange(): return lax.all_to_all(pieces, 'tm', split_axis=0, concat_axis=0, tiled=True)  26.4 us
    all_to_all x2, starting transfers between devices, exchange(): return lax.all_to_all(pieces, 'tm', split_axis=0, concat_axis=0, tiled=True)  14.3 us
    ppermute x1, waiting for transfers between devices, local(): lax.ppermute(block_out, 'section', [(i, (i + 1) % sections) for i in rang...  12.3 us
    all_to_all x2, waiting for transfers between devices, exchange(): return lax.all_to_all(pieces, 'tm', split_axis=0, concat_axis=0, tiled=True)  5.61 us
    ppermute x1, waiting for transfers between devices, local(): lax.ppermute(jnp.concatenate([resid[frames - SUB:], cotangent[frames - ed...  5.53 us
    pallas_call x1, Pallas kernels, local(): call(lambda *refs: conv_kernel(groups, count, *refs), (shape((count, SUB,...  5.16 us
    pallas_call x1, Pallas kernels, local(): call(lambda *refs: backward_first_kernel(block, chunk, *refs), (part_shap...  4.63 us
    pallas_call x1, Pallas kernels, local(): call(lambda *refs: backward_second_kernel(block, chunk, *refs), (part_sha...  4.63 us
  transfers between devices with their start and end apart: 7, of which 5 were waited for; matrix products, arithmetic and copies ran while one was open for 1% of the time, Pallas kernels for 7%

profile of v7, /device:TPU:1, one launch (start us, length us, event | category | flops | bytes accessed | tf_op | source)
XLA Modules:
  0.0 107.2 jit_solution(9931389456128302424)
XLA Ops:
  0.7 2.4 %pack_qkv.1 = bf16[32,128,128]{2,1,0:T(8,128)(2,1)} custom-call(bf16[128,768]{1,0:T(8,128)(2,1)} %bitcast.25, bf16[128,768]{1,0:T(8,128)(2,1)} %bitcast.26, bf16[128,768]{1,0:T(8,128)(2,1)} %bitcast.27), custom_call_target="tpu_custom_call" | custom-call | flops 1000000 | bytes 2097152 | tf_op jit(solution)/shard_map/pack_qkv/pallas_call | solution.py:605
  3.1 10.5 %all-to-all-start = ((bf16[32,128,128]{2,1,0:T(8,128)(2,1)}), bf16[32,128,128]{2,1,0:T(8,128)(2,1)S(1)}, u32[]{:S(2)}, u32[]{:S(2)}) async-start(bf16[32,128,128]{2,1,0:T(8,128)(2,1)} %pack_qkv.1), calls=%async_computation | async-start | bytes 2097152 | tf_op jit(solution)/shard_map/all_to_all | solution.py:573
  13.6 0.8 slice_bitcast_fusion.2
  14.3 0.8 slice_bitcast_fusion
  15.2 3.5 %collective-permute-start = (bf16[48,768]{1,0:T(8,128)(2,1)S(1)}, bf16[48,768]{1,0:T(8,128)(2,1)S(1)}, u32[]{:S(2)}, u32[]{:S(2)}) collective-permute-start(bf16[48,768]{1,0:T(8,128)(2,1)S(1)} %pad_maximum_fusion), channel_id=1, source_target_pairs={{0,1},{1,2},{2,3},{3,4},{4,5},{5,6},{6,7},{7,8},{8,9},{9,10},{10,1... | collective-permute-start | bytes 221192 | tf_op jit(solution)/shard_map/ppermute | solution.py:595
  18.8 1.9 %collective-permute-start.1 = (bf16[48,768]{1,0:T(8,128)(2,1)S(1)}, bf16[48,768]{1,0:T(8,128)(2,1)S(1)}, u32[]{:S(2)}, u32[]{:S(2)}) collective-permute-start(bf16[48,768]{1,0:T(8,128)(2,1)S(1)} %pad_maximum_fusion.1), channel_id=1, source_target_pairs={{1,0},{2,1},{3,2},{4,3},{5,4},{6,5},{7,6},{8,7},{9,8},{10,9},{11,1... | collective-permute-start | bytes 221192 | tf_op jit(solution)/shard_map/ppermute | solution.py:598
  20.7 5.5 %collective-permute-done.refs_1_.refs_4_ = bf16[48,768]{1,0:T(8,128)(2,1)S(1)} collective-permute-done((bf16[48,768]{1,0:T(8,128)(2,1)S(1)}, bf16[48,768]{1,0:T(8,128)(2,1)S(1)}, u32[]{:S(2)}, u32[]{:S(2)}) %collective-permute-start) | collective-permute-done | bytes 73760 | tf_op jit(solution)/shard_map/ppermute | solution.py:595
  26.2 2.1 %collective-permute-done.1.refs_2_.refs_5_ = bf16[48,768]{1,0:T(8,128)(2,1)S(1)} collective-permute-done((bf16[48,768]{1,0:T(8,128)(2,1)S(1)}, bf16[48,768]{1,0:T(8,128)(2,1)S(1)}, u32[]{:S(2)}, u32[]{:S(2)}) %collective-permute-start.1) | collective-permute-done | bytes 73760 | tf_op jit(solution)/shard_map/ppermute | solution.py:598
  28.3 2.5 %all-to-all-done.refs_0_ = bf16[32,128,128]{2,1,0:T(8,128)(2,1)S(1)} async-done(((bf16[32,128,128]{2,1,0:T(8,128)(2,1)}), bf16[32,128,128]{2,1,0:T(8,128)(2,1)S(1)}, u32[]{:S(2)}, u32[]{:S(2)}) %all-to-all-start) | async-done | bytes 1048608 | tf_op jit(solution)/shard_map/all_to_all | solution.py:573
  30.9 2.3 %collective-permute-start.2 = (bf16[32,128,128]{2,1,0:T(8,128)(2,1)S(1)}, bf16[32,128,128]{2,1,0:T(8,128)(2,1)S(1)}, u32[]{:S(2)}, u32[]{:S(2)}) collective-permute-start(bf16[32,128,128]{2,1,0:T(8,128)(2,1)S(1)} %received.1.refs_0_.refs_1_.refs_2_), channel_id=1, source_target_pairs={{0,1},{1,0},{2,3},{3,2},{4,5},{5,4},{6,7},{7,6},{8,9},{9,8},{10,11... | collective-permute-start | bytes 3145736 | tf_op jit(solution)/shard_map/ppermute | solution.py:629
  33.2 3.2 %attend_forward_own.1 = (f32[1024,128]{1,0:T(8,128)S(1)}, f32[1024,128]{1,0:T(8,128)S(1)}, f32[1024,128]{1,0:T(8,128)S(1)}, bf16[1024,2048]{1,0:T(8,128)(2,1)S(1)}) custom-call(bf16[32,128,128]{2,1,0:T(8,128)(2,1)S(1)} %received.1.refs_0_.refs_1_.refs_2_), custom_call_target="tpu_custom_call" | custom-call | flops 1073741824 | bytes 2097152 | tf_op jit(solution)/shard_map/attend_forward_own/pallas_call | solution.py:637
  36.4 3.9 %attend_forward_other.1 = (bf16[32,48,128]{2,1,0:T(8,128)(2,1)S(1)}, bf16[1024,128]{1,0:T(8,128)(2,1)S(1)}, bf16[1024,2048]{1,0:T(8,128)(2,1)S(1)}) custom-call(s32[1]{0:T(128)} %bitcast.8.refs_0_, bf16[32,128,128]{2,1,0:T(8,128)(2,1)S(1)} %received.1.refs_0_.refs_1_.refs_2_, bf16[32,128,128]{2,1,0:T(8,128)(2,1)S(1)} %collective-permute-done.2.refs_2_.refs_1_, ...), custom_call_target="tpu_custom_call" | custom-call | flops 1073741824 | bytes 2097152 | tf_op jit(solution)/shard_map/attend_forward_other/pallas_call | solution.py:648
  40.3 13.9 %all_to_all.20.refs_1_ = bf16[32,48,128]{2,1,0:T(8,128)(2,1)S(1)} all-to-all(bf16[32,48,128]{2,1,0:T(8,128)(2,1)S(1)} %get-tuple-element.31), channel_id=1, replica_groups=mesh['section'=16,'tm'=32] {'tm'}, dimensions={0} | all-to-all | bytes 786432 | tf_op jit(solution)/shard_map/all_to_all | solution.py:573
  54.3 5.2 %conv_block.1 = (bf16[32,32,128]{2,1,0:T(8,128)(2,1)S(1)}, bf16[128,768]{1,0:T(8,128)(2,1)S(1)}, bf16[128,768]{1,0:T(8,128)(2,1)}) custom-call(s32[1]{0:T(128)} %bitcast.8.refs_0_, bf16[32,48,128]{2,1,0:T(8,128)(2,1)S(1)} %all_to_all.20.refs_1_, bf16[128,768]{1,0:T(8,128)(2,1)S(1)} %bitcast.21, bf16[128,768]{1,0:T(8,128)(2,1)S(1)} %bitcast.24, ...), custom_call_target="tpu_custom_call" | custom-call | flops 10000000 | bytes 2097152 | tf_op jit(solution)/shard_map/conv_block/pallas_call | solution.py:661
  59.4 12.5 %all_to_all.21.refs_3_.refs_2_ = bf16[32,32,128]{2,1,0:T(8,128)(2,1)S(1)} all-to-all(bf16[32,32,128]{2,1,0:T(8,128)(2,1)S(1)} %get-tuple-element.32), channel_id=1, replica_groups=mesh['section'=16,'tm'=32] {'tm'}, dimensions={0} | all-to-all | bytes 524288 | tf_op jit(solution)/shard_map/all_to_all | solution.py:573
  71.9 4.6 %attend_backward_other.1 = (bf16[32,96,128]{2,1,0:T(8,128)(2,1)S(1)}, f32[1024,128]{1,0:T(8,128)S(1)}) custom-call(bf16[1024,2048]{1,0:T(8,128)(2,1)S(1)} %get-tuple-element.34.refs_0_, bf16[32,128,128]{2,1,0:T(8,128)(2,1)S(1)} %collective-permute-done.2.refs_2_.refs_1_, bf16[32,128,128]{2,1,0:T(8,128)(2,1)S(1)} %received.1.refs_0_.refs_1_.refs_2_, ...), custom_call_target="tpu_custom_call" | custom-call | flops 2147483648 | bytes 2097152 | tf_op jit(solution)/shard_map/attend_backward_other/pallas_call | solution.py:692
  76.5 2.4 %collective-permute-start.3 = (bf16[32,96,128]{2,1,0:T(8,128)(2,1)S(1)}, bf16[32,96,128]{2,1,0:T(8,128)(2,1)S(1)}, u32[]{:S(2)}, u32[]{:S(2)}) collective-permute-start(bf16[32,96,128]{2,1,0:T(8,128)(2,1)S(1)} %get-tuple-element.37), channel_id=1, source_target_pairs={{0,1},{1,0},{2,3},{3,2},{4,5},{5,4},{6,7},{7,6},{8,9},{9,8},{10,11... | collective-permute-start | bytes 2359304 | tf_op jit(solution)/shard_map/ppermute | solution.py:702
  78.9 4.6 %attend_backward_own.1 = (bf16[32,96,128]{2,1,0:T(8,128)(2,1)S(1)}, bf16[32,32,128]{2,1,0:T(8,128)(2,1)S(1)}) custom-call(bf16[1024,2048]{1,0:T(8,128)(2,1)S(1)} %get-tuple-element.27.refs_0_, bf16[32,128,128]{2,1,0:T(8,128)(2,1)S(1)} %received.1.refs_0_.refs_1_.refs_2_, bf16[32,32,128]{2,1,0:T(8,128)(2,1)S(1)} %all_to_all.21.refs_3_.refs_2_, ...), custom_call_target="tpu_custom_call" | custom-call | flops 2147483648 | bytes 2097152 | tf_op jit(solution)/shard_map/attend_backward_own/pallas_call | solution.py:703
  83.5 1.2 %join_grads.1 = bf16[32,128,128]{2,1,0:T(8,128)(2,1)} custom-call(bf16[32,96,128]{2,1,0:T(8,128)(2,1)S(1)} %get-tuple-element.36.part_ref, bf16[32,96,128]{2,1,0:T(8,128)(2,1)S(1)} %collective-permute-done.3.other_ref, bf16[32,32,128]{2,1,0:T(8,128)(2,1)S(1)} %get-tuple-element.38.piece_ref), custom_call_target="tpu_custom_call" | custom-call | flops 1000000 | bytes 2097152 | tf_op jit(solution)/shard_map/join_grads/pallas_call | solution.py:713
  84.7 3.9 %all-to-all-start.3 = ((bf16[32,128,128]{2,1,0:T(8,128)(2,1)}), bf16[32,128,128]{2,1,0:T(8,128)(2,1)S(1)}, u32[]{:S(2)}, u32[]{:S(2)}) async-start(bf16[32,128,128]{2,1,0:T(8,128)(2,1)} %join_grads.1), calls=%async_computation.3 | async-start | bytes 2097152 | tf_op jit(solution)/shard_map/all_to_all | solution.py:573
  88.6 1.9 %collective-permute-start.4 = (bf16[128,768]{1,0:T(8,128)(2,1)S(1)}, bf16[128,768]{1,0:T(8,128)(2,1)S(1)}, u32[]{:S(2)}, u32[]{:S(2)}) collective-permute-start(bf16[128,768]{1,0:T(8,128)(2,1)S(1)} %get-tuple-element.39), channel_id=1, source_target_pairs={{0,32},{32,64},{64,96},{96,128},{128,160},{160,192},{192,224},{224... | collective-permute-start | bytes 589832 | tf_op jit(solution)/shard_map/ppermute | solution.py:680
  90.5 12.3 %collective-permute-done.4.refs_1_ = bf16[128,768]{1,0:T(8,128)(2,1)S(1)} collective-permute-done((bf16[128,768]{1,0:T(8,128)(2,1)S(1)}, bf16[128,768]{1,0:T(8,128)(2,1)S(1)}, u32[]{:S(2)}, u32[]{:S(2)}) %collective-permute-start.4) | collective-permute-done | bytes 196640 | tf_op jit(solution)/shard_map/ppermute | solution.py:680
  102.8 3.1 %all-to-all-done.3.refs_0_ = bf16[32,128,128]{2,1,0:T(8,128)(2,1)S(1)} async-done(((bf16[32,128,128]{2,1,0:T(8,128)(2,1)}), bf16[32,128,128]{2,1,0:T(8,128)(2,1)S(1)}, u32[]{:S(2)}, u32[]{:S(2)}) %all-to-all-start.3) | async-done | bytes 1048608 | tf_op jit(solution)/shard_map/all_to_all | solution.py:573
  105.9 1.3 %unpack_grads.1 = (bf16[128,768]{1,0:T(8,128)(2,1)}, bf16[128,768]{1,0:T(8,128)(2,1)}, bf16[128,768]{1,0:T(8,128)(2,1)}, f32[1,768]{1,0:T(1,128)}, f32[31,1,768]{2,1,0:T(1,128)}, /*index=5*/bf16[128,768]{1,0:T(8,128)(2,1)}) custom-call(bf16[32,128,128]{2,1,0:T(8,128)(2,1)S(1)} %all-to-all-done.3.refs_0_, bf16[128,768]{1,0:T(8,128)(2,1)S(1)} %collective-permute-done.4.refs_1_), custom_call_target="tpu_custom_call" | custom-call | flops 1000000 | bytes 2097152 | tf_op jit(solution)/shard_map/unpack_grads/pallas_call | solution.py:725
  (13 shorter events, 0.0 us)
Async XLA Ops:
  0.6 30.2 %copy-start.3 = (f32[1,768]{1,0:T(1,128)S(1)}, f32[1,768]{1,0:T(1,128)}, u32[]{:S(2)}) copy-start(f32[1,768]{1,0:T(1,128)} %refs_6_.1) | copy-start | bytes 9220
  0.6 30.2 %copy-start.1 = (f32[1,31,768]{2,0,1:T(1,128)S(1)}, f32[1,31,768]{2,0,1:T(1,128)}, u32[]{:S(2)}) copy-start(f32[1,31,768]{2,0,1:T(1,128)} %param.12) | copy-start | bytes 285700
  3.1 27.8 %all-to-all-start = ((bf16[32,128,128]{2,1,0:T(8,128)(2,1)}), bf16[32,128,128]{2,1,0:T(8,128)(2,1)S(1)}, u32[]{:S(2)}, u32[]{:S(2)}) async-start(bf16[32,128,128]{2,1,0:T(8,128)(2,1)} %pack_qkv.1), calls=%async_computation | async-start | bytes 2097152 | tf_op jit(solution)/shard_map/all_to_all | solution.py:573
  15.2 11.0 %collective-permute-start = (bf16[48,768]{1,0:T(8,128)(2,1)S(1)}, bf16[48,768]{1,0:T(8,128)(2,1)S(1)}, u32[]{:S(2)}, u32[]{:S(2)}) collective-permute-start(bf16[48,768]{1,0:T(8,128)(2,1)S(1)} %pad_maximum_fusion), channel_id=1, source_target_pairs={{0,1},{1,2},{2,3},{3,4},{4,5},{5,6},{6,7},{7,8},{8,9},{9,10},{10,1... | collective-permute-start | bytes 221192 | tf_op jit(solution)/shard_map/ppermute | solution.py:595
  18.8 9.6 %collective-permute-start.1 = (bf16[48,768]{1,0:T(8,128)(2,1)S(1)}, bf16[48,768]{1,0:T(8,128)(2,1)S(1)}, u32[]{:S(2)}, u32[]{:S(2)}) collective-permute-start(bf16[48,768]{1,0:T(8,128)(2,1)S(1)} %pad_maximum_fusion.1), channel_id=1, source_target_pairs={{1,0},{2,1},{3,2},{4,3},{5,4},{6,5},{7,6},{8,7},{9,8},{10,9},{11,1... | collective-permute-start | bytes 221192 | tf_op jit(solution)/shard_map/ppermute | solution.py:598
  30.9 5.5 %collective-permute-start.2 = (bf16[32,128,128]{2,1,0:T(8,128)(2,1)S(1)}, bf16[32,128,128]{2,1,0:T(8,128)(2,1)S(1)}, u32[]{:S(2)}, u32[]{:S(2)}) collective-permute-start(bf16[32,128,128]{2,1,0:T(8,128)(2,1)S(1)} %received.1.refs_0_.refs_1_.refs_2_), channel_id=1, source_target_pairs={{0,1},{1,0},{2,3},{3,2},{4,5},{5,4},{6,7},{7,6},{8,9},{9,8},{10,11... | collective-permute-start | bytes 3145736 | tf_op jit(solution)/shard_map/ppermute | solution.py:629
  33.2 21.1 %copy-start = (bf16[1,128,768]{2,1,0:T(8,128)(2,1)S(1)}, bf16[1,128,768]{2,1,0:T(8,128)(2,1)}, u32[]{:S(2)}) copy-start(bf16[1,128,768]{2,1,0:T(8,128)(2,1)} %param.7) | copy-start | bytes 589828
  33.2 21.1 %copy-start.2 = (bf16[1,128,768]{2,1,0:T(8,128)(2,1)S(1)}, bf16[1,128,768]{2,1,0:T(8,128)(2,1)}, u32[]{:S(2)}) copy-start(bf16[1,128,768]{2,1,0:T(8,128)(2,1)} %param.13) | copy-start | bytes 589828
  76.5 7.0 %collective-permute-start.3 = (bf16[32,96,128]{2,1,0:T(8,128)(2,1)S(1)}, bf16[32,96,128]{2,1,0:T(8,128)(2,1)S(1)}, u32[]{:S(2)}, u32[]{:S(2)}) collective-permute-start(bf16[32,96,128]{2,1,0:T(8,128)(2,1)S(1)} %get-tuple-element.37), channel_id=1, source_target_pairs={{0,1},{1,0},{2,3},{3,2},{4,5},{5,4},{6,7},{7,6},{8,9},{9,8},{10,11... | collective-permute-start | bytes 2359304 | tf_op jit(solution)/shard_map/ppermute | solution.py:702
  84.7 21.2 %all-to-all-start.3 = ((bf16[32,128,128]{2,1,0:T(8,128)(2,1)}), bf16[32,128,128]{2,1,0:T(8,128)(2,1)S(1)}, u32[]{:S(2)}, u32[]{:S(2)}) async-start(bf16[32,128,128]{2,1,0:T(8,128)(2,1)} %join_grads.1), calls=%async_computation.3 | async-start | bytes 2097152 | tf_op jit(solution)/shard_map/all_to_all | solution.py:573
  88.6 14.2 %collective-permute-start.4 = (bf16[128,768]{1,0:T(8,128)(2,1)S(1)}, bf16[128,768]{1,0:T(8,128)(2,1)S(1)}, u32[]{:S(2)}, u32[]{:S(2)}) collective-permute-start(bf16[128,768]{1,0:T(8,128)(2,1)S(1)} %get-tuple-element.39), channel_id=1, source_target_pairs={{0,32},{32,64},{64,96},{96,128},{128,160},{160,192},{192,224},{224... | collective-permute-start | bytes 589832 | tf_op jit(solution)/shard_map/ppermute | solution.py:680

commit v8 on v7

--- a/solution.py
+++ b/solution.py
@@ -628,7 +628,7 @@
     )(exchange(sent), before, after, gain, taps)
     swapped = lax.ppermute(got, "tm", partner)
 
-    block, chunk = 256, 512
+    block, chunk = 512, 512
     attend_scratch = [
         pltpu.VMEM((LANES, half), BF16),
         pltpu.VMEM((half, LANES), BF16),
@@ -640,7 +640,7 @@
         [VMEM],
         (VMEM,) * 4,
         attend_scratch,
-        24,
+        36,
         2 * matmul,
         "attend_forward_own",
         own * half,
@@ -651,7 +651,7 @@
         [SMEM] + [VMEM] * 5,
         (VMEM,) * 3,
         attend_scratch,
-        24,
+        36,
         2 * matmul,
         "attend_forward_other",
         own * half,
@@ -681,7 +681,7 @@
         block_out, "section", [(i, (i + 1) % sections) for i in range(sections)]
     )
 
-    block, chunk = 512, 512
+    block, chunk = own, 512
     backward_scratch = [
         pltpu.VMEM((LANES, half), BF16),
         pltpu.VMEM((half, LANES), BF16),
@@ -695,7 +695,7 @@
         [VMEM] * 5,
         (VMEM,) * 2,
         backward_scratch,
-        24,
+        36,
         4 * matmul,
         "attend_backward_other",
     )(other_kept, swapped, got, grads_got, head_out)
@@ -706,7 +706,7 @@
         [VMEM] * 5,
         (VMEM,) * 2,
         backward_scratch,
-        24,
+        36,
         4 * matmul,
         "attend_backward_own",
     )(own_kept, got, grads_got, head_out, grad_q)

time: 108 us -> 107 us (level)
  Pallas kernels: 26.4 us -> 25.1 us
  transfers between devices with their start and end apart: 7 -> 7, of which waited for: 5 -> 5; matrix products, arithmetic and copies ran while one was open for 1% -> 2% of each run, Pallas kernels for 7% -> 7%
where the time goes in v8:
time: 107 us; the launch traced here: 106 us
  starting transfers between devices  26.4 us (25%)
  blocking collectives  26.4 us (25%)
  waiting for transfers between devices  25.6 us (24%)
  Pallas kernels  25.1 us (23%)
  local copies, waits for them, and re-layouts  1.61 us (2%)
    all_to_all x2, blocking collectives, exchange(): return lax.all_to_all(pieces, 'tm', split_axis=0, concat_axis=0, tiled=True)  26.4 us
    all_to_all x2, starting transfers between devices, exchange(): return lax.all_to_all(pieces, 'tm', split_axis=0, concat_axis=0, tiled=True)  14.3 us
    ppermute x1, waiting for transfers between devices, local(): lax.ppermute(block_out, 'section', [(i, (i + 1) % sections) for i in rang...  12.3 us
    all_to_all x2, waiting for transfers between devices, exchange(): return lax.all_to_all(pieces, 'tm', split_axis=0, concat_axis=0, tiled=True)  5.62 us
    ppermute x1, waiting for transfers between devices, local(): lax.ppermute(jnp.concatenate([resid[frames - SUB:], cotangent[frames - ed...  5.53 us
    pallas_call x1, Pallas kernels, local(): call(lambda *refs: conv_kernel(groups, count, *refs), (shape((count, SUB,...  5.16 us
    pallas_call x1, Pallas kernels, local(): call(lambda *refs: backward_first_kernel(block, chunk, *refs), (part_shap...  4 us
    pallas_call x1, Pallas kernels, local(): call(lambda *refs: backward_second_kernel(block, chunk, *refs), (part_sha...  3.94 us
  transfers between devices with their start and end apart: 7, of which 5 were waited for; matrix products, arithmetic and copies ran while one was open for 2% of the time, Pallas kernels for 7%

profile of v8, /device:TPU:1, one launch (start us, length us, event | category | flops | bytes accessed | tf_op | source)
XLA Modules:
  0.0 105.9 jit_solution(12657317275987854973)
XLA Ops:
  0.7 2.4 %pack_qkv.1 = bf16[32,128,128]{2,1,0:T(8,128)(2,1)} custom-call(bf16[128,768]{1,0:T(8,128)(2,1)} %bitcast.25, bf16[128,768]{1,0:T(8,128)(2,1)} %bitcast.26, bf16[128,768]{1,0:T(8,128)(2,1)} %bitcast.27), custom_call_target="tpu_custom_call" | custom-call | flops 1000000 | bytes 2097152 | tf_op jit(solution)/shard_map/pack_qkv/pallas_call | solution.py:605
  3.1 10.5 %all-to-all-start = ((bf16[32,128,128]{2,1,0:T(8,128)(2,1)}), bf16[32,128,128]{2,1,0:T(8,128)(2,1)S(1)}, u32[]{:S(2)}, u32[]{:S(2)}) async-start(bf16[32,128,128]{2,1,0:T(8,128)(2,1)} %pack_qkv.1), calls=%async_computation | async-start | bytes 2097152 | tf_op jit(solution)/shard_map/all_to_all | solution.py:573
  13.6 0.8 slice_bitcast_fusion.2
  14.3 0.8 slice_bitcast_fusion
  15.2 3.5 %collective-permute-start = (bf16[48,768]{1,0:T(8,128)(2,1)S(1)}, bf16[48,768]{1,0:T(8,128)(2,1)S(1)}, u32[]{:S(2)}, u32[]{:S(2)}) collective-permute-start(bf16[48,768]{1,0:T(8,128)(2,1)S(1)} %pad_maximum_fusion), channel_id=1, source_target_pairs={{0,1},{1,2},{2,3},{3,4},{4,5},{5,6},{6,7},{7,8},{8,9},{9,10},{10,1... | collective-permute-start | bytes 221192 | tf_op jit(solution)/shard_map/ppermute | solution.py:595
  18.8 1.9 %collective-permute-start.1 = (bf16[48,768]{1,0:T(8,128)(2,1)S(1)}, bf16[48,768]{1,0:T(8,128)(2,1)S(1)}, u32[]{:S(2)}, u32[]{:S(2)}) collective-permute-start(bf16[48,768]{1,0:T(8,128)(2,1)S(1)} %pad_maximum_fusion.1), channel_id=1, source_target_pairs={{1,0},{2,1},{3,2},{4,3},{5,4},{6,5},{7,6},{8,7},{9,8},{10,9},{11,1... | collective-permute-start | bytes 221192 | tf_op jit(solution)/shard_map/ppermute | solution.py:598
  20.7 5.5 %collective-permute-done.refs_1_.refs_4_ = bf16[48,768]{1,0:T(8,128)(2,1)S(1)} collective-permute-done((bf16[48,768]{1,0:T(8,128)(2,1)S(1)}, bf16[48,768]{1,0:T(8,128)(2,1)S(1)}, u32[]{:S(2)}, u32[]{:S(2)}) %collective-permute-start) | collective-permute-done | bytes 73760 | tf_op jit(solution)/shard_map/ppermute | solution.py:595
  26.2 2.1 %collective-permute-done.1.refs_2_.refs_5_ = bf16[48,768]{1,0:T(8,128)(2,1)S(1)} collective-permute-done((bf16[48,768]{1,0:T(8,128)(2,1)S(1)}, bf16[48,768]{1,0:T(8,128)(2,1)S(1)}, u32[]{:S(2)}, u32[]{:S(2)}) %collective-permute-start.1) | collective-permute-done | bytes 73760 | tf_op jit(solution)/shard_map/ppermute | solution.py:598
  28.3 2.5 %all-to-all-done.refs_0_ = bf16[32,128,128]{2,1,0:T(8,128)(2,1)S(1)} async-done(((bf16[32,128,128]{2,1,0:T(8,128)(2,1)}), bf16[32,128,128]{2,1,0:T(8,128)(2,1)S(1)}, u32[]{:S(2)}, u32[]{:S(2)}) %all-to-all-start) | async-done | bytes 1048608 | tf_op jit(solution)/shard_map/all_to_all | solution.py:573
  30.9 2.3 %collective-permute-start.2 = (bf16[32,128,128]{2,1,0:T(8,128)(2,1)S(1)}, bf16[32,128,128]{2,1,0:T(8,128)(2,1)S(1)}, u32[]{:S(2)}, u32[]{:S(2)}) collective-permute-start(bf16[32,128,128]{2,1,0:T(8,128)(2,1)S(1)} %received.1.refs_0_.refs_1_.refs_2_), channel_id=1, source_target_pairs={{0,1},{1,0},{2,3},{3,2},{4,5},{5,4},{6,7},{7,6},{8,9},{9,8},{10,11... | collective-permute-start | bytes 3145736 | tf_op jit(solution)/shard_map/ppermute | solution.py:629
  33.2 3.2 %attend_forward_own.1 = (f32[1024,128]{1,0:T(8,128)S(1)}, f32[1024,128]{1,0:T(8,128)S(1)}, f32[1024,128]{1,0:T(8,128)S(1)}, bf16[1024,2048]{1,0:T(8,128)(2,1)S(1)}) custom-call(bf16[32,128,128]{2,1,0:T(8,128)(2,1)S(1)} %received.1.refs_0_.refs_1_.refs_2_), custom_call_target="tpu_custom_call" | custom-call | flops 1073741824 | bytes 2097152 | tf_op jit(solution)/shard_map/attend_forward_own/pallas_call | solution.py:637
  36.4 3.9 %attend_forward_other.1 = (bf16[32,48,128]{2,1,0:T(8,128)(2,1)S(1)}, bf16[1024,128]{1,0:T(8,128)(2,1)S(1)}, bf16[1024,2048]{1,0:T(8,128)(2,1)S(1)}) custom-call(s32[1]{0:T(128)} %bitcast.8.refs_0_, bf16[32,128,128]{2,1,0:T(8,128)(2,1)S(1)} %received.1.refs_0_.refs_1_.refs_2_, bf16[32,128,128]{2,1,0:T(8,128)(2,1)S(1)} %collective-permute-done.2.refs_2_.refs_1_, ...), custom_call_target="tpu_custom_call" | custom-call | flops 1073741824 | bytes 2097152 | tf_op jit(solution)/shard_map/attend_forward_other/pallas_call | solution.py:648
  40.3 13.9 %all_to_all.20.refs_1_ = bf16[32,48,128]{2,1,0:T(8,128)(2,1)S(1)} all-to-all(bf16[32,48,128]{2,1,0:T(8,128)(2,1)S(1)} %get-tuple-element.31), channel_id=1, replica_groups=mesh['section'=16,'tm'=32] {'tm'}, dimensions={0} | all-to-all | bytes 786432 | tf_op jit(solution)/shard_map/all_to_all | solution.py:573
  54.3 5.2 %conv_block.1 = (bf16[32,32,128]{2,1,0:T(8,128)(2,1)S(1)}, bf16[128,768]{1,0:T(8,128)(2,1)S(1)}, bf16[128,768]{1,0:T(8,128)(2,1)}) custom-call(s32[1]{0:T(128)} %bitcast.8.refs_0_, bf16[32,48,128]{2,1,0:T(8,128)(2,1)S(1)} %all_to_all.20.refs_1_, bf16[128,768]{1,0:T(8,128)(2,1)S(1)} %bitcast.21, bf16[128,768]{1,0:T(8,128)(2,1)S(1)} %bitcast.24, ...), custom_call_target="tpu_custom_call" | custom-call | flops 10000000 | bytes 2097152 | tf_op jit(solution)/shard_map/conv_block/pallas_call | solution.py:661
  59.4 12.5 %all_to_all.21.refs_3_.refs_2_ = bf16[32,32,128]{2,1,0:T(8,128)(2,1)S(1)} all-to-all(bf16[32,32,128]{2,1,0:T(8,128)(2,1)S(1)} %get-tuple-element.32), channel_id=1, replica_groups=mesh['section'=16,'tm'=32] {'tm'}, dimensions={0} | all-to-all | bytes 524288 | tf_op jit(solution)/shard_map/all_to_all | solution.py:573
  71.9 4.0 %attend_backward_other.1 = (bf16[32,96,128]{2,1,0:T(8,128)(2,1)S(1)}, f32[1024,128]{1,0:T(8,128)S(1)}) custom-call(bf16[1024,2048]{1,0:T(8,128)(2,1)S(1)} %get-tuple-element.34.refs_0_, bf16[32,128,128]{2,1,0:T(8,128)(2,1)S(1)} %collective-permute-done.2.refs_2_.refs_1_, bf16[32,128,128]{2,1,0:T(8,128)(2,1)S(1)} %received.1.refs_0_.refs_1_.refs_2_, ...), custom_call_target="tpu_custom_call" | custom-call | flops 2147483648 | bytes 2097152 | tf_op jit(solution)/shard_map/attend_backward_other/pallas_call | solution.py:692
  75.9 2.4 %collective-permute-start.3 = (bf16[32,96,128]{2,1,0:T(8,128)(2,1)S(1)}, bf16[32,96,128]{2,1,0:T(8,128)(2,1)S(1)}, u32[]{:S(2)}, u32[]{:S(2)}) collective-permute-start(bf16[32,96,128]{2,1,0:T(8,128)(2,1)S(1)} %get-tuple-element.37), channel_id=1, source_target_pairs={{0,1},{1,0},{2,3},{3,2},{4,5},{5,4},{6,7},{7,6},{8,9},{9,8},{10,11... | collective-permute-start | bytes 2359304 | tf_op jit(solution)/shard_map/ppermute | solution.py:702
  78.3 3.9 %attend_backward_own.1 = (bf16[32,96,128]{2,1,0:T(8,128)(2,1)S(1)}, bf16[32,32,128]{2,1,0:T(8,128)(2,1)S(1)}) custom-call(bf16[1024,2048]{1,0:T(8,128)(2,1)S(1)} %get-tuple-element.27.refs_0_, bf16[32,128,128]{2,1,0:T(8,128)(2,1)S(1)} %received.1.refs_0_.refs_1_.refs_2_, bf16[32,32,128]{2,1,0:T(8,128)(2,1)S(1)} %all_to_all.21.refs_3_.refs_2_, ...), custom_call_target="tpu_custom_call" | custom-call | flops 2147483648 | bytes 2097152 | tf_op jit(solution)/shard_map/attend_backward_own/pallas_call | solution.py:703
  82.2 1.2 %join_grads.1 = bf16[32,128,128]{2,1,0:T(8,128)(2,1)} custom-call(bf16[32,96,128]{2,1,0:T(8,128)(2,1)S(1)} %get-tuple-element.36.part_ref, bf16[32,96,128]{2,1,0:T(8,128)(2,1)S(1)} %collective-permute-done.3.other_ref, bf16[32,32,128]{2,1,0:T(8,128)(2,1)S(1)} %get-tuple-element.38.piece_ref), custom_call_target="tpu_custom_call" | custom-call | flops 1000000 | bytes 2097152 | tf_op jit(solution)/shard_map/join_grads/pallas_call | solution.py:713
  83.4 3.9 %all-to-all-start.3 = ((bf16[32,128,128]{2,1,0:T(8,128)(2,1)}), bf16[32,128,128]{2,1,0:T(8,128)(2,1)S(1)}, u32[]{:S(2)}, u32[]{:S(2)}) async-start(bf16[32,128,128]{2,1,0:T(8,128)(2,1)} %join_grads.1), calls=%async_computation.3 | async-start | bytes 2097152 | tf_op jit(solution)/shard_map/all_to_all | solution.py:573
  87.3 1.9 %collective-permute-start.4 = (bf16[128,768]{1,0:T(8,128)(2,1)S(1)}, bf16[128,768]{1,0:T(8,128)(2,1)S(1)}, u32[]{:S(2)}, u32[]{:S(2)}) collective-permute-start(bf16[128,768]{1,0:T(8,128)(2,1)S(1)} %get-tuple-element.39), channel_id=1, source_target_pairs={{0,32},{32,64},{64,96},{96,128},{128,160},{160,192},{192,224},{224... | collective-permute-start | bytes 589832 | tf_op jit(solution)/shard_map/ppermute | solution.py:680
  89.2 12.3 %collective-permute-done.4.refs_1_ = bf16[128,768]{1,0:T(8,128)(2,1)S(1)} collective-permute-done((bf16[128,768]{1,0:T(8,128)(2,1)S(1)}, bf16[128,768]{1,0:T(8,128)(2,1)S(1)}, u32[]{:S(2)}, u32[]{:S(2)}) %collective-permute-start.4) | collective-permute-done | bytes 196640 | tf_op jit(solution)/shard_map/ppermute | solution.py:680
  101.5 3.1 %all-to-all-done.3.refs_0_ = bf16[32,128,128]{2,1,0:T(8,128)(2,1)S(1)} async-done(((bf16[32,128,128]{2,1,0:T(8,128)(2,1)}), bf16[32,128,128]{2,1,0:T(8,128)(2,1)S(1)}, u32[]{:S(2)}, u32[]{:S(2)}) %all-to-all-start.3) | async-done | bytes 1048608 | tf_op jit(solution)/shard_map/all_to_all | solution.py:573
  104.6 1.3 %unpack_grads.1 = (bf16[128,768]{1,0:T(8,128)(2,1)}, bf16[128,768]{1,0:T(8,128)(2,1)}, bf16[128,768]{1,0:T(8,128)(2,1)}, f32[1,768]{1,0:T(1,128)}, f32[31,1,768]{2,1,0:T(1,128)}, /*index=5*/bf16[128,768]{1,0:T(8,128)(2,1)}) custom-call(bf16[32,128,128]{2,1,0:T(8,128)(2,1)S(1)} %all-to-all-done.3.refs_0_, bf16[128,768]{1,0:T(8,128)(2,1)S(1)} %collective-permute-done.4.refs_1_), custom_call_target="tpu_custom_call" | custom-call | flops 1000000 | bytes 2097152 | tf_op jit(solution)/shard_map/unpack_grads/pallas_call | solution.py:725
  (13 shorter events, 0.0 us)
Async XLA Ops:
  0.6 30.2 %copy-start.3 = (f32[1,768]{1,0:T(1,128)S(1)}, f32[1,768]{1,0:T(1,128)}, u32[]{:S(2)}) copy-start(f32[1,768]{1,0:T(1,128)} %refs_6_.1) | copy-start | bytes 9220
  0.6 30.2 %copy-start.1 = (f32[1,31,768]{2,0,1:T(1,128)S(1)}, f32[1,31,768]{2,0,1:T(1,128)}, u32[]{:S(2)}) copy-start(f32[1,31,768]{2,0,1:T(1,128)} %param.12) | copy-start | bytes 285700
  3.1 27.8 %all-to-all-start = ((bf16[32,128,128]{2,1,0:T(8,128)(2,1)}), bf16[32,128,128]{2,1,0:T(8,128)(2,1)S(1)}, u32[]{:S(2)}, u32[]{:S(2)}) async-start(bf16[32,128,128]{2,1,0:T(8,128)(2,1)} %pack_qkv.1), calls=%async_computation | async-start | bytes 2097152 | tf_op jit(solution)/shard_map/all_to_all | solution.py:573
  15.2 11.0 %collective-permute-start = (bf16[48,768]{1,0:T(8,128)(2,1)S(1)}, bf16[48,768]{1,0:T(8,128)(2,1)S(1)}, u32[]{:S(2)}, u32[]{:S(2)}) collective-permute-start(bf16[48,768]{1,0:T(8,128)(2,1)S(1)} %pad_maximum_fusion), channel_id=1, source_target_pairs={{0,1},{1,2},{2,3},{3,4},{4,5},{5,6},{6,7},{7,8},{8,9},{9,10},{10,1... | collective-permute-start | bytes 221192 | tf_op jit(solution)/shard_map/ppermute | solution.py:595
  18.8 9.6 %collective-permute-start.1 = (bf16[48,768]{1,0:T(8,128)(2,1)S(1)}, bf16[48,768]{1,0:T(8,128)(2,1)S(1)}, u32[]{:S(2)}, u32[]{:S(2)}) collective-permute-start(bf16[48,768]{1,0:T(8,128)(2,1)S(1)} %pad_maximum_fusion.1), channel_id=1, source_target_pairs={{1,0},{2,1},{3,2},{4,3},{5,4},{6,5},{7,6},{8,7},{9,8},{10,9},{11,1... | collective-permute-start | bytes 221192 | tf_op jit(solution)/shard_map/ppermute | solution.py:598
  30.9 5.5 %collective-permute-start.2 = (bf16[32,128,128]{2,1,0:T(8,128)(2,1)S(1)}, bf16[32,128,128]{2,1,0:T(8,128)(2,1)S(1)}, u32[]{:S(2)}, u32[]{:S(2)}) collective-permute-start(bf16[32,128,128]{2,1,0:T(8,128)(2,1)S(1)} %received.1.refs_0_.refs_1_.refs_2_), channel_id=1, source_target_pairs={{0,1},{1,0},{2,3},{3,2},{4,5},{5,4},{6,7},{7,6},{8,9},{9,8},{10,11... | collective-permute-start | bytes 3145736 | tf_op jit(solution)/shard_map/ppermute | solution.py:629
  33.2 21.1 %copy-start = (bf16[1,128,768]{2,1,0:T(8,128)(2,1)S(1)}, bf16[1,128,768]{2,1,0:T(8,128)(2,1)}, u32[]{:S(2)}) copy-start(bf16[1,128,768]{2,1,0:T(8,128)(2,1)} %param.7) | copy-start | bytes 589828
  33.2 21.1 %copy-start.2 = (bf16[1,128,768]{2,1,0:T(8,128)(2,1)S(1)}, bf16[1,128,768]{2,1,0:T(8,128)(2,1)}, u32[]{:S(2)}) copy-start(bf16[1,128,768]{2,1,0:T(8,128)(2,1)} %param.13) | copy-start | bytes 589828
  75.9 6.3 %collective-permute-start.3 = (bf16[32,96,128]{2,1,0:T(8,128)(2,1)S(1)}, bf16[32,96,128]{2,1,0:T(8,128)(2,1)S(1)}, u32[]{:S(2)}, u32[]{:S(2)}) collective-permute-start(bf16[32,96,128]{2,1,0:T(8,128)(2,1)S(1)} %get-tuple-element.37), channel_id=1, source_target_pairs={{0,1},{1,0},{2,3},{3,2},{4,5},{5,4},{6,7},{7,6},{8,9},{9,8},{10,11... | collective-permute-start | bytes 2359304 | tf_op jit(solution)/shard_map/ppermute | solution.py:702
  83.4 21.2 %all-to-all-start.3 = ((bf16[32,128,128]{2,1,0:T(8,128)(2,1)}), bf16[32,128,128]{2,1,0:T(8,128)(2,1)S(1)}, u32[]{:S(2)}, u32[]{:S(2)}) async-start(bf16[32,128,128]{2,1,0:T(8,128)(2,1)} %join_grads.1), calls=%async_computation.3 | async-start | bytes 2097152 | tf_op jit(solution)/shard_map/all_to_all | solution.py:573
  87.3 14.2 %collective-permute-start.4 = (bf16[128,768]{1,0:T(8,128)(2,1)S(1)}, bf16[128,768]{1,0:T(8,128)(2,1)S(1)}, u32[]{:S(2)}, u32[]{:S(2)}) collective-permute-start(bf16[128,768]{1,0:T(8,128)(2,1)S(1)} %get-tuple-element.39), channel_id=1, source_target_pairs={{0,32},{32,64},{64,96},{96,128},{128,160},{160,192},{192,224},{224... | collective-permute-start | bytes 589832 | tf_op jit(solution)/shard_map/ppermute | solution.py:680

commit v9 on v8

--- a/solution.py
+++ b/solution.py
@@ -32,6 +32,11 @@
 SMEM = pl.BlockSpec(memory_space=pltpu.SMEM)
 ANY = pl.BlockSpec(memory_space=pl.ANY)
 MIB = 1024 * 1024
+
+
+def stripes(block, group):
+    low, high = 16 * group, HALF + 16 * group
+    return jnp.concatenate([block[low : low + 16], block[high : high + 16]], axis=0)
 
 
 def lanes_of(rows):
@@ -100,9 +105,7 @@
         for i, block in enumerate(tiles_to_heads(tiles)):
             block = jnp.where(lane < HEAD_DIM, block, jnp.zeros_like(block))
             for group in range(groups):
-                send_ref[(4 * half + i) * groups + group, Q_ROWS, :] = block[
-                    group * SUB : (group + 1) * SUB
-                ]
+                send_ref[(4 * half + i) * groups + group, Q_ROWS, :] = stripes(block, group)
     for copy, source, turned in ((copies[1], k_ref, keys_t), (copies[2], v_ref, values_t)):
         copy.wait()
         for tile in range(CH // LANES):
@@ -251,26 +254,12 @@
     state = (top_ref, total_ref, result_ref)
     attend(got_ref, swapped_ref, state, finish, block, chunk, kept_ref, keys, values, scores)
     count = got_ref.shape[0]
-    side = jnp.where(place_ref[0] % groups == groups - 1, -1, 1)
-    lane = lanes_of(48)
+    before = place_ref[0] % groups >= groups // 2
+    side, offset = jnp.where(before, -1, 1), jnp.where(before, 16, 0)
     for device in range(count):
-        near = jnp.clip(device + side, 0, count - 1)
-        beside = out_ref[pl.ds(pl.multiple_of(near * SUB, SUB), SUB), :]
-        own = out_ref[device * SUB : (device + 1) * SUB, :]
-        tail = beside[16:32]
-        spare = jnp.concatenate([roll_lanes(tail, by) for by in (96, 64, 32)], axis=0)
-        piece = jnp.concatenate([own, beside[0:16]], axis=0)
-        send_ref[device] = jnp.where(lane < HEAD_DIM, piece, spare)
-
-
-def halo_of(piece):
-    lane = lanes_of(16)
-    tail = jnp.where(
-        lane < 32,
-        roll_lanes(piece[0:16], 32),
-        jnp.where(lane < 64, roll_lanes(piece[16:32], 64), roll_lanes(piece[32:48], 96)),
-    )
-    return [piece[32:48], tail]
+        near = jnp.clip(device + side, 0, count - 1) * SUB + offset
+        send_ref[device, 0:SUB, :] = out_ref[device * SUB : (device + 1) * SUB, :]
+        send_ref[device, SUB:48, :] = out_ref[pl.ds(pl.multiple_of(near, 16), 16), :]
 
 
 def conv_kernel(
@@ -288,12 +277,12 @@
     out_ref,
     grad_ref,
     mixed,
-    normed,
-    grad_conv,
+    normed_both,
+    grad_conv_both,
     scaled,
     sums,
     shifted,
-    grad_wide,
+    grad_wide_both,
 ):
     frames = resid_ref.shape[0]
     sub = frames // groups
@@ -308,11 +297,10 @@
         heads = []
         for i in range(4):
             first = (4 * half + i) * groups
-            before_piece = got_ref[first + groups - 1].astype(F32)
-            after_piece = got_ref[first].astype(F32)
-            parts = halo_of(before_piece)
-            parts += [got_ref[first + group, 0:sub, :].astype(F32) for group in range(groups)]
-            parts += halo_of(after_piece)
+            pieces = [got_ref[first + group].astype(F32) for group in range(groups)]
+            parts = [piece[32:48] for piece in pieces[2:]]
+            parts += [piece[0:16] for piece in pieces] + [piece[16:32] for piece in pieces]
+            parts += [piece[32:48] for piece in pieces[:2]]
             heads.append(jnp.concatenate(parts, axis=0))
         for i, attended in enumerate(heads_to_tiles(heads)):
             at = slice((3 * half + i) * LANES, (3 * half + i + 1) * LANES)
@@ -334,21 +322,25 @@
     own = slice(sub, sub + frames)
     inverse_own = inverse[sub : sub + frames]
 
-    grad_wide[0:8, :] = jnp.zeros((8, LANES), F32)
-    grad_wide[8 + frames : 16 + frames, :] = jnp.zeros((8, LANES), F32)
+    for tile in range(2):
+        grad_wide_both[tile, 0:8, :] = jnp.zeros((8, LANES), F32)
+        grad_wide_both[tile, 8 + frames : 16 + frames, :] = jnp.zeros((8, LANES), F32)
     dots = jnp.zeros((frames, LANES), F32)
     for tile in range(tiles):
         at = slice(tile * LANES, (tile + 1) * LANES)
         gain_row = gain_ref[0:1, at]
         value = (mixed[:, at] * inverse * gain_row).astype(BF16).astype(F32)
+        normed = normed_both.at[tile % 2]
+        grad_conv = grad_conv_both.at[tile % 2]
+        grad_wide = grad_wide_both.at[tile % 2]
         normed[...] = jnp.where(inside, value, 0.0)
         conv = jnp.zeros((inner, LANES), F32)
         for b in range(8):
             part = jnp.zeros((inner + 8, LANES), F32)
             for tap in range(b, TAPS, 8):
                 part = part + taps_ref[tap, :, at] * normed[tap - b : tap - b + inner + 8, :]
-            shifted[...] = part
-            conv = conv + shifted[b + 1 : b + 1 + inner, :]
+            shifted[b] = part
+            conv = conv + shifted[b, b + 1 : b + 1 + inner, :]
         sig = jax.nn.sigmoid(conv)
         out_ref[:, at] = (
             mixed[own, at] + (conv * sig)[edge : edge + frames]
@@ -371,8 +363,8 @@
                 sums[tap : tap + 1, at] = jnp.sum(
                     grad_here * normed[first : first + frames + 8, :], axis=0, keepdims=True
                 )
-            shifted[0 : frames + 8, :] = part
-            grad_normed = grad_normed + shifted[b + 1 : b + 1 + frames, :]
+            shifted[8 + b, 0 : frames + 8, :] = part
+            grad_normed = grad_normed + shifted[8 + b, b + 1 : b + 1 + frames, :]
         unit = mixed[own, at] * inverse_own
         sums[TAPS : TAPS + 1, at] = jnp.sum(grad_normed * unit, axis=0, keepdims=True)
         here = grad_normed * gain_row
@@ -400,7 +392,7 @@
                 spare = jnp.concatenate(
                     [roll_lanes(eight, 96 - 32 * a) for a in range(4)], axis=0
                 )
-                piece = jnp.where(lane < HEAD_DIM, block[group * sub : (group + 1) * sub], spare)
+                piece = jnp.where(lane < HEAD_DIM, stripes(block, group), spare)
                 send_ref[device] = piece.astype(BF16)
 
 
@@ -545,7 +537,11 @@
     for half in range(2):
         heads = [
             jnp.concatenate(
-                [got_ref[(4 * half + i) * groups + group, Q_ROWS, :] for group in range(groups)],
+                [
+                    got_ref[(4 * half + i) * groups + group, Q_ROWS.start + row : Q_ROWS.start + row + 16, :]
+                    for row in (0, 16)
+                    for group in range(groups)
+                ],
                 axis=0,
             )
             for i in range(4)
@@ -665,12 +661,12 @@
         (VMEM,) * 3,
         [
             pltpu.VMEM((frames + 2 * SUB, CH), F32),
-            pltpu.VMEM((frames + 2 * SUB, LANES), F32),
-            pltpu.VMEM((frames + 2 * edge, LANES), F32),
+            pltpu.VMEM((2, frames + 2 * SUB, LANES), F32),
+            pltpu.VMEM((2, frames + 2 * edge, LANES), F32),
             pltpu.VMEM((frames, CH), F32),
             pltpu.VMEM((TAPS + 1, CH), F32),
-            pltpu.VMEM((frames + 2 * edge + 8, LANES), F32),
-            pltpu.VMEM((frames + 16, LANES), F32),
+            pltpu.VMEM((16, frames + 2 * edge + 8, LANES), F32),
+            pltpu.VMEM((2, frames + 16, LANES), F32),
         ],
         16,
         10000000,

time: 107 us -> 106 us (level)
  no operation moved by 1% of the time
where the time goes in v9:
time: 106 us
  starting transfers between devices  26.4 us (25%)
  blocking collectives  26.4 us (25%)
  waiting for transfers between devices  25.6 us (24%)
  Pallas kernels  25.1 us (24%)
  local copies, waits for them, and re-layouts  1.61 us (2%)
    all_to_all x2, blocking collectives, exchange(): return lax.all_to_all(pieces, 'tm', split_axis=0, concat_axis=0, tiled=True)  26.4 us
    all_to_all x2, starting transfers between devices, exchange(): return lax.all_to_all(pieces, 'tm', split_axis=0, concat_axis=0, tiled=True)  14.3 us
    ppermute x1, waiting for transfers between devices, local(): lax.ppermute(block_out, 'section', [(i, (i + 1) % sections) for i in rang...  12.3 us
    all_to_all x2, waiting for transfers between devices, exchange(): return lax.all_to_all(pieces, 'tm', split_axis=0, concat_axis=0, tiled=True)  5.61 us
    ppermute x1, waiting for transfers between devices, local(): lax.ppermute(jnp.concatenate([resid[frames - SUB:], cotangent[frames - ed...  5.53 us
    pallas_call x1, Pallas kernels, local(): call(lambda *refs: conv_kernel(groups, count, *refs), (shape((count, SUB,...  5.19 us
    pallas_call x1, Pallas kernels, local(): call(lambda *refs: backward_first_kernel(block, chunk, *refs), (part_shap...  4 us
    pallas_call x1, Pallas kernels, local(): call(lambda *refs: backward_second_kernel(block, chunk, *refs), (part_sha...  3.95 us
  transfers between devices with their start and end apart: 7, of which 5 were waited for; matrix products, arithmetic and copies ran while one was open for 2% of the time, Pallas kernels for 7%

profile of v9, /device:TPU:1, one launch (start us, length us, event | category | flops | bytes accessed | tf_op | source)
XLA Modules:
  0.0 105.9 jit_solution(524348842478666968)
XLA Ops:
  0.7 2.4 %pack_qkv.1 = bf16[32,128,128]{2,1,0:T(8,128)(2,1)} custom-call(bf16[128,768]{1,0:T(8,128)(2,1)} %bitcast.25, bf16[128,768]{1,0:T(8,128)(2,1)} %bitcast.26, bf16[128,768]{1,0:T(8,128)(2,1)} %bitcast.27), custom_call_target="tpu_custom_call" | custom-call | flops 1000000 | bytes 2097152 | tf_op jit(solution)/shard_map/pack_qkv/pallas_call | solution.py:601
  3.1 10.5 %all-to-all-start = ((bf16[32,128,128]{2,1,0:T(8,128)(2,1)}), bf16[32,128,128]{2,1,0:T(8,128)(2,1)S(1)}, u32[]{:S(2)}, u32[]{:S(2)}) async-start(bf16[32,128,128]{2,1,0:T(8,128)(2,1)} %pack_qkv.1), calls=%async_computation | async-start | bytes 2097152 | tf_op jit(solution)/shard_map/all_to_all | solution.py:569
  13.6 0.8 slice_bitcast_fusion.2
  14.3 0.8 slice_bitcast_fusion
  15.2 3.5 %collective-permute-start = (bf16[48,768]{1,0:T(8,128)(2,1)S(1)}, bf16[48,768]{1,0:T(8,128)(2,1)S(1)}, u32[]{:S(2)}, u32[]{:S(2)}) collective-permute-start(bf16[48,768]{1,0:T(8,128)(2,1)S(1)} %pad_maximum_fusion), channel_id=1, source_target_pairs={{0,1},{1,2},{2,3},{3,4},{4,5},{5,6},{6,7},{7,8},{8,9},{9,10},{10,1... | collective-permute-start | bytes 221192 | tf_op jit(solution)/shard_map/ppermute | solution.py:591
  18.8 1.9 %collective-permute-start.1 = (bf16[48,768]{1,0:T(8,128)(2,1)S(1)}, bf16[48,768]{1,0:T(8,128)(2,1)S(1)}, u32[]{:S(2)}, u32[]{:S(2)}) collective-permute-start(bf16[48,768]{1,0:T(8,128)(2,1)S(1)} %pad_maximum_fusion.1), channel_id=1, source_target_pairs={{1,0},{2,1},{3,2},{4,3},{5,4},{6,5},{7,6},{8,7},{9,8},{10,9},{11,1... | collective-permute-start | bytes 221192 | tf_op jit(solution)/shard_map/ppermute | solution.py:594
  20.7 5.5 %collective-permute-done.refs_1_.refs_4_ = bf16[48,768]{1,0:T(8,128)(2,1)S(1)} collective-permute-done((bf16[48,768]{1,0:T(8,128)(2,1)S(1)}, bf16[48,768]{1,0:T(8,128)(2,1)S(1)}, u32[]{:S(2)}, u32[]{:S(2)}) %collective-permute-start) | collective-permute-done | bytes 73760 | tf_op jit(solution)/shard_map/ppermute | solution.py:591
  26.2 2.1 %collective-permute-done.1.refs_2_.refs_5_ = bf16[48,768]{1,0:T(8,128)(2,1)S(1)} collective-permute-done((bf16[48,768]{1,0:T(8,128)(2,1)S(1)}, bf16[48,768]{1,0:T(8,128)(2,1)S(1)}, u32[]{:S(2)}, u32[]{:S(2)}) %collective-permute-start.1) | collective-permute-done | bytes 73760 | tf_op jit(solution)/shard_map/ppermute | solution.py:594
  28.3 2.5 %all-to-all-done.refs_0_ = bf16[32,128,128]{2,1,0:T(8,128)(2,1)S(1)} async-done(((bf16[32,128,128]{2,1,0:T(8,128)(2,1)}), bf16[32,128,128]{2,1,0:T(8,128)(2,1)S(1)}, u32[]{:S(2)}, u32[]{:S(2)}) %all-to-all-start) | async-done | bytes 1048608 | tf_op jit(solution)/shard_map/all_to_all | solution.py:569
  30.9 2.3 %collective-permute-start.2 = (bf16[32,128,128]{2,1,0:T(8,128)(2,1)S(1)}, bf16[32,128,128]{2,1,0:T(8,128)(2,1)S(1)}, u32[]{:S(2)}, u32[]{:S(2)}) collective-permute-start(bf16[32,128,128]{2,1,0:T(8,128)(2,1)S(1)} %received.1.refs_0_.refs_1_.refs_2_), channel_id=1, source_target_pairs={{0,1},{1,0},{2,3},{3,2},{4,5},{5,4},{6,7},{7,6},{8,9},{9,8},{10,11... | collective-permute-start | bytes 3145736 | tf_op jit(solution)/shard_map/ppermute | solution.py:625
  33.2 3.2 %attend_forward_own.1 = (f32[1024,128]{1,0:T(8,128)S(1)}, f32[1024,128]{1,0:T(8,128)S(1)}, f32[1024,128]{1,0:T(8,128)S(1)}, bf16[1024,2048]{1,0:T(8,128)(2,1)S(1)}) custom-call(bf16[32,128,128]{2,1,0:T(8,128)(2,1)S(1)} %received.1.refs_0_.refs_1_.refs_2_), custom_call_target="tpu_custom_call" | custom-call | flops 1073741824 | bytes 2097152 | tf_op jit(solution)/shard_map/attend_forward_own/pallas_call | solution.py:633
  36.4 3.8 %attend_forward_other.1 = (bf16[32,48,128]{2,1,0:T(8,128)(2,1)S(1)}, bf16[1024,128]{1,0:T(8,128)(2,1)S(1)}, bf16[1024,2048]{1,0:T(8,128)(2,1)S(1)}) custom-call(s32[1]{0:T(128)} %bitcast.8.refs_0_, bf16[32,128,128]{2,1,0:T(8,128)(2,1)S(1)} %received.1.refs_0_.refs_1_.refs_2_, bf16[32,128,128]{2,1,0:T(8,128)(2,1)S(1)} %collective-permute-done.2.refs_2_.refs_1_, ...), custom_call_target="tpu_custom_call" | custom-call | flops 1073741824 | bytes 2097152 | tf_op jit(solution)/shard_map/attend_forward_other/pallas_call | solution.py:644
  40.3 13.9 %all_to_all.20.refs_1_ = bf16[32,48,128]{2,1,0:T(8,128)(2,1)S(1)} all-to-all(bf16[32,48,128]{2,1,0:T(8,128)(2,1)S(1)} %get-tuple-element.31), channel_id=1, replica_groups=mesh['section'=16,'tm'=32] {'tm'}, dimensions={0} | all-to-all | bytes 786432 | tf_op jit(solution)/shard_map/all_to_all | solution.py:569
  54.2 5.2 %conv_block.1 = (bf16[32,32,128]{2,1,0:T(8,128)(2,1)S(1)}, bf16[128,768]{1,0:T(8,128)(2,1)S(1)}, bf16[128,768]{1,0:T(8,128)(2,1)}) custom-call(s32[1]{0:T(128)} %bitcast.8.refs_0_, bf16[32,48,128]{2,1,0:T(8,128)(2,1)S(1)} %all_to_all.20.refs_1_, bf16[128,768]{1,0:T(8,128)(2,1)S(1)} %bitcast.21, bf16[128,768]{1,0:T(8,128)(2,1)S(1)} %bitcast.24, ...), custom_call_target="tpu_custom_call" | custom-call | flops 10000000 | bytes 2097152 | tf_op jit(solution)/shard_map/conv_block/pallas_call | solution.py:657
  59.4 12.5 %all_to_all.21.refs_3_.refs_2_ = bf16[32,32,128]{2,1,0:T(8,128)(2,1)S(1)} all-to-all(bf16[32,32,128]{2,1,0:T(8,128)(2,1)S(1)} %get-tuple-element.32), channel_id=1, replica_groups=mesh['section'=16,'tm'=32] {'tm'}, dimensions={0} | all-to-all | bytes 524288 | tf_op jit(solution)/shard_map/all_to_all | solution.py:569
  71.9 4.0 %attend_backward_other.1 = (bf16[32,96,128]{2,1,0:T(8,128)(2,1)S(1)}, f32[1024,128]{1,0:T(8,128)S(1)}) custom-call(bf16[1024,2048]{1,0:T(8,128)(2,1)S(1)} %get-tuple-element.34.refs_0_, bf16[32,128,128]{2,1,0:T(8,128)(2,1)S(1)} %collective-permute-done.2.refs_2_.refs_1_, bf16[32,128,128]{2,1,0:T(8,128)(2,1)S(1)} %received.1.refs_0_.refs_1_.refs_2_, ...), custom_call_target="tpu_custom_call" | custom-call | flops 2147483648 | bytes 2097152 | tf_op jit(solution)/shard_map/attend_backward_other/pallas_call | solution.py:688
  75.9 2.4 %collective-permute-start.3 = (bf16[32,96,128]{2,1,0:T(8,128)(2,1)S(1)}, bf16[32,96,128]{2,1,0:T(8,128)(2,1)S(1)}, u32[]{:S(2)}, u32[]{:S(2)}) collective-permute-start(bf16[32,96,128]{2,1,0:T(8,128)(2,1)S(1)} %get-tuple-element.37), channel_id=1, source_target_pairs={{0,1},{1,0},{2,3},{3,2},{4,5},{5,4},{6,7},{7,6},{8,9},{9,8},{10,11... | collective-permute-start | bytes 2359304 | tf_op jit(solution)/shard_map/ppermute | solution.py:698
  78.3 3.9 %attend_backward_own.1 = (bf16[32,96,128]{2,1,0:T(8,128)(2,1)S(1)}, bf16[32,32,128]{2,1,0:T(8,128)(2,1)S(1)}) custom-call(bf16[1024,2048]{1,0:T(8,128)(2,1)S(1)} %get-tuple-element.27.refs_0_, bf16[32,128,128]{2,1,0:T(8,128)(2,1)S(1)} %received.1.refs_0_.refs_1_.refs_2_, bf16[32,32,128]{2,1,0:T(8,128)(2,1)S(1)} %all_to_all.21.refs_3_.refs_2_, ...), custom_call_target="tpu_custom_call" | custom-call | flops 2147483648 | bytes 2097152 | tf_op jit(solution)/shard_map/attend_backward_own/pallas_call | solution.py:699
  82.2 1.2 %join_grads.1 = bf16[32,128,128]{2,1,0:T(8,128)(2,1)} custom-call(bf16[32,96,128]{2,1,0:T(8,128)(2,1)S(1)} %get-tuple-element.36.part_ref, bf16[32,96,128]{2,1,0:T(8,128)(2,1)S(1)} %collective-permute-done.3.other_ref, bf16[32,32,128]{2,1,0:T(8,128)(2,1)S(1)} %get-tuple-element.38.piece_ref), custom_call_target="tpu_custom_call" | custom-call | flops 1000000 | bytes 2097152 | tf_op jit(solution)/shard_map/join_grads/pallas_call | solution.py:709
  83.4 3.8 %all-to-all-start.3 = ((bf16[32,128,128]{2,1,0:T(8,128)(2,1)}), bf16[32,128,128]{2,1,0:T(8,128)(2,1)S(1)}, u32[]{:S(2)}, u32[]{:S(2)}) async-start(bf16[32,128,128]{2,1,0:T(8,128)(2,1)} %join_grads.1), calls=%async_computation.3 | async-start | bytes 2097152 | tf_op jit(solution)/shard_map/all_to_all | solution.py:569
  87.2 1.9 %collective-permute-start.4 = (bf16[128,768]{1,0:T(8,128)(2,1)S(1)}, bf16[128,768]{1,0:T(8,128)(2,1)S(1)}, u32[]{:S(2)}, u32[]{:S(2)}) collective-permute-start(bf16[128,768]{1,0:T(8,128)(2,1)S(1)} %get-tuple-element.39), channel_id=1, source_target_pairs={{0,32},{32,64},{64,96},{96,128},{128,160},{160,192},{192,224},{224... | collective-permute-start | bytes 589832 | tf_op jit(solution)/shard_map/ppermute | solution.py:676
  89.2 12.3 %collective-permute-done.4.refs_1_ = bf16[128,768]{1,0:T(8,128)(2,1)S(1)} collective-permute-done((bf16[128,768]{1,0:T(8,128)(2,1)S(1)}, bf16[128,768]{1,0:T(8,128)(2,1)S(1)}, u32[]{:S(2)}, u32[]{:S(2)}) %collective-permute-start.4) | collective-permute-done | bytes 196640 | tf_op jit(solution)/shard_map/ppermute | solution.py:676
  101.5 3.1 %all-to-all-done.3.refs_0_ = bf16[32,128,128]{2,1,0:T(8,128)(2,1)S(1)} async-done(((bf16[32,128,128]{2,1,0:T(8,128)(2,1)}), bf16[32,128,128]{2,1,0:T(8,128)(2,1)S(1)}, u32[]{:S(2)}, u32[]{:S(2)}) %all-to-all-start.3) | async-done | bytes 1048608 | tf_op jit(solution)/shard_map/all_to_all | solution.py:569
  104.5 1.3 %unpack_grads.1 = (bf16[128,768]{1,0:T(8,128)(2,1)}, bf16[128,768]{1,0:T(8,128)(2,1)}, bf16[128,768]{1,0:T(8,128)(2,1)}, f32[1,768]{1,0:T(1,128)}, f32[31,1,768]{2,1,0:T(1,128)}, /*index=5*/bf16[128,768]{1,0:T(8,128)(2,1)}) custom-call(bf16[32,128,128]{2,1,0:T(8,128)(2,1)S(1)} %all-to-all-done.3.refs_0_, bf16[128,768]{1,0:T(8,128)(2,1)S(1)} %collective-permute-done.4.refs_1_), custom_call_target="tpu_custom_call" | custom-call | flops 1000000 | bytes 2097152 | tf_op jit(solution)/shard_map/unpack_grads/pallas_call | solution.py:721
  (13 shorter events, 0.0 us)
Async XLA Ops:
  0.6 30.2 %copy-start.3 = (f32[1,768]{1,0:T(1,128)S(1)}, f32[1,768]{1,0:T(1,128)}, u32[]{:S(2)}) copy-start(f32[1,768]{1,0:T(1,128)} %refs_6_.1) | copy-start | bytes 9220
  0.6 30.2 %copy-start.1 = (f32[1,31,768]{2,0,1:T(1,128)S(1)}, f32[1,31,768]{2,0,1:T(1,128)}, u32[]{:S(2)}) copy-start(f32[1,31,768]{2,0,1:T(1,128)} %param.12) | copy-start | bytes 285700
  3.1 27.8 %all-to-all-start = ((bf16[32,128,128]{2,1,0:T(8,128)(2,1)}), bf16[32,128,128]{2,1,0:T(8,128)(2,1)S(1)}, u32[]{:S(2)}, u32[]{:S(2)}) async-start(bf16[32,128,128]{2,1,0:T(8,128)(2,1)} %pack_qkv.1), calls=%async_computation | async-start | bytes 2097152 | tf_op jit(solution)/shard_map/all_to_all | solution.py:569
  15.2 11.0 %collective-permute-start = (bf16[48,768]{1,0:T(8,128)(2,1)S(1)}, bf16[48,768]{1,0:T(8,128)(2,1)S(1)}, u32[]{:S(2)}, u32[]{:S(2)}) collective-permute-start(bf16[48,768]{1,0:T(8,128)(2,1)S(1)} %pad_maximum_fusion), channel_id=1, source_target_pairs={{0,1},{1,2},{2,3},{3,4},{4,5},{5,6},{6,7},{7,8},{8,9},{9,10},{10,1... | collective-permute-start | bytes 221192 | tf_op jit(solution)/shard_map/ppermute | solution.py:591
  18.8 9.6 %collective-permute-start.1 = (bf16[48,768]{1,0:T(8,128)(2,1)S(1)}, bf16[48,768]{1,0:T(8,128)(2,1)S(1)}, u32[]{:S(2)}, u32[]{:S(2)}) collective-permute-start(bf16[48,768]{1,0:T(8,128)(2,1)S(1)} %pad_maximum_fusion.1), channel_id=1, source_target_pairs={{1,0},{2,1},{3,2},{4,3},{5,4},{6,5},{7,6},{8,7},{9,8},{10,9},{11,1... | collective-permute-start | bytes 221192 | tf_op jit(solution)/shard_map/ppermute | solution.py:594
  30.9 5.5 %collective-permute-start.2 = (bf16[32,128,128]{2,1,0:T(8,128)(2,1)S(1)}, bf16[32,128,128]{2,1,0:T(8,128)(2,1)S(1)}, u32[]{:S(2)}, u32[]{:S(2)}) collective-permute-start(bf16[32,128,128]{2,1,0:T(8,128)(2,1)S(1)} %received.1.refs_0_.refs_1_.refs_2_), channel_id=1, source_target_pairs={{0,1},{1,0},{2,3},{3,2},{4,5},{5,4},{6,7},{7,6},{8,9},{9,8},{10,11... | collective-permute-start | bytes 3145736 | tf_op jit(solution)/shard_map/ppermute | solution.py:625
  33.2 21.0 %copy-start = (bf16[1,128,768]{2,1,0:T(8,128)(2,1)S(1)}, bf16[1,128,768]{2,1,0:T(8,128)(2,1)}, u32[]{:S(2)}) copy-start(bf16[1,128,768]{2,1,0:T(8,128)(2,1)} %param.7) | copy-start | bytes 589828
  33.2 21.0 %copy-start.2 = (bf16[1,128,768]{2,1,0:T(8,128)(2,1)S(1)}, bf16[1,128,768]{2,1,0:T(8,128)(2,1)}, u32[]{:S(2)}) copy-start(bf16[1,128,768]{2,1,0:T(8,128)(2,1)} %param.13) | copy-start | bytes 589828
  75.9 6.3 %collective-permute-start.3 = (bf16[32,96,128]{2,1,0:T(8,128)(2,1)S(1)}, bf16[32,96,128]{2,1,0:T(8,128)(2,1)S(1)}, u32[]{:S(2)}, u32[]{:S(2)}) collective-permute-start(bf16[32,96,128]{2,1,0:T(8,128)(2,1)S(1)} %get-tuple-element.37), channel_id=1, source_target_pairs={{0,1},{1,0},{2,3},{3,2},{4,5},{5,4},{6,7},{7,6},{8,9},{9,8},{10,11... | collective-permute-start | bytes 2359304 | tf_op jit(solution)/shard_map/ppermute | solution.py:698
  83.4 21.1 %all-to-all-start.3 = ((bf16[32,128,128]{2,1,0:T(8,128)(2,1)}), bf16[32,128,128]{2,1,0:T(8,128)(2,1)S(1)}, u32[]{:S(2)}, u32[]{:S(2)}) async-start(bf16[32,128,128]{2,1,0:T(8,128)(2,1)} %join_grads.1), calls=%async_computation.3 | async-start | bytes 2097152 | tf_op jit(solution)/shard_map/all_to_all | solution.py:569
  87.2 14.2 %collective-permute-start.4 = (bf16[128,768]{1,0:T(8,128)(2,1)S(1)}, bf16[128,768]{1,0:T(8,128)(2,1)S(1)}, u32[]{:S(2)}, u32[]{:S(2)}) collective-permute-start(bf16[128,768]{1,0:T(8,128)(2,1)S(1)} %get-tuple-element.39), channel_id=1, source_target_pairs={{0,32},{32,64},{64,96},{96,128},{128,160},{160,192},{192,224},{224... | collective-permute-start | bytes 589832 | tf_op jit(solution)/shard_map/ppermute | solution.py:676

commit v10 on v9

--- a/solution.py
+++ b/solution.py
@@ -134,15 +134,17 @@
 def fill_half(half_ref, start, stop, keys_t, values_t, keys, values):
     lane = lanes_of(HEAD_DIM)
     zeros = jnp.zeros((LANES - HEAD_DIM, LANES), BF16)
+    first_row = lax.broadcasted_iota(jnp.int32, zeros.shape, 0) == 0
+    ones = jnp.where(first_row, 1.0, 0.0).astype(BF16)
     for pair in range(start // LANES, stop // LANES):
         at = slice(pair * LANES, (pair + 1) * LANES)
         even = half_ref[2 * pair, KV_ROWS, :]
         odd = half_ref[2 * pair + 1, KV_ROWS, :]
-        for turned, natural, block in (
-            (keys_t, keys, jnp.where(lane < HALF, even, roll_lanes(odd, HALF))),
-            (values_t, values, jnp.where(lane < HALF, roll_lanes(even, HALF), odd)),
+        for turned, natural, pad, block in (
+            (keys_t, keys, zeros, jnp.where(lane < HALF, even, roll_lanes(odd, HALF))),
+            (values_t, values, ones, jnp.where(lane < HALF, roll_lanes(even, HALF), odd)),
         ):
-            block = jnp.concatenate([block, zeros], axis=0)
+            block = jnp.concatenate([block, pad], axis=0)
             if turned is not None:
                 turned[:, at] = block
             if natural is not None:
@@ -174,14 +176,12 @@
         at = slice(step * block, (step + 1) * block)
         top = jnp.broadcast_to(jnp.max(peak, axis=1, keepdims=True) * SCALE2, (block, LANES))
         if state is None:
-            total = jnp.zeros((block, LANES), F32)
             result = jnp.zeros((block, LANES), F32)
         else:
             old = state[0][at, :]
             top = jnp.maximum(top, old)
             shrink = jnp.exp2(old - top)
-            total = state[1][at, :] * shrink
-            result = state[2][at, :] * shrink
+            result = state[1][at, :] * shrink
         tops = jnp.concatenate([top] * (chunk // LANES), axis=1)
         peak = lowest
         if step + 1 < blocks:
@@ -190,14 +190,12 @@
             if step + 1 < blocks:
                 peak = score(step + 1, rows, start, peak)
             weights = jnp.exp2(scores[step % 2, :, start : start + chunk] * SCALE2 - tops)
-            for tile in range(0, chunk, LANES):
-                total = total + weights[:, tile : tile + LANES]
             weights = weights.astype(BF16)
             kept_ref[at, start : start + chunk] = weights
             result = result + jnp.dot(
                 weights, values[start : start + chunk, :], preferred_element_type=F32
             )
-        finish(at, top, total, result)
+        finish(at, top, result)
 
 
 def forward_first_kernel(
@@ -205,16 +203,14 @@
     chunk,
     got_ref,
     top_ref,
-    total_ref,
     result_ref,
     kept_ref,
     keys,
     values,
     scores,
 ):
-    def finish(at, top, total, result):
+    def finish(at, top, result):
         top_ref[at, :] = top
-        total_ref[at, :] = total
         result_ref[at, :] = result
 
     attend(got_ref, got_ref, None, finish, block, chunk, kept_ref, keys, values, scores)
@@ -228,7 +224,6 @@
     got_ref,
     swapped_ref,
     top_ref,
-    total_ref,
     result_ref,
     send_ref,
     out_ref,
@@ -237,10 +232,10 @@
     values,
     scores,
 ):
-    def finish(at, top, total, result):
-        total = jnp.sum(total, axis=1, keepdims=True)
+    def finish(at, top, result):
+        lane = lanes_of(block)
+        total = jnp.sum(jnp.where(lane == HEAD_DIM, result, 0.0), axis=1, keepdims=True)
         merged = result / total
-        lane = lanes_of(block)
         for spots, rest in (
             (OWN_FACTOR, jnp.exp2(top_ref[at, :] - top) / total),
             (OTHER_FACTOR, jnp.broadcast_to(1.0 / total, (block, LANES))),
@@ -251,7 +246,7 @@
                 rest = rest - part
         out_ref[at, :] = merged.astype(BF16)
 
-    state = (top_ref, total_ref, result_ref)
+    state = (top_ref, result_ref)
     attend(got_ref, swapped_ref, state, finish, block, chunk, kept_ref, keys, values, scores)
     count = got_ref.shape[0]
     before = place_ref[0] % groups >= groups // 2
@@ -334,13 +329,14 @@
         grad_conv = grad_conv_both.at[tile % 2]
         grad_wide = grad_wide_both.at[tile % 2]
         normed[...] = jnp.where(inside, value, 0.0)
-        conv = jnp.zeros((inner, LANES), F32)
         for b in range(8):
-            part = jnp.zeros((inner + 8, LANES), F32)
+            part = None
             for tap in range(b, TAPS, 8):
-                part = part + taps_ref[tap, :, at] * normed[tap - b : tap - b + inner + 8, :]
+                term = taps_ref[tap, :, at] * normed[tap - b : tap - b + inner + 8, :]
+                part = term if part is None else part + term
             shifted[b] = part
-            conv = conv + shifted[b, b + 1 : b + 1 + inner, :]
+            term = shifted[b, b + 1 : b + 1 + inner, :]
+            conv = term if b == 0 else conv + term
         sig = jax.nn.sigmoid(conv)
         out_ref[:, at] = (
             mixed[own, at] + (conv * sig)[edge : edge + frames]
@@ -351,20 +347,21 @@
         ).astype(F32)
         value = (cot * sig * (1.0 + conv * (1.0 - sig))).astype(BF16).astype(F32)
         grad_conv[...] = jnp.where(inside_inner, value, 0.0)
-        grad_normed = jnp.zeros((frames, LANES), F32)
         grad_wide[8 : 8 + frames, :] = grad_conv[edge : edge + frames, :]
         for b in range(8):
-            part = jnp.zeros((frames + 8, LANES), F32)
+            part = None
             grad_here = grad_wide[7 - b : 15 - b + frames, :]
             for tap in range(b, TAPS, 8):
                 first = tap - b
-                part = part + taps_ref[TAPS - 1 - tap, :, at] * grad_conv[first : first + frames + 8, :]
+                term = taps_ref[TAPS - 1 - tap, :, at] * grad_conv[first : first + frames + 8, :]
+                part = term if part is None else part + term
                 first = first + edge
                 sums[tap : tap + 1, at] = jnp.sum(
                     grad_here * normed[first : first + frames + 8, :], axis=0, keepdims=True
                 )
             shifted[8 + b, 0 : frames + 8, :] = part
-            grad_normed = grad_normed + shifted[8 + b, b + 1 : b + 1 + frames, :]
+            term = shifted[8 + b, b + 1 : b + 1 + frames, :]
+            grad_normed = term if b == 0 else grad_normed + term
         unit = mixed[own, at] * inverse_own
         sums[TAPS : TAPS + 1, at] = jnp.sum(grad_normed * unit, axis=0, keepdims=True)
         here = grad_normed * gain_row
@@ -632,9 +629,9 @@
     ]
     *state, own_kept = call(
         lambda *refs: forward_first_kernel(block, chunk, *refs),
-        (own_shape,) * 3 + (kept_shape,),
+        (own_shape,) * 2 + (kept_shape,),
         [VMEM],
-        (VMEM,) * 4,
+        (VMEM,) * 3,
         attend_scratch,
         36,
         2 * matmul,
@@ -644,7 +641,7 @@
     results, head_out, other_kept = call(
         lambda *refs: forward_second_kernel(block, chunk, groups, *refs),
         (shape((count, 48, LANES), BF16), shape((own, LANES), BF16), kept_shape),
-        [SMEM] + [VMEM] * 5,
+        [SMEM] + [VMEM] * 4,
         (VMEM,) * 3,
         attend_scratch,
         36,

time: 106 us -> 106 us (level)
  transfers between devices with their start and end apart: 7 -> 7, of which waited for: 5 -> 5; matrix products, arithmetic and copies ran while one was open for 2% -> 2% of each run, Pallas kernels for 7% -> 6%
where the time goes in v10:
time: 106 us; the launch traced here: 105 us
  blocking collectives  26.6 us (25%)
  starting transfers between devices  26.2 us (25%)
  waiting for transfers between devices  25.6 us (24%)
  Pallas kernels  24.3 us (23%)
  local copies, waits for them, and re-layouts  1.61 us (2%)
    all_to_all x2, blocking collectives, exchange(): return lax.all_to_all(pieces, 'tm', split_axis=0, concat_axis=0, tiled=True)  26.6 us
    all_to_all x2, starting transfers between devices, exchange(): return lax.all_to_all(pieces, 'tm', split_axis=0, concat_axis=0, tiled=True)  14.3 us
    ppermute x1, waiting for transfers between devices, local(): lax.ppermute(block_out, 'section', [(i, (i + 1) % sections) for i in rang...  12.3 us
    all_to_all x2, waiting for transfers between devices, exchange(): return lax.all_to_all(pieces, 'tm', split_axis=0, concat_axis=0, tiled=True)  5.62 us
    ppermute x1, waiting for transfers between devices, local(): lax.ppermute(jnp.concatenate([resid[frames - SUB:], cotangent[frames - ed...  5.53 us
    pallas_call x1, Pallas kernels, local(): call(lambda *refs: conv_kernel(groups, count, *refs), (shape((count, SUB,...  5.19 us
    pallas_call x1, Pallas kernels, local(): call(lambda *refs: backward_first_kernel(block, chunk, *refs), (part_shap...  4 us
    pallas_call x1, Pallas kernels, local(): call(lambda *refs: backward_second_kernel(block, chunk, *refs), (part_sha...  3.94 us
  transfers between devices with their start and end apart: 7, of which 5 were waited for; matrix products, arithmetic and copies ran while one was open for 2% of the time, Pallas kernels for 6%

profile of v10, /device:TPU:1, one launch (start us, length us, event | category | flops | bytes accessed | tf_op | source)
XLA Modules:
  0.0 105.0 jit_solution(14212453497013150300)
XLA Ops:
  0.7 2.4 %pack_qkv.1 = bf16[32,128,128]{2,1,0:T(8,128)(2,1)} custom-call(bf16[128,768]{1,0:T(8,128)(2,1)} %bitcast.25, bf16[128,768]{1,0:T(8,128)(2,1)} %bitcast.26, bf16[128,768]{1,0:T(8,128)(2,1)} %bitcast.27), custom_call_target="tpu_custom_call" | custom-call | flops 1000000 | bytes 2097152 | tf_op jit(solution)/shard_map/pack_qkv/pallas_call | solution.py:598
  3.1 10.5 %all-to-all-start = ((bf16[32,128,128]{2,1,0:T(8,128)(2,1)}), bf16[32,128,128]{2,1,0:T(8,128)(2,1)S(1)}, u32[]{:S(2)}, u32[]{:S(2)}) async-start(bf16[32,128,128]{2,1,0:T(8,128)(2,1)} %pack_qkv.1), calls=%async_computation | async-start | bytes 2097152 | tf_op jit(solution)/shard_map/all_to_all | solution.py:566
  13.6 0.8 slice_bitcast_fusion.2
  14.3 0.8 slice_bitcast_fusion
  15.2 3.5 %collective-permute-start = (bf16[48,768]{1,0:T(8,128)(2,1)S(1)}, bf16[48,768]{1,0:T(8,128)(2,1)S(1)}, u32[]{:S(2)}, u32[]{:S(2)}) collective-permute-start(bf16[48,768]{1,0:T(8,128)(2,1)S(1)} %pad_maximum_fusion), channel_id=1, source_target_pairs={{0,1},{1,2},{2,3},{3,4},{4,5},{5,6},{6,7},{7,8},{8,9},{9,10},{10,1... | collective-permute-start | bytes 221192 | tf_op jit(solution)/shard_map/ppermute | solution.py:588
  18.8 1.9 %collective-permute-start.1 = (bf16[48,768]{1,0:T(8,128)(2,1)S(1)}, bf16[48,768]{1,0:T(8,128)(2,1)S(1)}, u32[]{:S(2)}, u32[]{:S(2)}) collective-permute-start(bf16[48,768]{1,0:T(8,128)(2,1)S(1)} %pad_maximum_fusion.1), channel_id=1, source_target_pairs={{1,0},{2,1},{3,2},{4,3},{5,4},{6,5},{7,6},{8,7},{9,8},{10,9},{11,1... | collective-permute-start | bytes 221192 | tf_op jit(solution)/shard_map/ppermute | solution.py:591
  20.7 5.5 %collective-permute-done.refs_1_.refs_4_ = bf16[48,768]{1,0:T(8,128)(2,1)S(1)} collective-permute-done((bf16[48,768]{1,0:T(8,128)(2,1)S(1)}, bf16[48,768]{1,0:T(8,128)(2,1)S(1)}, u32[]{:S(2)}, u32[]{:S(2)}) %collective-permute-start) | collective-permute-done | bytes 73760 | tf_op jit(solution)/shard_map/ppermute | solution.py:588
  26.2 2.1 %collective-permute-done.1.refs_2_.refs_5_ = bf16[48,768]{1,0:T(8,128)(2,1)S(1)} collective-permute-done((bf16[48,768]{1,0:T(8,128)(2,1)S(1)}, bf16[48,768]{1,0:T(8,128)(2,1)S(1)}, u32[]{:S(2)}, u32[]{:S(2)}) %collective-permute-start.1) | collective-permute-done | bytes 73760 | tf_op jit(solution)/shard_map/ppermute | solution.py:591
  28.3 2.5 %all-to-all-done.refs_0_ = bf16[32,128,128]{2,1,0:T(8,128)(2,1)S(1)} async-done(((bf16[32,128,128]{2,1,0:T(8,128)(2,1)}), bf16[32,128,128]{2,1,0:T(8,128)(2,1)S(1)}, u32[]{:S(2)}, u32[]{:S(2)}) %all-to-all-start) | async-done | bytes 1048608 | tf_op jit(solution)/shard_map/all_to_all | solution.py:566
  30.9 2.3 %collective-permute-start.2 = (bf16[32,128,128]{2,1,0:T(8,128)(2,1)S(1)}, bf16[32,128,128]{2,1,0:T(8,128)(2,1)S(1)}, u32[]{:S(2)}, u32[]{:S(2)}) collective-permute-start(bf16[32,128,128]{2,1,0:T(8,128)(2,1)S(1)} %received.1.refs_0_.refs_1_.refs_2_), channel_id=1, source_target_pairs={{0,1},{1,0},{2,3},{3,2},{4,5},{5,4},{6,7},{7,6},{8,9},{9,8},{10,11... | collective-permute-start | bytes 3145736 | tf_op jit(solution)/shard_map/ppermute | solution.py:622
  33.2 2.8 %attend_forward_own.1 = (f32[1024,128]{1,0:T(8,128)S(1)}, f32[1024,128]{1,0:T(8,128)S(1)}, bf16[1024,2048]{1,0:T(8,128)(2,1)S(1)}) custom-call(bf16[32,128,128]{2,1,0:T(8,128)(2,1)S(1)} %received.1.refs_0_.refs_1_.refs_2_), custom_call_target="tpu_custom_call" | custom-call | flops 1073741824 | bytes 2097152 | tf_op jit(solution)/shard_map/attend_forward_own/pallas_call | solution.py:630
  36.1 3.4 %attend_forward_other.1 = (bf16[32,48,128]{2,1,0:T(8,128)(2,1)S(1)}, bf16[1024,128]{1,0:T(8,128)(2,1)S(1)}, bf16[1024,2048]{1,0:T(8,128)(2,1)S(1)}) custom-call(s32[1]{0:T(128)} %bitcast.8.refs_0_, bf16[32,128,128]{2,1,0:T(8,128)(2,1)S(1)} %received.1.refs_0_.refs_1_.refs_2_, bf16[32,128,128]{2,1,0:T(8,128)(2,1)S(1)} %collective-permute-done.2.refs_2_.refs_1_, ...), custom_call_target="tpu_custom_call" | custom-call | flops 1073741824 | bytes 2097152 | tf_op jit(solution)/shard_map/attend_forward_other/pallas_call | solution.py:641
  39.4 13.9 %all_to_all.20.refs_1_ = bf16[32,48,128]{2,1,0:T(8,128)(2,1)S(1)} all-to-all(bf16[32,48,128]{2,1,0:T(8,128)(2,1)S(1)} %get-tuple-element.29), channel_id=1, replica_groups=mesh['section'=16,'tm'=32] {'tm'}, dimensions={0} | all-to-all | bytes 786432 | tf_op jit(solution)/shard_map/all_to_all | solution.py:566
  53.4 5.2 %conv_block.1 = (bf16[32,32,128]{2,1,0:T(8,128)(2,1)S(1)}, bf16[128,768]{1,0:T(8,128)(2,1)S(1)}, bf16[128,768]{1,0:T(8,128)(2,1)}) custom-call(s32[1]{0:T(128)} %bitcast.8.refs_0_, bf16[32,48,128]{2,1,0:T(8,128)(2,1)S(1)} %all_to_all.20.refs_1_, bf16[128,768]{1,0:T(8,128)(2,1)S(1)} %bitcast.21, bf16[128,768]{1,0:T(8,128)(2,1)S(1)} %bitcast.24, ...), custom_call_target="tpu_custom_call" | custom-call | flops 10000000 | bytes 2097152 | tf_op jit(solution)/shard_map/conv_block/pallas_call | solution.py:654
  58.6 12.6 %all_to_all.21.refs_3_.refs_2_ = bf16[32,32,128]{2,1,0:T(8,128)(2,1)S(1)} all-to-all(bf16[32,32,128]{2,1,0:T(8,128)(2,1)S(1)} %get-tuple-element.30), channel_id=1, replica_groups=mesh['section'=16,'tm'=32] {'tm'}, dimensions={0} | all-to-all | bytes 524288 | tf_op jit(solution)/shard_map/all_to_all | solution.py:566
  71.2 4.0 %attend_backward_other.1 = (bf16[32,96,128]{2,1,0:T(8,128)(2,1)S(1)}, f32[1024,128]{1,0:T(8,128)S(1)}) custom-call(bf16[1024,2048]{1,0:T(8,128)(2,1)S(1)} %get-tuple-element.32.refs_0_, bf16[32,128,128]{2,1,0:T(8,128)(2,1)S(1)} %collective-permute-done.2.refs_2_.refs_1_, bf16[32,128,128]{2,1,0:T(8,128)(2,1)S(1)} %received.1.refs_0_.refs_1_.refs_2_, ...), custom_call_target="tpu_custom_call" | custom-call | flops 2147483648 | bytes 2097152 | tf_op jit(solution)/shard_map/attend_backward_other/pallas_call | solution.py:685
  75.2 2.1 %collective-permute-start.3 = (bf16[32,96,128]{2,1,0:T(8,128)(2,1)S(1)}, bf16[32,96,128]{2,1,0:T(8,128)(2,1)S(1)}, u32[]{:S(2)}, u32[]{:S(2)}) collective-permute-start(bf16[32,96,128]{2,1,0:T(8,128)(2,1)S(1)} %get-tuple-element.35), channel_id=1, source_target_pairs={{0,1},{1,0},{2,3},{3,2},{4,5},{5,4},{6,7},{7,6},{8,9},{9,8},{10,11... | collective-permute-start | bytes 2359304 | tf_op jit(solution)/shard_map/ppermute | solution.py:695
  77.4 3.9 %attend_backward_own.1 = (bf16[32,96,128]{2,1,0:T(8,128)(2,1)S(1)}, bf16[32,32,128]{2,1,0:T(8,128)(2,1)S(1)}) custom-call(bf16[1024,2048]{1,0:T(8,128)(2,1)S(1)} %get-tuple-element.26.refs_0_, bf16[32,128,128]{2,1,0:T(8,128)(2,1)S(1)} %received.1.refs_0_.refs_1_.refs_2_, bf16[32,32,128]{2,1,0:T(8,128)(2,1)S(1)} %all_to_all.21.refs_3_.refs_2_, ...), custom_call_target="tpu_custom_call" | custom-call | flops 2147483648 | bytes 2097152 | tf_op jit(solution)/shard_map/attend_backward_own/pallas_call | solution.py:696
  81.3 1.2 %join_grads.1 = bf16[32,128,128]{2,1,0:T(8,128)(2,1)} custom-call(bf16[32,96,128]{2,1,0:T(8,128)(2,1)S(1)} %get-tuple-element.34.part_ref, bf16[32,96,128]{2,1,0:T(8,128)(2,1)S(1)} %collective-permute-done.3.other_ref, bf16[32,32,128]{2,1,0:T(8,128)(2,1)S(1)} %get-tuple-element.36.piece_ref), custom_call_target="tpu_custom_call" | custom-call | flops 1000000 | bytes 2097152 | tf_op jit(solution)/shard_map/join_grads/pallas_call | solution.py:706
  82.5 3.9 %all-to-all-start.3 = ((bf16[32,128,128]{2,1,0:T(8,128)(2,1)}), bf16[32,128,128]{2,1,0:T(8,128)(2,1)S(1)}, u32[]{:S(2)}, u32[]{:S(2)}) async-start(bf16[32,128,128]{2,1,0:T(8,128)(2,1)} %join_grads.1), calls=%async_computation.3 | async-start | bytes 2097152 | tf_op jit(solution)/shard_map/all_to_all | solution.py:566
  86.4 1.9 %collective-permute-start.4 = (bf16[128,768]{1,0:T(8,128)(2,1)S(1)}, bf16[128,768]{1,0:T(8,128)(2,1)S(1)}, u32[]{:S(2)}, u32[]{:S(2)}) collective-permute-start(bf16[128,768]{1,0:T(8,128)(2,1)S(1)} %get-tuple-element.37), channel_id=1, source_target_pairs={{0,32},{32,64},{64,96},{96,128},{128,160},{160,192},{192,224},{224... | collective-permute-start | bytes 589832 | tf_op jit(solution)/shard_map/ppermute | solution.py:673
  88.3 12.3 %collective-permute-done.4.refs_1_ = bf16[128,768]{1,0:T(8,128)(2,1)S(1)} collective-permute-done((bf16[128,768]{1,0:T(8,128)(2,1)S(1)}, bf16[128,768]{1,0:T(8,128)(2,1)S(1)}, u32[]{:S(2)}, u32[]{:S(2)}) %collective-permute-start.4) | collective-permute-done | bytes 196640 | tf_op jit(solution)/shard_map/ppermute | solution.py:673
  100.6 3.1 %all-to-all-done.3.refs_0_ = bf16[32,128,128]{2,1,0:T(8,128)(2,1)S(1)} async-done(((bf16[32,128,128]{2,1,0:T(8,128)(2,1)}), bf16[32,128,128]{2,1,0:T(8,128)(2,1)S(1)}, u32[]{:S(2)}, u32[]{:S(2)}) %all-to-all-start.3) | async-done | bytes 1048608 | tf_op jit(solution)/shard_map/all_to_all | solution.py:566
  103.6 1.3 %unpack_grads.1 = (bf16[128,768]{1,0:T(8,128)(2,1)}, bf16[128,768]{1,0:T(8,128)(2,1)}, bf16[128,768]{1,0:T(8,128)(2,1)}, f32[1,768]{1,0:T(1,128)}, f32[31,1,768]{2,1,0:T(1,128)}, /*index=5*/bf16[128,768]{1,0:T(8,128)(2,1)}) custom-call(bf16[32,128,128]{2,1,0:T(8,128)(2,1)S(1)} %all-to-all-done.3.refs_0_, bf16[128,768]{1,0:T(8,128)(2,1)S(1)} %collective-permute-done.4.refs_1_), custom_call_target="tpu_custom_call" | custom-call | flops 1000000 | bytes 2097152 | tf_op jit(solution)/shard_map/unpack_grads/pallas_call | solution.py:718
  (13 shorter events, 0.0 us)
Async XLA Ops:
  0.6 30.2 %copy-start.3 = (f32[1,768]{1,0:T(1,128)S(1)}, f32[1,768]{1,0:T(1,128)}, u32[]{:S(2)}) copy-start(f32[1,768]{1,0:T(1,128)} %refs_6_.1) | copy-start | bytes 9220
  0.6 30.2 %copy-start.1 = (f32[1,31,768]{2,0,1:T(1,128)S(1)}, f32[1,31,768]{2,0,1:T(1,128)}, u32[]{:S(2)}) copy-start(f32[1,31,768]{2,0,1:T(1,128)} %param.12) | copy-start | bytes 285700
  3.1 27.8 %all-to-all-start = ((bf16[32,128,128]{2,1,0:T(8,128)(2,1)}), bf16[32,128,128]{2,1,0:T(8,128)(2,1)S(1)}, u32[]{:S(2)}, u32[]{:S(2)}) async-start(bf16[32,128,128]{2,1,0:T(8,128)(2,1)} %pack_qkv.1), calls=%async_computation | async-start | bytes 2097152 | tf_op jit(solution)/shard_map/all_to_all | solution.py:566
  15.2 11.0 %collective-permute-start = (bf16[48,768]{1,0:T(8,128)(2,1)S(1)}, bf16[48,768]{1,0:T(8,128)(2,1)S(1)}, u32[]{:S(2)}, u32[]{:S(2)}) collective-permute-start(bf16[48,768]{1,0:T(8,128)(2,1)S(1)} %pad_maximum_fusion), channel_id=1, source_target_pairs={{0,1},{1,2},{2,3},{3,4},{4,5},{5,6},{6,7},{7,8},{8,9},{9,10},{10,1... | collective-permute-start | bytes 221192 | tf_op jit(solution)/shard_map/ppermute | solution.py:588
  18.8 9.6 %collective-permute-start.1 = (bf16[48,768]{1,0:T(8,128)(2,1)S(1)}, bf16[48,768]{1,0:T(8,128)(2,1)S(1)}, u32[]{:S(2)}, u32[]{:S(2)}) collective-permute-start(bf16[48,768]{1,0:T(8,128)(2,1)S(1)} %pad_maximum_fusion.1), channel_id=1, source_target_pairs={{1,0},{2,1},{3,2},{4,3},{5,4},{6,5},{7,6},{8,7},{9,8},{10,9},{11,1... | collective-permute-start | bytes 221192 | tf_op jit(solution)/shard_map/ppermute | solution.py:591
  30.9 5.2 %collective-permute-start.2 = (bf16[32,128,128]{2,1,0:T(8,128)(2,1)S(1)}, bf16[32,128,128]{2,1,0:T(8,128)(2,1)S(1)}, u32[]{:S(2)}, u32[]{:S(2)}) collective-permute-start(bf16[32,128,128]{2,1,0:T(8,128)(2,1)S(1)} %received.1.refs_0_.refs_1_.refs_2_), channel_id=1, source_target_pairs={{0,1},{1,0},{2,3},{3,2},{4,5},{5,4},{6,7},{7,6},{8,9},{9,8},{10,11... | collective-permute-start | bytes 3145736 | tf_op jit(solution)/shard_map/ppermute | solution.py:622
  33.2 20.2 %copy-start = (bf16[1,128,768]{2,1,0:T(8,128)(2,1)S(1)}, bf16[1,128,768]{2,1,0:T(8,128)(2,1)}, u32[]{:S(2)}) copy-start(bf16[1,128,768]{2,1,0:T(8,128)(2,1)} %param.7) | copy-start | bytes 589828
  33.2 20.2 %copy-start.2 = (bf16[1,128,768]{2,1,0:T(8,128)(2,1)S(1)}, bf16[1,128,768]{2,1,0:T(8,128)(2,1)}, u32[]{:S(2)}) copy-start(bf16[1,128,768]{2,1,0:T(8,128)(2,1)} %param.13) | copy-start | bytes 589828
  75.2 6.1 %collective-permute-start.3 = (bf16[32,96,128]{2,1,0:T(8,128)(2,1)S(1)}, bf16[32,96,128]{2,1,0:T(8,128)(2,1)S(1)}, u32[]{:S(2)}, u32[]{:S(2)}) collective-permute-start(bf16[32,96,128]{2,1,0:T(8,128)(2,1)S(1)} %get-tuple-element.35), channel_id=1, source_target_pairs={{0,1},{1,0},{2,3},{3,2},{4,5},{5,4},{6,7},{7,6},{8,9},{9,8},{10,11... | collective-permute-start | bytes 2359304 | tf_op jit(solution)/shard_map/ppermute | solution.py:695
  82.5 21.2 %all-to-all-start.3 = ((bf16[32,128,128]{2,1,0:T(8,128)(2,1)}), bf16[32,128,128]{2,1,0:T(8,128)(2,1)S(1)}, u32[]{:S(2)}, u32[]{:S(2)}) async-start(bf16[32,128,128]{2,1,0:T(8,128)(2,1)} %join_grads.1), calls=%async_computation.3 | async-start | bytes 2097152 | tf_op jit(solution)/shard_map/all_to_all | solution.py:566
  86.4 14.2 %collective-permute-start.4 = (bf16[128,768]{1,0:T(8,128)(2,1)S(1)}, bf16[128,768]{1,0:T(8,128)(2,1)S(1)}, u32[]{:S(2)}, u32[]{:S(2)}) collective-permute-start(bf16[128,768]{1,0:T(8,128)(2,1)S(1)} %get-tuple-element.37), channel_id=1, source_target_pairs={{0,32},{32,64},{64,96},{96,128},{128,160},{160,192},{192,224},{224... | collective-permute-start | bytes 589832 | tf_op jit(solution)/shard_map/ppermute | solution.py:673
